TPU v7x, 32 devices: a whole 2x2x4 slice. The times are simulated.
32 devices in a mesh: row: 4 (over y, x), col: 8 (over z, core).
Axes of the slice: x: 2, y: 2, z: 4, core: 2. Of those that a mesh axis runs over, the one named last changes fastest.
Arguments:
- features: bfloat16 [16, 1024, 2048], P(None, 'row', 'col'), may hold values from -6 to 6
- conv_weight: bfloat16 [3, 16, 3, 3], replicated, may hold values from -0.5 to 0.5
- bias: float32 [3], replicated, may hold values from -3 to 3
- inv_wavelength: float32 [3], replicated, may hold values from 12 to 18
- distance: float32 [1], replicated, may hold values from 16000 to 32000
Outputs:
- propagated: bfloat16 [3, 2, 1024, 2048], P(None, None, ('row', 'col'))
All inputs are finite; a program needn't handle non-finite values.
Results may differ from a plain program's by a relative error of at most 0.0025.
Values may be sent and summed in bfloat16 or wider, within the bound.
No kernel may reach another device: no remote copies, remote signals or barrier semaphores. Data moves between devices by JAX's collectives and lax.ppermute only.
A program may use at most 128 MiB of HBM per device.

v0:
```python
from functools import partial
import math

import numpy as np
import jax
import jax.numpy as jnp
from jax import lax
from jax.experimental import pallas as pl
from jax.experimental.pallas import tpu as pltpu
from jax.sharding import PartitionSpec as P

F32 = jnp.float32
BF16 = jnp.bfloat16
TILE = 256
CODE = 124.0
TINY = 1.2e-38
VMEM_LIMIT = 56 * 1024 * 1024


def split_np(table):
    high = table.astype(jnp.bfloat16)
    low = (table - high.astype(np.float64)).astype(jnp.bfloat16)
    return high, low


def dft_np(rows, cols, length):
    product = np.outer(np.arange(rows), np.arange(cols)) % length
    angle = 2.0 * np.pi * product / length
    return np.cos(angle), np.sin(angle)


def interleaved(table, parts):
    rows = table.shape[0]
    return table.reshape(rows, 2, parts, TILE // parts).transpose(0, 2, 1, 3).reshape(rows, 2 * TILE)


def forward_y_np(parts):
    c, s = dft_np(TILE, TILE, TILE)
    full = np.block([[c, -s], [s, c]])
    return split_np(interleaved(full, parts))


def inverse_y_np(parts):
    c, s = dft_np(TILE, TILE, TILE)
    full = np.block([[c, s], [-s, c]])
    return split_np(np.ascontiguousarray(interleaved(full.T.copy(), parts).T))


def stacked_x_np():
    c, s = dft_np(TILE, TILE, TILE)
    return split_np(np.concatenate([c, s], 0))


def sincos_half(t):
    u = t * t
    h = np.pi / 2
    sp = [(-1) ** k * h ** (2 * k + 1) / math.factorial(2 * k + 1) for k in range(6)]
    cp = [(-1) ** k * h ** (2 * k) / math.factorial(2 * k) for k in range(7)]
    s = jnp.full_like(u, sp[-1])
    for coef in sp[-2::-1]:
        s = s * u + coef
    s = s * t
    c = jnp.full_like(u, cp[-1])
    for coef in cp[-2::-1]:
        c = c * u + coef
    return 1.0 - 2.0 * s * s, 2.0 * s * c


def encode(v):
    v2 = v * v
    v4 = v2 * v2
    return (v4 * (v2 * v)).astype(BF16)


def decode(w):
    w = w.astype(F32)
    mag = jnp.exp2(jnp.log2(jnp.maximum(jnp.abs(w), TINY)) * (1.0 / 7.0))
    return jnp.where(w < 0, -mag, mag)


def split(x):
    high = x.astype(BF16)
    return high, (x - high.astype(F32)).astype(BF16)


def dot(a, b):
    return lax.dot_general(a, b, (((1,), (0,)), ((), ())), preferred_element_type=F32)


def lane_shift(x, shift):
    width = x.shape[-1]
    shift = shift % width
    if shift == 0:
        return x
    if width % 128 == 0:
        return pltpu.roll(x, shift, x.ndim - 1)
    return jnp.concatenate([x[..., width - shift :], x[..., : width - shift]], -1)


class Pair:
    def __init__(self, re, im):
        self.re, self.im = re, im

    def __add__(self, o):
        return Pair(self.re + o.re, self.im + o.im)

    def __sub__(self, o):
        return Pair(self.re - o.re, self.im - o.im)

    def turn(self, sign):
        return Pair(-self.im, self.re) if sign > 0 else Pair(self.im, -self.re)

    def times(self, c, s):
        return Pair(self.re * c - self.im * s, self.re * s + self.im * c)


class Lanes:
    def __init__(self, x, sign_row):
        self.x, self.sign_row = x, sign_row

    def __add__(self, o):
        return Lanes(self.x + o.x, self.sign_row)

    def __sub__(self, o):
        return Lanes(self.x - o.x, self.sign_row)

    def turn(self, sign):
        half = lane_shift(self.x, self.x.shape[-1] // 2) * self.sign_row
        return Lanes(half if sign > 0 else -half, self.sign_row)

    def times(self, c, s):
        return Lanes(self.x * c + self.turn(1).x * s, self.sign_row)


def small_dft(items, sign):
    n = len(items)
    if n == 1:
        return items
    even = small_dft(items[0::2], sign)
    odd = small_dft(items[1::2], sign)
    out = [None] * n
    for k in range(n // 2):
        if k == 0:
            o = odd[k]
        elif 4 * k == n:
            o = odd[k].turn(sign)
        else:
            angle = sign * 2.0 * math.pi * k / n
            o = odd[k].times(math.cos(angle), math.sin(angle))
        out[k] = even[k] + o
        out[k + n // 2] = even[k] - o
    return out


def edge_slot(color, part):
    return 8 * (2 * color + part) + 4


def head_kernel(colors, chans, band, feat, halo, taps, expand, spread, masks, bias, out, table):
    step = 16
    rows = feat.shape[1]
    chunks = rows // step
    groups = 3 * colors
    total = None
    for u in range(3):
        wide = dot(expand[...], taps[u]).astype(BF16)
        wide = dot(wide, spread[...]) * masks[u]
        total = wide if total is None else total + wide
    table[...] = total.astype(BF16)
    halo_table = dot(expand[groups * step :, :], taps[2]).astype(BF16)
    lower = dot(expand[groups * step :, :], taps[0]).astype(BF16)

    lane = lax.broadcasted_iota(jnp.int32, (1, TILE), 1)
    keep_left = (lane != 0).astype(F32)
    keep_right = (lane != TILE - 1).astype(F32)
    lane_half = lax.broadcasted_iota(jnp.int32, (1, TILE // 2), 1)
    outer = (lane_half == 0) | (lane_half == TILE // 2 - 1)
    row16 = lax.broadcasted_iota(jnp.int32, (step, 1), 0)

    def combine(q0, q1, q2):
        r0 = pltpu.roll(q0, 1, 1)
        r2 = pltpu.roll(q2, TILE - 1, 1)
        own = q1 + r0 * keep_left + r2 * keep_right
        cross = jnp.where(lane_half == 0, r0[:, : TILE // 2], r2[:, TILE // 2 :])
        return own, cross

    def ring(block, base):
        res = []
        for o in range(colors):
            q = [block[base + v * colors + o : base + v * colors + o + 1] for v in range(3)]
            q = [jnp.broadcast_to(x, (8, TILE)) for x in q]
            own, cross = combine(*q)
            res.append((own[:1], cross[:1]))
        return res

    above = ring(dot(lower, halo[0]), 16)
    below = ring(dot(halo_table, halo[1]), 0)

    def chunk(i):
        block = feat[:, step * i : step * (i + 1), :].reshape(chans * step, TILE)
        prod = dot(table[...], block)
        main = []
        for o in range(colors):
            q = [prod[(v * colors + o) * step : (v * colors + o + 1) * step] for v in range(3)]
            main.append(combine(*q))
        base = groups * step
        return main, ring(prod, base), ring(prod, base + 16)

    def finish(i, main, from_above, from_below):
        extra = jnp.zeros((step, TILE // 2), F32)
        j, r = divmod(step * i, band)
        for o in range(colors):
            own, cross = main[o]
            own = own + jnp.where(row16 == 0, from_above[o][0], 0.0) + jnp.where(row16 == step - 1, from_below[o][0], 0.0)
            cross = cross + jnp.where(row16 == 0, from_above[o][1], 0.0) + jnp.where(row16 == step - 1, from_below[o][1], 0.0)
            own = own + bias[o]
            code = jnp.exp2(CODE * jnp.tanh(own))
            out[j, o * band + r : o * band + r + step, :] = code.astype(BF16)
            edges = jnp.where(lane_half == 0, own[:, : TILE // 2], own[:, TILE // 2 :])
            edges = jnp.where(outer, edges, 0.0) + pltpu.roll(jnp.where(outer, cross, 0.0), 2, 1)
            high = edges.astype(BF16).astype(F32)
            extra = extra + pltpu.roll(high, edge_slot(o, 0), 1) + pltpu.roll(edges - high, edge_slot(o, 1), 1)
        base = colors * band
        if band >= 2 * step:
            half = r // step
            row = base + (half // 2) * step
            start = (half % 2) * (TILE // 2)
            out[j, row : row + step, start : start + TILE // 2] = extra.astype(BF16)
        else:
            out[j, base + r : base + r + step, : TILE // 2] = extra.astype(BF16)
            out[j, base + r : base + r + step, TILE // 2 :] = jnp.zeros((step, TILE // 2), BF16)

    held = chunk(0)
    from_above = above
    for i in range(chunks):
        after = chunk(i + 1) if i + 1 < chunks else None
        from_below = after[1] if after is not None else below
        finish(i, held[0], from_above, from_below)
        from_above = held[2]
        held = after


def head_tables(colors, chans):
    step = 16
    groups = 3 * colors
    rows = groups * step + 32
    expand = np.zeros((rows, 16), np.float32)
    masks = np.zeros((3, rows, chans * step), np.float32)
    spread = np.zeros((chans, chans * step), np.float32)
    x_in = np.tile(np.arange(step), chans)
    for c in range(chans):
        spread[c, c * step : (c + 1) * step] = 1
    for g in range(groups):
        for xo in range(step):
            row = g * step + xo
            expand[row, g] = 1
            for u in range(3):
                masks[u, row] = x_in - xo + 1 == u
        top, bottom = groups * step + g, groups * step + 16 + g
        expand[top, g] = 1
        expand[bottom, g] = 1
        masks[2, top] = x_in == 0
        masks[0, bottom] = x_in == step - 1
    return expand.astype(jnp.bfloat16), spread.astype(jnp.bfloat16), masks


def head(features, halo, conv_weight, bias, band, peers):
    chans, rows, cols = features.shape
    colors = conv_weight.shape[0]
    expand, spread, masks = head_tables(colors, chans)
    taps = conv_weight.transpose(2, 3, 0, 1).reshape(3, 3 * colors, chans)
    taps = jnp.pad(taps, ((0, 0), (0, 16 - 3 * colors), (0, 0)))
    extra = max(16, band // 2)
    vm = pl.BlockSpec(memory_space=pltpu.VMEM)
    return pl.pallas_call(
        partial(head_kernel, colors, chans, band),
        out_shape=jax.ShapeDtypeStruct((peers, colors * band + extra, cols), BF16),
        in_specs=[vm] * 6 + [pl.BlockSpec(memory_space=pltpu.SMEM)],
        out_specs=vm,
        scratch_shapes=[pltpu.VMEM((3 * colors * 16 + 32, chans * 16), BF16)],
        compiler_params=pltpu.CompilerParams(vmem_limit_bytes=VMEM_LIMIT),
        name="conv_head",
    )(features, halo, taps, jnp.asarray(expand), jnp.asarray(spread), jnp.asarray(masks), bias)


def forward_y_kernel(colors, band, parts, coded, m_hi, m_lo, tw_c, tw_s, out, hi, lo):
    peers = coded.shape[0]
    step = 16
    half_lanes = TILE // 2
    lane = lax.broadcasted_iota(jnp.int32, (1, half_lanes), 1)
    for o in range(colors):
        for r in range(0, band, step):
            edge = []
            for p in range(peers):
                base = colors * band
                if band >= 2 * step:
                    half = r // step
                    row = base + (half // 2) * step
                    start = (half % 2) * half_lanes
                else:
                    row, start = base + r, 0
                block = coded[p, row : row + step, start : start + half_lanes].astype(F32)
                edge.append(
                    pltpu.roll(block, half_lanes - edge_slot(o, 0), 1) + pltpu.roll(block, half_lanes - edge_slot(o, 1), 1)
                )
            cross = [pltpu.roll(x, half_lanes - 2, 1) for x in edge]
            zero = jnp.zeros_like(cross[0])
            rows = slice(o * band + r, o * band + r + step)
            fixed = []
            for p in range(peers):
                before = cross[p - 1] if p > 0 else zero
                after = cross[p + 1] if p + 1 < peers else zero
                fixed.append(jnp.tanh(edge[p] + jnp.where(lane < half_lanes // 2, before, after)))
            for h in range(2):
                at = slice(h * half_lanes, (h + 1) * half_lanes)
                items = []
                for p in range(peers):
                    t = jnp.log2(coded[p, rows, at].astype(F32)) * (1.0 / CODE)
                    t = jnp.where(lane == (half_lanes - 1) * h, fixed[p], t)
                    items.append(Pair(*sincos_half(t)))
                items = small_dft(items, -1)
                for k, z in enumerate(items):
                    if k:
                        z = z.times(tw_c[k : k + 1, at], -tw_s[k : k + 1, at])
                    for part, x in enumerate((z.re, z.im)):
                        x_hi, x_lo = split(x)
                        to = slice(part * TILE + h * half_lanes, part * TILE + (h + 1) * half_lanes)
                        hi[k, rows, to] = x_hi
                        lo[k, rows, to] = x_lo
    width = 2 * TILE // parts
    for k in range(peers):
        acc = dot(hi[k], m_hi[...]) + dot(lo[k], m_hi[...]) + dot(hi[k], m_lo[...])
        code = encode(acc)
        for q in range(parts):
            out[parts * k + q] = code[:, q * width : (q + 1) * width]


def forward_y(coded, colors, band, parts):
    peers = coded.shape[0]
    m_hi, m_lo = forward_y_np(parts)
    tw_c, tw_s = dft_np(peers, TILE, peers * TILE)
    vm = pl.BlockSpec(memory_space=pltpu.VMEM)
    return pl.pallas_call(
        partial(forward_y_kernel, colors, band, parts),
        out_shape=jax.ShapeDtypeStruct((peers * parts, colors * band, 2 * TILE // parts), BF16),
        in_specs=[vm] * 5,
        out_specs=vm,
        scratch_shapes=[pltpu.VMEM((peers, colors * band, 2 * TILE), BF16)] * 2,
        compiler_params=pltpu.CompilerParams(vmem_limit_bytes=VMEM_LIMIT),
        name="forward_y",
    )(coded, jnp.asarray(m_hi), jnp.asarray(m_lo), jnp.asarray(tw_c, F32), jnp.asarray(tw_s, F32))


def transfer_kernel(sizes, position, wave, travel, out):
    height, width, parts, peers, block = sizes
    color, k = pl.program_id(0), pl.program_id(1)
    k0 = position[0] // parts
    q = position[0] % parts
    shape = out.shape[2:]
    m = lax.broadcasted_iota(jnp.int32, shape, 0)
    lane = lax.broadcasted_iota(jnp.int32, shape, 1)
    kx = k + (height // TILE) * m
    ky = k0 + peers * (block * q + lane % block)
    sx = jnp.where(kx < height // 2, kx, kx - height).astype(F32) / height
    sy = jnp.where(ky < width // 2, ky, ky - width).astype(F32) / width
    f2 = sx * sx + sy * sy
    a = wave[color]
    turns = travel[0] * f2 / (a + jnp.sqrt(a * a - f2))
    turns = turns - jnp.round(turns)
    turns = jnp.where(lane < block, turns, turns - 0.25)
    turns = turns - jnp.round(turns)
    c, _ = sincos_half(2.0 * turns)
    out[0, 0] = c * (1.0 / height)


def transfer(position, inv_wavelength, distance, sizes):
    height, width, parts, peers, block = sizes
    colors = inv_wavelength.shape[0]
    sm = pl.BlockSpec(memory_space=pltpu.SMEM)
    n = height // TILE
    return pl.pallas_call(
        partial(transfer_kernel, sizes),
        grid=(colors, n),
        out_shape=jax.ShapeDtypeStruct((colors, n, TILE, 2 * block), F32),
        in_specs=[sm] * 3,
        out_specs=pl.BlockSpec((1, 1, TILE, 2 * block), lambda c, k: (c, k, 0, 0)),
        compiler_params=pltpu.CompilerParams(vmem_limit_bytes=VMEM_LIMIT),
        name="transfer",
    )(position, inv_wavelength, distance)


def middle_kernel(coded, table, d_hi, d_lo, tw_c, tw_s, out, f_hi, f_lo):
    n = table.shape[1]
    width = coded.shape[-1]
    block = width // 2
    per = coded.shape[0] // n
    band = coded.shape[2]
    lane = lax.broadcasted_iota(jnp.int32, (1, width), 1)
    sign_row = jnp.where(lane < block, -1.0, 1.0)
    step = 16
    pieces = TILE // step
    for i in range(pieces):
        s, r = divmod(i * step, band)
        items = [Lanes(decode(coded[per * a + s, 0, r : r + step, :]), sign_row) for a in range(n)]
        items = small_dft(items, -1)
        rows = slice(i * step, (i + 1) * step)
        for k, z in enumerate(items):
            if k:
                z = z.times(tw_c[k, rows, :], -tw_s[k, rows, :])
            x_hi, x_lo = split(z.x)
            f_hi[rows, k * width : (k + 1) * width] = x_hi
            f_lo[rows, k * width : (k + 1) * width] = x_lo
    group = max(1, min(n, 256 // width))
    values = [None] * n
    for g in range(0, n, group):
        cols = slice(g * width, (g + group) * width)
        acc = dot(d_hi[...], f_hi[:, cols]) + dot(d_lo[...], f_hi[:, cols]) + dot(d_hi[...], f_lo[:, cols])
        for j in range(group):
            k = g + j
            re = acc[:TILE, j * width : (j + 1) * width]
            im = acc[TILE:, j * width : (j + 1) * width]
            z = Lanes(re, sign_row) + Lanes(im, sign_row).turn(-1)
            t = table[0, k]
            swapped = lane_shift(t, block)
            c = jnp.where(lane < block, t, swapped)
            s = jnp.where(lane < block, swapped, t)
            z = z.times(c, -s)
            x_hi, x_lo = split(z.x)
            f_hi[:, k * width : (k + 1) * width] = x_hi
            f_lo[:, k * width : (k + 1) * width] = x_lo
        acc = dot(d_hi[...], f_hi[:, cols]) + dot(d_lo[...], f_hi[:, cols]) + dot(d_hi[...], f_lo[:, cols])
        for j in range(group):
            k = g + j
            re = acc[:TILE, j * width : (j + 1) * width]
            im = acc[TILE:, j * width : (j + 1) * width]
            z = Lanes(re, sign_row) + Lanes(im, sign_row).turn(1)
            if k:
                z = z.times(tw_c[k], tw_s[k])
            values[k] = z
    for a, z in enumerate(small_dft(values, 1)):
        code = encode(z.x)
        for s in range(per):
            out[per * a + s, 0] = code[s * band : (s + 1) * band]


def middle(coded, table):
    groups, colors, band, width = coded.shape
    n = table.shape[1]
    d_hi, d_lo = stacked_x_np()
    tw_c, tw_s = dft_np(n, TILE, n * TILE)
    tw_c = np.repeat(tw_c[:, :, None], width, 2)
    tw_s = np.repeat(tw_s[:, :, None], width, 2)
    vm = pl.BlockSpec(memory_space=pltpu.VMEM)
    return pl.pallas_call(
        middle_kernel,
        grid=(colors,),
        out_shape=jax.ShapeDtypeStruct(coded.shape, BF16),
        in_specs=[
            pl.BlockSpec((groups, 1, band, width), lambda c: (0, c, 0, 0)),
            pl.BlockSpec((1, n, TILE, width), lambda c: (c, 0, 0, 0)),
            vm,
            vm,
            vm,
            vm,
        ],
        out_specs=pl.BlockSpec((groups, 1, band, width), lambda c: (0, c, 0, 0)),
        scratch_shapes=[pltpu.VMEM((TILE, n * width), BF16)] * 2,
        compiler_params=pltpu.CompilerParams(vmem_limit_bytes=VMEM_LIMIT),
        name="middle_x",
    )(coded, table, jnp.asarray(d_hi), jnp.asarray(d_lo), jnp.asarray(tw_c, F32), jnp.asarray(tw_s, F32))


def inverse_y_kernel(parts, coded, m_hi, m_lo, tw_c, tw_s, out, field):
    peers = tw_c.shape[0]
    colors, band = coded.shape[1], coded.shape[2]
    width = coded.shape[3]
    rows = colors * band
    for k in range(peers):
        z = [decode(coded[parts * k + q].reshape(rows, width)) for q in range(parts)]
        z = jnp.concatenate(z, -1)
        hi, lo = split(z)
        acc = dot(hi, m_hi[...]) + dot(lo, m_hi[...]) + dot(hi, m_lo[...])
        field[k] = acc
    step = 8
    half_lanes = TILE // 2
    scale = 1.0 / (peers * TILE)
    for o in range(colors):
        for r in range(0, band, 16):
            for h in range(2):
                at = slice(h * half_lanes, (h + 1) * half_lanes)
                at_im = slice(TILE + h * half_lanes, TILE + (h + 1) * half_lanes)
                got = slice(o * band + r, o * band + r + 16)
                items = []
                for k in range(peers):
                    z = Pair(field[k, got, at], field[k, got, at_im])
                    items.append(z.times(tw_c[k : k + 1, at] * scale, tw_s[k : k + 1, at] * scale))
                for p, z in enumerate(small_dft(items, 1)):
                    to = slice(p * TILE + h * half_lanes, p * TILE + (h + 1) * half_lanes)
                    out[o, 0, r : r + 16, to] = z.re.astype(BF16)
                    out[o, 1, r : r + 16, to] = z.im.astype(BF16)


def inverse_y(coded, parts):
    groups, colors, band, width = coded.shape
    peers = groups // parts
    m_hi, m_lo = inverse_y_np(parts)
    tw_c, tw_s = dft_np(peers, TILE, peers * TILE)
    vm = pl.BlockSpec(memory_space=pltpu.VMEM)
    return pl.pallas_call(
        partial(inverse_y_kernel, parts),
        out_shape=jax.ShapeDtypeStruct((colors, 2, band, peers * TILE), BF16),
        in_specs=[vm] * 5,
        out_specs=vm,
        scratch_shapes=[pltpu.VMEM((peers, colors * band, 2 * TILE), F32)],
        compiler_params=pltpu.CompilerParams(vmem_limit_bytes=VMEM_LIMIT),
        name="inverse_y",
    )(coded, jnp.asarray(m_hi), jnp.asarray(m_lo), jnp.asarray(tw_c, F32), jnp.asarray(tw_s, F32))


def per_device(features, conv_weight, bias, inv_wavelength, distance):
    mesh_rows = lax.axis_size("row")
    mesh_cols = lax.axis_size("col")
    groups = mesh_rows * mesh_cols
    chans, tile_rows, tile_cols = features.shape
    colors = conv_weight.shape[0]
    band = tile_rows // mesh_cols
    height = tile_rows * mesh_rows
    width = tile_cols * mesh_cols
    block = width // groups
    position = (lax.axis_index("row") * mesh_cols + lax.axis_index("col")).astype(jnp.int32)
    up = [(i, i + 1) for i in range(mesh_rows - 1)]
    down = [(j, i) for i, j in up]
    above = lax.ppermute(features[:, tile_rows - 1, :], "row", up)
    below = lax.ppermute(features[:, 0, :], "row", down)
    coded = head(features, jnp.stack((above, below)), conv_weight, bias, band, mesh_cols)
    coded = lax.all_to_all(coded, "col", split_axis=0, concat_axis=0, tiled=True)
    spectrum = forward_y(coded, colors, band, mesh_rows)
    table = transfer(position[None], inv_wavelength, distance, (height, width, mesh_rows, mesh_cols, block))
    spectrum = lax.all_to_all(spectrum, ("row", "col"), split_axis=0, concat_axis=0, tiled=True)
    back = middle(spectrum.reshape(groups, colors, band, 2 * block), table)
    back = lax.all_to_all(back, ("row", "col"), split_axis=0, concat_axis=0, tiled=True)
    return inverse_y(back, mesh_rows)


def solution(mesh):
    in_specs = (P(None, "row", "col"), P(), P(), P(), P())
    out_specs = P(None, None, ("row", "col"), None)
    return jax.shard_map(
        per_device, mesh=mesh, in_specs=in_specs, out_specs=out_specs, check_vma=False
    )
```

profile of v0, /device:TPU:0, one launch (start us, length us, event | category | flops | bytes accessed | tf_op | source)
XLA Modules:
  0.0 106.4 jit_solution(17560727580402278404)
XLA Ops:
  0.0 0.9 fusion
  0.9 1.3 %collective-permute-start.1 = (bf16[16,256]{1,0:T(8,128)(2,1)S(1)}, bf16[16,256]{1,0:T(8,128)(2,1)S(1)}, u32[]{:S(2)}, u32[]{:S(2)}) collective-permute-start(bf16[16,256]{1,0:T(8,128)(2,1)S(1)} %bitcast.15), channel_id=1, source_target_pairs={{8,0},{16,8},{24,16},{9,1},{17,9},{25,17},{10,2},{18,10},{26,18},{... | collective-permute-start | bytes 24584 | tf_op jit(solution)/shard_map/ppermute | solution.py:534
  2.2 5.5 %collective-permute-start = (bf16[16,256]{1,0:T(8,128)(2,1)S(1)}, bf16[16,256]{1,0:T(8,128)(2,1)S(1)}, u32[]{:S(2)}, u32[]{:S(2)}) collective-permute-start(bf16[16,256]{1,0:T(8,128)(2,1)S(1)} %bitcast.16), channel_id=1, source_target_pairs={{0,8},{8,16},{16,24},{1,9},{9,17},{17,25},{2,10},{10,18},{18,26},{... | collective-permute-start | bytes 24584 | tf_op jit(solution)/shard_map/ppermute | solution.py:533
  7.7 0.7 copy.26
  8.4 0.6 pad.4.taps
  9.0 0.0 collective-permute-done.1
  9.0 0.0 collective-permute-done
  9.1 0.6 pad_maximum_fusion.halo
  9.7 4.3 %conv_head.1 = bf16[8,112,256]{2,1,0:T(8,128)(2,1)} custom-call(bf16[16,256,256]{2,1,0:T(8,128)(2,1)} %feat.1, bf16[2,16,256]{2,1,0:T(8,128)(2,1)} %pad_maximum_fusion.halo, bf16[3,16,16]{2,1,0:T(8,128)(2,1)} %pad.4.taps, bf16[176,16]{1,0:T(8,128)(2,1)} %constant.39.clone.expand, bf16[16,256]{1,0:T(8,128)(2,1)} %constant.40.clone.spread, ...), custom_call_target="tpu_custom_call" | custom-call | tf_op jit(solution)/shard_map/conv_head/pallas_call | solution.py:275
  13.9 19.5 %all_to_all.15.coded = bf16[8,112,256]{2,1,0:T(8,128)(2,1)} all-to-all(bf16[8,112,256]{2,1,0:T(8,128)(2,1)} %conv_head.1), channel_id=1, replica_groups=mesh['row'=4,'col'=8] {'col'}, dimensions={0} | all-to-all | bytes 917504 | tf_op jit(solution)/shard_map/all_to_all | solution.py:536
  33.4 5.8 %forward_y.1 = bf16[32,96,128]{2,1,0:T(8,128)(2,1)} custom-call(bf16[8,112,256]{2,1,0:T(8,128)(2,1)} %all_to_all.15.coded, bf16[512,512]{1,0:T(8,128)(2,1)} %constant.42.clone.m_hi, bf16[512,512]{1,0:T(8,128)(2,1)} %constant.43.clone.m_lo, f32[8,256]{1,0:T(8,128)} %constant.44.clone.tw_c, f32[8,256]{1,0:T(8,128)} %constant.45.clone.tw_s), custom_call_target="tpu_custom_call" | custom-call | tf_op jit(solution)/shard_map/forward_y/pallas_call | solution.py:343
  39.2 5.2 %all-to-all-start.1 = ((bf16[32,96,128]{2,1,0:T(8,128)(2,1)}), bf16[32,96,128]{2,1,0:T(8,128)(2,1)S(1)}, u32[]{:S(2)}, u32[]{:S(2)}) async-start(bf16[32,96,128]{2,1,0:T(8,128)(2,1)} %forward_y.1), calls=%async_computation.1 | async-start | bytes 1572864 | tf_op jit(solution)/shard_map/all_to_all | solution.py:539
  45.0 6.1 %transfer.1.table = f32[3,4,256,128]{3,2,1,0:T(8,128)} custom-call(s32[1]{0:T(128)} %bitcast.7.position, f32[3]{0:T(128)} %wave.1, f32[1]{0:T(128)S(6)} %copy.34.travel), custom_call_target="tpu_custom_call" | custom-call | tf_op jit(solution)/shard_map/transfer/pallas_call | solution.py:381
  51.2 15.2 %all-to-all-done.1 = bf16[32,96,128]{2,1,0:T(8,128)(2,1)S(1)} async-done(((bf16[32,96,128]{2,1,0:T(8,128)(2,1)}), bf16[32,96,128]{2,1,0:T(8,128)(2,1)S(1)}, u32[]{:S(2)}, u32[]{:S(2)}) %all-to-all-start.1) | async-done | bytes 786464 | tf_op jit(solution)/shard_map/all_to_all | solution.py:539
  66.4 0.0 copy-start
  66.4 0.9 copy-done
  67.2 9.2 %middle_x.1 = bf16[32,3,32,128]{3,2,1,0:T(8,128)(2,1)} custom-call(bf16[32,3,32,128]{3,2,1,0:T(8,128)(2,1)} %bitcast.12, f32[3,4,256,128]{3,2,1,0:T(8,128)} %transfer.1.table, bf16[512,256]{1,0:T(8,128)(2,1)} %constant.46.clone.d_hi, bf16[512,256]{1,0:T(8,128)(2,1)} %constant.47.clone.d_lo, f32[4,256,128]{2,1,0:T(8,128)} %constant.48.clone.tw_c, ...), custom_call_target="tpu_custom_call" | custom-call | tf_op jit(solution)/shard_map/middle_x/pallas_call | solution.py:454
  76.4 25.3 %all_to_all.16.coded = bf16[32,3,32,128]{3,2,1,0:T(8,128)(2,1)} all-to-all(bf16[32,3,32,128]{3,2,1,0:T(8,128)(2,1)} %middle_x.1), channel_id=1, replica_groups=mesh['row'=4,'col'=8] {'row','col'}, dimensions={0} | all-to-all | bytes 1572864 | tf_op jit(solution)/shard_map/all_to_all | solution.py:541
  101.7 4.7 %inverse_y.1 = bf16[3,2,32,2048]{3,2,1,0:T(8,128)(2,1)} custom-call(bf16[32,3,32,128]{3,2,1,0:T(8,128)(2,1)} %all_to_all.16.coded, bf16[512,512]{1,0:T(8,128)(2,1)} %constant.50.clone.m_hi, bf16[512,512]{1,0:T(8,128)(2,1)} %constant.51.clone.m_lo, f32[8,256]{1,0:T(8,128)} %constant.44.clone.tw_c, f32[8,256]{1,0:T(8,128)} %constant.45.clone.tw_s), custom_call_target="tpu_custom_call" | custom-call | tf_op jit(solution)/shard_map/inverse_y/pallas_call | solution.py:509
  (3 shorter events, 0.0 us)
Async XLA Ops:
  0.9 8.1 %collective-permute-start.1 = (bf16[16,256]{1,0:T(8,128)(2,1)S(1)}, bf16[16,256]{1,0:T(8,128)(2,1)S(1)}, u32[]{:S(2)}, u32[]{:S(2)}) collective-permute-start(bf16[16,256]{1,0:T(8,128)(2,1)S(1)} %bitcast.15), channel_id=1, source_target_pairs={{8,0},{16,8},{24,16},{9,1},{17,9},{25,17},{10,2},{18,10},{26,18},{... | collective-permute-start | bytes 24584 | tf_op jit(solution)/shard_map/ppermute | solution.py:534
  2.2 6.8 %collective-permute-start = (bf16[16,256]{1,0:T(8,128)(2,1)S(1)}, bf16[16,256]{1,0:T(8,128)(2,1)S(1)}, u32[]{:S(2)}, u32[]{:S(2)}) collective-permute-start(bf16[16,256]{1,0:T(8,128)(2,1)S(1)} %bitcast.16), channel_id=1, source_target_pairs={{0,8},{8,16},{16,24},{1,9},{9,17},{17,25},{2,10},{10,18},{18,26},{... | collective-permute-start | bytes 24584 | tf_op jit(solution)/shard_map/ppermute | solution.py:533
  39.2 27.1 %all-to-all-start.1 = ((bf16[32,96,128]{2,1,0:T(8,128)(2,1)}), bf16[32,96,128]{2,1,0:T(8,128)(2,1)S(1)}, u32[]{:S(2)}, u32[]{:S(2)}) async-start(bf16[32,96,128]{2,1,0:T(8,128)(2,1)} %forward_y.1), calls=%async_computation.1 | async-start | bytes 1572864 | tf_op jit(solution)/shard_map/all_to_all | solution.py:539
  66.4 0.9 copy-start
where the time goes:
time: 107 us; the launch traced here: 106 us
  blocking collectives  44.8 us (42%)
  Pallas kernels  30.1 us (28%)
  waiting for transfers between devices  15.2 us (14%)
  starting transfers between devices  11.9 us (11%)
  local copies, waits for them, and re-layouts  3.12 us (3%)
    all_to_all x1, blocking collectives, per_device(): lax.all_to_all(back, ('row', 'col'), split_axis=0, concat_axis=0, tiled=T...  25.3 us
    all_to_all x1, blocking collectives, per_device(): lax.all_to_all(coded, 'col', split_axis=0, concat_axis=0, tiled=True)  19.5 us
    all_to_all x1, waiting for transfers between devices, per_device(): lax.all_to_all(spectrum, ('row', 'col'), split_axis=0, concat_axis=0, til...  15.2 us
    pallas_call x1, Pallas kernels, middle(): pl.pallas_call(middle_kernel, grid=(colors,), out_shape=jax.ShapeDtypeStr...  9.17 us
    pallas_call x1, Pallas kernels, transfer(): pl.pallas_call(partial(transfer_kernel, sizes), grid=(colors, n), out_sha...  6.14 us
    pallas_call x1, Pallas kernels, forward_y(): pl.pallas_call(partial(forward_y_kernel, colors, band, parts), out_shape=...  5.83 us
    ppermute x1, starting transfers between devices, per_device(): above = lax.ppermute(features[:, tile_rows - 1, :], 'row', up)  5.47 us
    all_to_all x1, starting transfers between devices, per_device(): lax.all_to_all(spectrum, ('row', 'col'), split_axis=0, concat_axis=0, til...  5.17 us
  transfers between devices with their start and end apart: 3, of which 1 were waited for; matrix products, arithmetic and copies ran while one was open for 1% of the time, Pallas kernels for 6%

commit v1 on v0

v1 whole, which is shorter than its diff:
```python
from functools import partial
import math

import numpy as np
import jax
import jax.numpy as jnp
from jax import lax
from jax.experimental import pallas as pl
from jax.experimental.pallas import tpu as pltpu
from jax.sharding import PartitionSpec as P

F32 = jnp.float32
BF16 = jnp.bfloat16
TILE = 256
HALF = 128
CODE = 124.0
TINY = 1.2e-38
VMEM_LIMIT = 20 * 1024 * 1024


def split_np(table):
    high = table.astype(jnp.bfloat16)
    low = (table - high.astype(np.float64)).astype(jnp.bfloat16)
    return high, low


def dft_np(rows, cols, length):
    product = np.outer(np.arange(rows), np.arange(cols)) % length
    angle = 2.0 * np.pi * product / length
    return np.cos(angle), np.sin(angle)


def interleaved(table, parts):
    rows = table.shape[0]
    return table.reshape(rows, 2, parts, HALF // parts).transpose(0, 2, 1, 3).reshape(rows, 2 * HALF)


def complex_np(sign):
    c, s = dft_np(HALF, HALF, HALF)
    return np.block([[c, sign * s], [-sign * s, c]])


def tall(table):
    high, low = split_np(table)
    return np.concatenate([high, high, low], 0)


def wide(table):
    high, low = split_np(table)
    return np.concatenate([high, low, high], 1)


def fitted(func, terms, odd):
    t = np.cos(np.pi * (np.arange(400) + 0.5) / 800)
    powers = np.stack([t ** (2 * k + odd) for k in range(terms)], 1)
    return [float(v) for v in np.linalg.lstsq(powers, func(np.pi / 2 * t), rcond=None)[0]]


def sincos_half(t, terms=5, scale=1.0):
    u = t * t
    sines = [v * scale ** (2 * k + 1) for k, v in enumerate(fitted(np.sin, terms, 1))]
    cosines = [v * scale ** (2 * k) for k, v in enumerate(fitted(np.cos, terms, 0))]
    s = sines[-1]
    for coef in sines[-2::-1]:
        s = s * u + coef
    s = s * t
    c = cosines[-1]
    for coef in cosines[-2::-1]:
        c = c * u + coef
    s2 = s + s
    return 1.0 - s2 * s, s2 * c


def log2(x):
    return lax.log(x) * (1.0 / math.log(2.0))


def encode(v):
    v2 = v * v
    return (v2 * v2 * v).astype(BF16)


def decode(w):
    w = w.astype(F32)
    return w * jnp.exp2(lax.log(jnp.maximum(jnp.abs(w), TINY)) * (-0.8 / math.log(2.0)))


def fetch(copies):
    for copy in copies:
        copy.start()
    return copies


def split(x):
    high = x.astype(BF16)
    return high, (x - high.astype(F32)).astype(BF16)


def dot(a, b):
    return lax.dot_general(a, b, (((1,), (0,)), ((), ())), preferred_element_type=F32)


def lane_shift(x, shift):
    width = x.shape[-1]
    shift = shift % width
    if shift == 0:
        return x
    if width % 128 == 0:
        return pltpu.roll(x, shift, x.ndim - 1)
    return jnp.concatenate([x[..., width - shift :], x[..., : width - shift]], -1)


class Pair:
    def __init__(self, re, im):
        self.re, self.im = re, im

    def __add__(self, o):
        return Pair(self.re + o.re, self.im + o.im)

    def __sub__(self, o):
        return Pair(self.re - o.re, self.im - o.im)

    def times(self, c, s):
        return Pair(self.re * c - self.im * s, self.re * s + self.im * c)


def butterfly(even, odd, k, n, sign):
    if k == 0:
        return even + odd, even - odd
    if 4 * k == n:
        plus = Pair(even.re - odd.im, even.im + odd.re)
        minus = Pair(even.re + odd.im, even.im - odd.re)
        return (plus, minus) if sign > 0 else (minus, plus)
    if 8 * k in (n, 3 * n):
        h = math.sqrt(0.5)
        a, b = (odd.re - odd.im) * h, (odd.re + odd.im) * h
        if sign > 0 and 8 * k == n:
            return Pair(even.re + a, even.im + b), Pair(even.re - a, even.im - b)
        if sign > 0:
            return Pair(even.re - b, even.im + a), Pair(even.re + b, even.im - a)
        if 8 * k == n:
            return Pair(even.re + b, even.im - a), Pair(even.re - b, even.im + a)
        return Pair(even.re - a, even.im - b), Pair(even.re + a, even.im + b)
    angle = sign * 2.0 * math.pi * k / n
    o = odd.times(math.cos(angle), math.sin(angle))
    return even + o, even - o


def small_dft(items, sign):
    n = len(items)
    if n == 1:
        return items
    even = small_dft(items[0::2], sign)
    odd = small_dft(items[1::2], sign)
    out = [None] * n
    for k in range(n // 2):
        out[k], out[k + n // 2] = butterfly(even[k], odd[k], k, n, sign)
    return out


def edge_slot(color, part):
    return 16 * color + 8 * part


def head_kernel(colors, chans, band, place, feat, above, below, taps, expand, spread, masks, bias, *rest):
    out, table = rest
    peers = out.shape[0]
    step = 16
    per = band // step
    groups = 3 * colors
    main_rows = groups * step
    me = place[0]
    for v in range(3):
        total = None
        for u in range(3):
            tall_taps = dot(expand[...], taps[u, v]).astype(BF16)
            part = dot(tall_taps, spread[...]) * masks[u].astype(F32)
            total = part if total is None else total + part
        main = colors * step
        table[v * main : (v + 1) * main, :] = total[:main].astype(BF16)
        ring = colors * 8
        start = main_rows + v * ring
        table[start : start + ring, :] = total[main:].astype(BF16)

    lane = lax.broadcasted_iota(jnp.int32, (1, TILE), 1)
    lane_half = lax.broadcasted_iota(jnp.int32, (1, HALF), 1)
    outer = (lane_half == 0) | (lane_half == HALF - 1)
    sub = lax.broadcasted_iota(jnp.int32, (8, 1), 0)

    first, last = sub == 0, sub == 7

    def outside(u, source):
        pieces = [dot(expand[colors * step :, :], taps[u, v]).astype(BF16) for v in range(3)]
        return [dot(piece, source) for piece in pieces]

    def ring_of(block):
        return [block[v * 8 * colors : (v + 1) * 8 * colors] for v in range(3)]

    def chunk(i):
        return feat[:, i * step : (i + 1) * step, :].reshape(chans * step, TILE)

    prods = [None] * (peers * per)
    rings = [None] * (peers * per + 2)
    rings[0] = outside(0, above[...])
    rings[-1] = outside(2, below[...])

    def multiply(j):
        for i in range(j * per, (j + 1) * per):
            prods[i] = dot(table[...], chunk(i))
            rings[i + 1] = ring_of(prods[i][main_rows:])

    def finish(j):
        slot = me ^ j
        total = None
        for i in range(per):
            at = j * per + i
            extra = None
            for o in range(colors):
                q = []
                for v in range(3):
                    g = v * colors + o
                    main = prods[at][g * step : (g + 1) * step]
                    top = main[:8] + jnp.where(first, rings[at][v][8 * o : 8 * o + 8], 0.0)
                    bottom = main[8:] + jnp.where(last, rings[at + 2][v][8 * o : 8 * o + 8], 0.0)
                    q.append(jnp.concatenate([top, bottom], 0))
                r0 = pltpu.roll(q[0], 1, 1)
                r2 = pltpu.roll(q[2], TILE - 1, 1)
                own = q[1] + jnp.where(lane == 0, 0.0, r0) + jnp.where(lane == TILE - 1, 0.0, r2) + bias[o]
                code = jnp.exp2(CODE * jnp.tanh(own)).astype(BF16)
                row = o * band + i * step
                for h in range(2):
                    start = h * colors * band + row
                    out[slot, start : start + step, :] = code[:, h * HALF : (h + 1) * HALF]
                cross = jnp.where(lane_half == 0, r0[:, :HALF], r2[:, HALF:])
                cross = pltpu.roll(jnp.where(outer, cross, 0.0), 2, 1)
                edges = jnp.where(lane_half == 0, own[:, :HALF], own[:, HALF:])
                edges = jnp.where(outer, edges, cross)
                high = edges.astype(BF16).astype(F32)
                both = high + pltpu.roll(edges - high, edge_slot(0, 1), 1)
                shift = edge_slot(o, 0) + 64 * i
                if shift:
                    both = pltpu.roll(both, shift, 1)
                extra = both if extra is None else extra + both
            total = extra if total is None else total + extra
        base = 2 * colors * band
        out[slot, base : base + step, :] = total.astype(BF16)

    multiply(0)
    for j in range(peers):
        if j + 1 < peers:
            multiply(j + 1)
        finish(j)


def head_tables(colors, chans):
    step = 16
    rows = colors * (step + 8)
    expand = np.zeros((rows, colors), np.float32)
    masks = np.zeros((3, rows, chans * step), np.float32)
    spread = np.zeros((chans, chans * step), np.float32)
    x_in = np.tile(np.arange(step), chans)
    for c in range(chans):
        spread[c, c * step : (c + 1) * step] = 1
    for o in range(colors):
        for xo in range(step):
            row = o * step + xo
            expand[row, o] = 1
            for u in range(3):
                masks[u, row] = x_in - xo + 1 == u
        base = colors * step + 8 * o
        expand[base, o] = 1
        expand[base + 7, o] = 1
        masks[0, base] = x_in == step - 1
        masks[2, base + 7] = x_in == 0
    return tuple(x.astype(jnp.bfloat16) for x in (expand, spread, masks))


def head(features, above, below, taps, bias, place, band, peers):
    chans, rows, cols = features.shape
    colors = bias.shape[0]
    expand, spread, masks = head_tables(colors, chans)
    vm = pl.BlockSpec(memory_space=pltpu.VMEM)
    sm = pl.BlockSpec(memory_space=pltpu.SMEM)
    return pl.pallas_call(
        partial(head_kernel, colors, chans, band),
        out_shape=jax.ShapeDtypeStruct((peers, 2 * colors * band + 16, HALF), BF16),
        in_specs=[sm] + [vm] * 7 + [sm],
        out_specs=vm,
        scratch_shapes=[pltpu.VMEM((3 * colors * 24, chans * 16), BF16)],
        compiler_params=pltpu.CompilerParams(vmem_limit_bytes=VMEM_LIMIT),
        name="conv_head",
    )(place, features, above, below, taps, jnp.asarray(expand), jnp.asarray(spread), jnp.asarray(masks), bias)


def forward_y_kernel(colors, band, parts, place, *refs):
    peers = len(refs) - 6
    matrix, tw_c, tw_s, out, coded, left = refs[peers:]
    for k in range(peers):
        coded[place[0] ^ k] = refs[k][...]
    step = 16
    lane = lax.broadcasted_iota(jnp.int32, (1, HALF), 1)
    for o in range(colors):
        for r in range(0, band, step):
            edge = []
            for p in range(peers):
                base = 2 * colors * band
                block = coded[p, base : base + step, :].astype(F32)
                shift = edge_slot(o, 0) + 64 * (r // step)
                if shift:
                    block = pltpu.roll(block, HALF - shift, 1)
                edge.append(block + pltpu.roll(block, HALF - edge_slot(0, 1), 1))
            cross = [pltpu.roll(x, HALF - 2, 1) for x in edge]
            zero = jnp.zeros_like(cross[0])
            fixed = []
            for p in range(peers):
                before = cross[p - 1] if p > 0 else zero
                after = cross[p + 1] if p + 1 < peers else zero
                fixed.append(CODE * jnp.tanh(edge[p] + jnp.where(lane < HALF // 2, before, after)))
            items = []
            for p in range(peers):
                for h in range(2):
                    start = (h * colors + o) * band + r
                    t = log2(coded[p, start : start + step, :].astype(F32))
                    t = jnp.where(lane == (HALF - 1) * h, fixed[p], t)
                    items.append(Pair(*sincos_half(t, 4, 1.0 / CODE)))
            for k, z in enumerate(small_dft(items, -1)):
                if k:
                    z = z.times(tw_c[k : k + 1, :], -tw_s[k : k + 1, :])
                for part, x in enumerate((z.re, z.im)):
                    high, low = split(x)
                    for j, value in enumerate((high, low, high)):
                        to = slice((2 * j + part) * HALF, (2 * j + part + 1) * HALF)
                        left[o, k, r : r + step, to] = value
        width = TILE // parts
        acc = dot(left[o].reshape(2 * peers * band, 3 * TILE), matrix[...])
        code = encode(acc)
        for k in range(2 * peers):
            for q in range(parts):
                out[parts * k + q, o * band : (o + 1) * band, :] = code[k * band : (k + 1) * band, q * width : (q + 1) * width]


def forward_y(blocks, place, colors, band, parts):
    peers = len(blocks)
    tw_c, tw_s = dft_np(2 * peers, HALF, peers * TILE)
    vm = pl.BlockSpec(memory_space=pltpu.VMEM)
    sm = pl.BlockSpec(memory_space=pltpu.SMEM)
    matrix = tall(interleaved(complex_np(-1), parts))
    return pl.pallas_call(
        partial(forward_y_kernel, colors, band, parts),
        out_shape=jax.ShapeDtypeStruct((2 * peers * parts, colors * band, TILE // parts), BF16),
        in_specs=[sm] + [vm] * (peers + 3),
        out_specs=vm,
        scratch_shapes=[
            pltpu.VMEM((peers,) + blocks[0].shape, BF16),
            pltpu.VMEM((colors, 2 * peers, band, 3 * TILE), BF16),
        ],
        compiler_params=pltpu.CompilerParams(vmem_limit_bytes=VMEM_LIMIT),
        name="forward_y",
    )(place, *blocks, jnp.asarray(matrix), jnp.asarray(tw_c, F32), jnp.asarray(tw_s, F32))


def transfer_kernel(sizes, position, wave, travel, out):
    height, width, parts, inner, block = sizes
    color, k = pl.program_id(0), pl.program_id(1)
    k0 = position[0] // parts
    q = position[0] % parts
    shape = out.shape[3:]
    m = lax.broadcasted_iota(jnp.int32, shape, 0)
    lane = lax.broadcasted_iota(jnp.int32, shape, 1)
    kx = 2 * k + lane // block + (height // HALF) * m
    ky = k0 + inner * (block * q + lane % block)
    sx = jnp.where(kx < height // 2, kx, kx - height).astype(F32) / height
    sy = jnp.where(ky < width // 2, ky, ky - width).astype(F32) / width
    f2 = sx * sx + sy * sy
    a = wave[color]
    turns = travel[0] * f2 / (a + jnp.sqrt(a * a - f2))
    turns = turns - jnp.round(turns)
    c, s = sincos_half(2.0 * turns)
    out[0, 0, 0] = c * (1.0 / height)
    out[0, 0, 1] = s * (1.0 / height)


def transfer(position, inv_wavelength, distance, sizes):
    height, width, parts, inner, block = sizes
    colors = inv_wavelength.shape[0]
    sm = pl.BlockSpec(memory_space=pltpu.SMEM)
    n = height // TILE
    return pl.pallas_call(
        partial(transfer_kernel, sizes),
        grid=(colors, n),
        out_shape=jax.ShapeDtypeStruct((colors, n, 2, HALF, 2 * block), F32),
        in_specs=[sm] * 3,
        out_specs=pl.BlockSpec((1, 1, 2, HALF, 2 * block), lambda c, k: (c, k, 0, 0, 0)),
        compiler_params=pltpu.CompilerParams(vmem_limit_bytes=VMEM_LIMIT),
        name="transfer",
    )(position, inv_wavelength, distance)


def middle_kernel(coded, tables, forward, inverse, tw_c, tw_s, out, right):
    for color in range(tables.shape[0]):
        middle_color(coded.at[:, color], tables.at[color], forward, inverse, tw_c, tw_s, out.at[:, color], right.at[color])


def middle_color(coded, table, forward, inverse, tw_c, tw_s, out, right):
    n = table.shape[0]
    width = coded.shape[-1]
    block = width // 2
    per = coded.shape[0] // (2 * n)
    band = coded.shape[1]
    lane = lax.broadcasted_iota(jnp.int32, (1, width), 1)
    left = lane < block
    step = 16
    turn_c = [jnp.where(left, 1.0, math.cos(math.pi * a / n)) for a in range(n)]
    turn_s = [jnp.where(left, 0.0, math.sin(math.pi * a / n)) for a in range(n)]

    def put(k, rows, z):
        for part, x in enumerate((z.re, z.im)):
            high, low = split(x)
            for j, value in enumerate((high, high, low)):
                to = (2 * j + part) * HALF
                right[to + rows.start : to + rows.stop, k * width : (k + 1) * width] = value

    for i in range(HALF // step):
        s, r = divmod(i * step, band)
        rows = slice(i * step, (i + 1) * step)
        items = []
        for a in range(n):
            x = decode(coded[per * a + s, r : r + step, :])
            y = decode(coded[per * (a + n) + s, r : r + step, :])
            u, v = x + y, x - y
            z = Pair(jnp.where(left, u, lane_shift(v, block)), jnp.where(left, lane_shift(u, block), v))
            if a:
                z = z.times(turn_c[a], -turn_s[a])
            items.append(z)
        for k, z in enumerate(small_dft(items, -1)):
            put(k, rows, z.times(tw_c[k, rows, :], -tw_s[k, rows, :]))
    acc = dot(forward[...], right[...])
    for k in range(n):
        cols = slice(k * width, (k + 1) * width)
        z = Pair(acc[:HALF, cols], acc[HALF:, cols])
        put(k, slice(0, HALF), z.times(table[k, 0], -table[k, 1]))
    acc = dot(inverse[...], right[...])
    for i in range(HALF // step):
        s, r = divmod(i * step, band)
        rows = slice(i * step, (i + 1) * step)
        items = []
        for k in range(n):
            cols = slice(k * width, (k + 1) * width)
            z = Pair(acc[rows, cols], acc[HALF + rows.start : HALF + rows.stop, cols])
            items.append(z.times(tw_c[k, rows, :], tw_s[k, rows, :]))
        for a, z in enumerate(small_dft(items, 1)):
            if a:
                z = z.times(turn_c[a], turn_s[a])
            u = jnp.where(left, z.re, lane_shift(z.im, block))
            v = jnp.where(left, lane_shift(z.re, block), z.im)
            out[per * a + s, r : r + step, :] = encode(u + v)
            out[per * (a + n) + s, r : r + step, :] = encode(u - v)


def middle(coded, table):
    groups, colors, band, width = coded.shape
    n = table.shape[1]
    tw_c, tw_s = dft_np(2 * n, HALF, 2 * n * HALF)
    tw_c, tw_s = (np.repeat(x.reshape(n, 2, HALF).transpose(0, 2, 1), width // 2, 2) for x in (tw_c, tw_s))
    vm = pl.BlockSpec(memory_space=pltpu.VMEM)
    forward = wide(complex_np(-1).T)
    inverse = wide(complex_np(1).T)
    return pl.pallas_call(
        middle_kernel,
        out_shape=jax.ShapeDtypeStruct(coded.shape, BF16),
        in_specs=[vm] * 6,
        out_specs=vm,
        scratch_shapes=[pltpu.VMEM((colors, 3 * TILE, n * width), BF16)],
        compiler_params=pltpu.CompilerParams(vmem_limit_bytes=VMEM_LIMIT),
        name="middle_x",
    )(coded, table, jnp.asarray(forward), jnp.asarray(inverse), jnp.asarray(tw_c, F32), jnp.asarray(tw_s, F32))


def inverse_y_kernel(parts, coded, matrix, tw_c, tw_s, target, left, out, sems):
    inner = tw_c.shape[0]
    colors, band, width = coded.shape[1], coded.shape[2], coded.shape[3]
    outs = []
    step = 16
    scale = 1.0 / (inner * HALF)
    for o in range(colors):
        for k in range(inner):
            for q in range(parts):
                high, low = split(decode(coded[parts * k + q, o]))
                for j, value in enumerate((high, low, high)):
                    left[o, k, :, j * TILE + q * width : j * TILE + (q + 1) * width] = value
        acc = dot(left[o].reshape(inner * band, 3 * TILE), matrix[...])
        for r in range(0, band, step):
            items = []
            for k in range(inner):
                z = acc[k * band + r : k * band + r + step]
                items.append(Pair(z[:, :HALF], z[:, HALF:]).times(tw_c[k : k + 1, :] * scale, tw_s[k : k + 1, :] * scale))
            for a, z in enumerate(small_dft(items, 1)):
                out[o, 0, r : r + step, a * HALF : (a + 1) * HALF] = z.re.astype(BF16)
                out[o, 1, r : r + step, a * HALF : (a + 1) * HALF] = z.im.astype(BF16)
        outs += fetch([pltpu.make_async_copy(out.at[o], target.at[o], sems.at[o])])
    for copy in outs:
        copy.wait()


def inverse_y(coded, parts):
    groups, colors, band, width = coded.shape
    inner = groups // parts
    tw_c, tw_s = dft_np(inner, HALF, inner * HALF)
    matrix = tall(np.ascontiguousarray(interleaved(complex_np(1).T.copy(), parts).T))
    hbm = pl.BlockSpec(memory_space=pltpu.HBM)
    vm = pl.BlockSpec(memory_space=pltpu.VMEM)
    return pl.pallas_call(
        partial(inverse_y_kernel, parts),
        out_shape=jax.ShapeDtypeStruct((colors, 2, band, inner * HALF), BF16),
        in_specs=[vm] * 4,
        out_specs=hbm,
        scratch_shapes=[
            pltpu.VMEM((colors, inner, band, 3 * TILE), BF16),
            pltpu.VMEM((colors, 2, band, inner * HALF), BF16),
            pltpu.SemaphoreType.DMA((colors,)),
        ],
        compiler_params=pltpu.CompilerParams(vmem_limit_bytes=VMEM_LIMIT),
        name="inverse_y",
    )(coded, jnp.asarray(matrix), jnp.asarray(tw_c, F32), jnp.asarray(tw_s, F32))


def per_device(features, conv_weight, bias, inv_wavelength, distance):
    mesh_rows = lax.axis_size("row")
    mesh_cols = lax.axis_size("col")
    groups = mesh_rows * mesh_cols
    chans, tile_rows, tile_cols = features.shape
    colors = conv_weight.shape[0]
    band = tile_rows // mesh_cols
    height = tile_rows * mesh_rows
    width = tile_cols * mesh_cols
    block = width // groups
    parts = mesh_rows // 2
    position = (lax.axis_index("row") * mesh_cols + lax.axis_index("col")).astype(jnp.int32)
    up = [(i, i + 1) for i in range(mesh_rows - 1)]
    down = [(j, i) for i, j in up]
    above = lax.ppermute(features[:, tile_rows - 1, :], "row", up)
    below = lax.ppermute(features[:, 0, :], "row", down)
    taps = conv_weight.transpose(2, 3, 0, 1)
    place = lax.axis_index("col").astype(jnp.int32)[None]
    bands = head(features, above, below, taps, bias, place, band, mesh_cols)
    blocks = [bands[0]]
    for k in range(1, mesh_cols):
        blocks.append(lax.ppermute(bands[k], "col", [(i, i ^ k) for i in range(mesh_cols)]))
    spectrum = forward_y(blocks, place, colors, band, parts)
    table = transfer(position[None], inv_wavelength, distance, (height, width, parts, 2 * mesh_cols, block))
    spectrum = lax.all_to_all(spectrum, ("row", "col"), split_axis=0, concat_axis=0, tiled=True)
    back = middle(spectrum.reshape(groups, colors, band, 2 * block), table)
    back = lax.all_to_all(back, ("row", "col"), split_axis=0, concat_axis=0, tiled=True)
    return inverse_y(back, parts)


def solution(mesh):
    in_specs = (P(None, "row", "col"), P(), P(), P(), P())
    out_specs = P(None, None, ("row", "col"), None)
    return jax.shard_map(
        per_device, mesh=mesh, in_specs=in_specs, out_specs=out_specs, check_vma=False
    )
```

time: 107 us -> 93.5 us (0.87)
  blocking collectives: 44.8 us -> 24 us
  Pallas kernels: 30.1 us -> 13.7 us
  waiting for transfers between devices: 15.2 us -> 27.9 us
  starting transfers between devices: 11.9 us -> 19.4 us
  local copies, waits for them, and re-layouts: 3.12 us -> 7.22 us
    all_to_all x1 -> x0, blocking collectives: 19.5 us -> none  [per_device(): lax.all_to_all(coded, 'col', split_axis=0, concat_axis=0, tiled=True)]
    ppermute x0 -> x7, starting transfers between devices: none -> 8.66 us  [per_device(): lax.ppermute(bands[k], 'col', [(i, i ^ k) for i in range(mesh_cols)])]
    pallas_call x1, Pallas kernels: 9.17 us -> 3.7 us  [middle(): pl.pallas_call(middle_kernel, out_shape=jax.ShapeDtypeStruct(coded.shape,...]
    unnamed x4 -> x31, local copies, waits for them, and re-layouts: 0.89 us -> 6.26 us
    ppermute x0 -> x7, waiting for transfers between devices: none -> 5.19 us  [per_device(): lax.ppermute(bands[k], 'col', [(i, i ^ k) for i in range(mesh_cols)])]
    pallas_call x1, Pallas kernels: 6.14 us -> 2.16 us  [transfer(): pl.pallas_call(partial(transfer_kernel, sizes), grid=(colors, n), out_sha...]
    all_to_all x1, waiting for transfers between devices: 15.2 us -> 19.1 us  [per_device(): lax.all_to_all(spectrum, ('row', 'col'), split_axis=0, concat_axis=0, til...]
    ppermute x1, waiting for transfers between devices: 0.01 us -> 3.53 us  [per_device(): below = lax.ppermute(features[:, 0, :], 'row', down)]
  transfers between devices with their start and end apart: 3 -> 10, of which waited for: 1 -> 5; matrix products, arithmetic and copies ran while one was open for 1% -> 1% of each run, Pallas kernels for 6% -> 2%
where the time goes in v1:
time: 93.5 us; the launch traced here: 93 us
  waiting for transfers between devices  27.9 us (30%)
  blocking collectives  24 us (26%)
  starting transfers between devices  19.4 us (21%)
  Pallas kernels  13.7 us (15%)
  local copies, waits for them, and re-layouts  7.22 us (8%)
    all_to_all x1, blocking collectives, per_device(): lax.all_to_all(back, ('row', 'col'), split_axis=0, concat_axis=0, tiled=T...  24 us
    all_to_all x1, waiting for transfers between devices, per_device(): lax.all_to_all(spectrum, ('row', 'col'), split_axis=0, concat_axis=0, til...  19.1 us
    ppermute x7, starting transfers between devices, per_device(): lax.ppermute(bands[k], 'col', [(i, i ^ k) for i in range(mesh_cols)])  8.66 us
    unnamed x31, local copies, waits for them, and re-layouts  6.26 us
    ppermute x7, waiting for transfers between devices, per_device(): lax.ppermute(bands[k], 'col', [(i, i ^ k) for i in range(mesh_cols)])  5.19 us
    ppermute x1, starting transfers between devices, per_device(): above = lax.ppermute(features[:, tile_rows - 1, :], 'row', up)  4.84 us
    all_to_all x1, starting transfers between devices, per_device(): lax.all_to_all(spectrum, ('row', 'col'), split_axis=0, concat_axis=0, til...  4.63 us
    pallas_call x1, Pallas kernels, middle(): pl.pallas_call(middle_kernel, out_shape=jax.ShapeDtypeStruct(coded.shape,...  3.7 us
  transfers between devices with their start and end apart: 10, of which 5 were waited for; matrix products, arithmetic and copies ran while one was open for 1% of the time, Pallas kernels for 2%

profile of v1, /device:TPU:0, one launch (start us, length us, event | category | flops | bytes accessed | tf_op | source)
XLA Modules:
  0.0 93.0 jit_solution(16582285862809067664)
XLA Ops:
  0.0 0.0 copy-start.8
  0.0 0.9 fusion
  0.9 4.8 %collective-permute-start = (bf16[16,256]{1,0:T(8,128)(2,1)S(1)}, bf16[16,256]{1,0:T(8,128)(2,1)S(1)}, u32[]{:S(2)}, u32[]{:S(2)}) collective-permute-start(bf16[16,256]{1,0:T(8,128)(2,1)S(1)} %bitcast.30), channel_id=1, source_target_pairs={{0,8},{8,16},{16,24},{1,9},{9,17},{17,25},{2,10},{10,18},{18,26},{... | collective-permute-start | bytes 24584 | tf_op jit(solution)/shard_map/ppermute | solution.py:541
  5.8 1.3 %collective-permute-start.1 = (bf16[16,256]{1,0:T(8,128)(2,1)S(1)}, bf16[16,256]{1,0:T(8,128)(2,1)S(1)}, u32[]{:S(2)}, u32[]{:S(2)}) collective-permute-start(bf16[16,256]{1,0:T(8,128)(2,1)S(1)} %bitcast.31), channel_id=1, source_target_pairs={{8,0},{16,8},{24,16},{9,1},{17,9},{25,17},{10,2},{18,10},{26,18},{... | collective-permute-start | bytes 24584 | tf_op jit(solution)/shard_map/ppermute | solution.py:542
  7.1 0.7 copy.27
  7.8 0.0 collective-permute-done.above
  7.8 3.5 %collective-permute-done.1.below = bf16[16,256]{1,0:T(8,128)(2,1)S(1)} collective-permute-done((bf16[16,256]{1,0:T(8,128)(2,1)S(1)}, bf16[16,256]{1,0:T(8,128)(2,1)S(1)}, u32[]{:S(2)}, u32[]{:S(2)}) %collective-permute-start.1) | collective-permute-done | bytes 8224 | tf_op jit(solution)/shard_map/ppermute | solution.py:542
  11.4 1.6 %copy-done = bf16[16,256,256]{2,1,0:T(8,128)(2,1)S(1)} copy-done((bf16[16,256,256]{2,1,0:T(8,128)(2,1)S(1)}, bf16[16,256,256]{2,1,0:T(8,128)(2,1)}, u32[]{:S(2)}) %copy-start) | copy-done | bytes 2097176
  13.0 0.9 copy-done.7
  13.8 0.7 copy-done.10
  14.6 0.7 copy-done.11
  15.3 0.7 copy-done.13
  15.9 2.3 %conv_head.1 = bf16[8,208,128]{2,1,0:T(8,128)(2,1)S(1)} custom-call(s32[1]{0:T(128)} %bitcast.place, bf16[16,256,256]{2,1,0:T(8,128)(2,1)S(1)} %copy-done, bf16[16,256]{1,0:T(8,128)(2,1)S(1)} %collective-permute-done.above, bf16[16,256]{1,0:T(8,128)(2,1)S(1)} %collective-permute-done.1.below, bf16[3,3,3,16]{3,2,1,0:T(4,128)(2,1)S(1)} %bitcast.29, ...), custom_call_target="tpu_custom_call" | custom-call | tf_op jit(solution)/shard_map/conv_head/pallas_call | solution.py:284
  18.2 0.0 copy-start.12
  18.3 1.7 %collective-permute-start.8 = (bf16[208,128]{1,0:T(8,128)(2,1)S(1)}, bf16[208,128]{1,0:T(8,128)(2,1)S(1)}, u32[]{:S(2)}, u32[]{:S(2)}) collective-permute-start(bf16[208,128]{1,0:T(8,128)(2,1)S(1)} %get-tuple-element.7), channel_id=1, source_target_pairs={{0,7},{1,6},{2,5},{3,4},{4,3},{5,2},{6,1},{7,0},{8,15},{9,14},{10,... | collective-permute-start | bytes 159752 | tf_op jit(solution)/shard_map/ppermute | solution.py:548
  19.9 2.1 %collective-permute-start.7 = (bf16[208,128]{1,0:T(8,128)(2,1)S(1)}, bf16[208,128]{1,0:T(8,128)(2,1)S(1)}, u32[]{:S(2)}, u32[]{:S(2)}) collective-permute-start(bf16[208,128]{1,0:T(8,128)(2,1)S(1)} %get-tuple-element.8), channel_id=1, source_target_pairs={{0,6},{1,7},{2,4},{3,5},{4,2},{5,3},{6,0},{7,1},{8,14},{9,15},{10,... | collective-permute-start | bytes 159752 | tf_op jit(solution)/shard_map/ppermute | solution.py:548
  22.0 0.4 collective-permute-start.6
  22.4 2.2 %collective-permute-start.5 = (bf16[208,128]{1,0:T(8,128)(2,1)S(1)}, bf16[208,128]{1,0:T(8,128)(2,1)S(1)}, u32[]{:S(2)}, u32[]{:S(2)}) collective-permute-start(bf16[208,128]{1,0:T(8,128)(2,1)S(1)} %get-tuple-element.10), channel_id=1, source_target_pairs={{0,4},{1,5},{2,6},{3,7},{4,0},{5,1},{6,2},{7,3},{8,12},{9,13},{10,... | collective-permute-start | bytes 159752 | tf_op jit(solution)/shard_map/ppermute | solution.py:548
  24.6 0.9 %collective-permute-start.4 = (bf16[208,128]{1,0:T(8,128)(2,1)S(1)}, bf16[208,128]{1,0:T(8,128)(2,1)S(1)}, u32[]{:S(2)}, u32[]{:S(2)}) collective-permute-start(bf16[208,128]{1,0:T(8,128)(2,1)S(1)} %get-tuple-element.11), channel_id=1, source_target_pairs={{0,3},{1,2},{2,1},{3,0},{4,7},{5,6},{6,5},{7,4},{8,11},{9,10},{10,... | collective-permute-start | bytes 159752 | tf_op jit(solution)/shard_map/ppermute | solution.py:548
  25.5 0.0 collective-permute-done.8.refs_7_
  25.5 0.9 collective-permute-start.3
  26.4 0.0 collective-permute-done.7.refs_6_
  26.4 0.5 collective-permute-start.2
  26.9 2.8 %collective-permute-done.6.refs_5_ = bf16[208,128]{1,0:T(8,128)(2,1)S(1)} collective-permute-done((bf16[208,128]{1,0:T(8,128)(2,1)S(1)}, bf16[208,128]{1,0:T(8,128)(2,1)S(1)}, u32[]{:S(2)}, u32[]{:S(2)}) %collective-permute-start.6) | collective-permute-done | bytes 53280 | tf_op jit(solution)/shard_map/ppermute | solution.py:548
  29.7 1.8 %collective-permute-done.5.refs_4_ = bf16[208,128]{1,0:T(8,128)(2,1)S(1)} collective-permute-done((bf16[208,128]{1,0:T(8,128)(2,1)S(1)}, bf16[208,128]{1,0:T(8,128)(2,1)S(1)}, u32[]{:S(2)}, u32[]{:S(2)}) %collective-permute-start.5) | collective-permute-done | bytes 53280 | tf_op jit(solution)/shard_map/ppermute | solution.py:548
  31.6 0.0 collective-permute-done.4.refs_3_
  31.6 0.6 collective-permute-done.3.refs_2_
  32.1 0.0 collective-permute-done.2.refs_1_
  32.1 0.0 copy-done.8
  32.1 0.0 copy-done.9
  32.1 0.0 copy-done.3
  32.2 0.0 copy-start.1
  32.2 0.0 copy-start.2
  32.2 0.0 copy-start.5
  32.2 3.1 %forward_y.1 = bf16[32,96,128]{2,1,0:T(8,128)(2,1)} custom-call(s32[1]{0:T(128)} %bitcast.place, bf16[208,128]{1,0:T(8,128)(2,1)S(1)} %get-tuple-element.14.refs_0_, bf16[208,128]{1,0:T(8,128)(2,1)S(1)} %collective-permute-done.2.refs_1_, bf16[208,128]{1,0:T(8,128)(2,1)S(1)} %collective-permute-done.3.refs_2_, ...), custom_call_target="tpu_custom_call" | custom-call | tf_op jit(solution)/shard_map/forward_y/pallas_call | solution.py:348
  35.3 4.6 %all-to-all-start = ((bf16[32,96,128]{2,1,0:T(8,128)(2,1)}), bf16[32,96,128]{2,1,0:T(8,128)(2,1)S(1)}, u32[]{:S(2)}, u32[]{:S(2)}) async-start(bf16[32,96,128]{2,1,0:T(8,128)(2,1)} %forward_y.1), calls=%async_computation | async-start | bytes 1572864 | tf_op jit(solution)/shard_map/all_to_all | solution.py:551
  40.6 0.0 copy-done.12
  40.6 2.2 %transfer.1.tables = f32[3,4,2,128,128]{4,3,2,1,0:T(8,128)S(1)} custom-call(s32[1]{0:T(128)} %bitcast.13.position, f32[3]{0:T(128)S(1)} %copy-done.12, f32[1]{0:T(128)S(6)} %copy.30.travel), custom_call_target="tpu_custom_call" | custom-call | tf_op jit(solution)/shard_map/transfer/pallas_call | solution.py:388
  42.8 19.1 %all-to-all-done = bf16[32,96,128]{2,1,0:T(8,128)(2,1)S(1)} async-done(((bf16[32,96,128]{2,1,0:T(8,128)(2,1)}), bf16[32,96,128]{2,1,0:T(8,128)(2,1)S(1)}, u32[]{:S(2)}, u32[]{:S(2)}) %all-to-all-start) | async-done | bytes 786464 | tf_op jit(solution)/shard_map/all_to_all | solution.py:551
  61.9 0.0 copy-done.1
  61.9 0.0 copy-done.2
  61.9 0.0 copy-done.5
  61.9 0.0 copy-start.6
  62.0 0.9 %copy-done.6 = f32[4,128,128]{2,1,0:T(8,128)S(1)} copy-done((f32[4,128,128]{2,1,0:T(8,128)S(1)}, f32[4,128,128]{2,1,0:T(8,128)}, u32[]{:S(2)}) %copy-start.6) | copy-done | bytes 262168
  62.9 3.7 %middle_x.1 = bf16[32,3,32,128]{3,2,1,0:T(8,128)(2,1)S(1)} custom-call(bf16[32,3,32,128]{3,2,1,0:T(8,128)(2,1)S(1)} %bitcast.28, f32[3,4,2,128,128]{4,3,2,1,0:T(8,128)S(1)} %transfer.1.tables, bf16[256,768]{1,0:T(8,128)(2,1)S(1)} %copy-done.2, bf16[256,768]{1,0:T(8,128)(2,1)S(1)} %copy-done.1, f32[4,128,128]{2,1,0:T(8,128)S(1)} %copy-done.6, ...), custom_call_target="tpu_custom_call" | custom-call | tf_op jit(solution)/shard_map/middle_x/pallas_call | solution.py:468
  66.6 24.0 %all_to_all.10.coded = bf16[32,3,32,128]{3,2,1,0:T(8,128)(2,1)S(1)} all-to-all(bf16[32,3,32,128]{3,2,1,0:T(8,128)(2,1)S(1)} %middle_x.1), channel_id=1, replica_groups=mesh['row'=4,'col'=8] {'row','col'}, dimensions={0} | all-to-all | bytes 1572864 | tf_op jit(solution)/shard_map/all_to_all | solution.py:553
  90.6 0.0 copy-done.4
  90.6 2.4 %inverse_y.1 = bf16[3,2,32,2048]{3,2,1,0:T(8,128)(2,1)} custom-call(bf16[32,3,32,128]{3,2,1,0:T(8,128)(2,1)S(1)} %all_to_all.10.coded, bf16[768,256]{1,0:T(8,128)(2,1)S(1)} %copy-done.4, f32[16,128]{1,0:T(8,128)S(1)} %copy-done.9, f32[16,128]{1,0:T(8,128)S(1)} %copy-done.8), custom_call_target="tpu_custom_call" | custom-call | tf_op jit(solution)/shard_map/inverse_y/pallas_call | solution.py:512
  (11 shorter events, 0.1 us)
Async XLA Ops:
  0.0 32.1 %copy-start.8 = (f32[16,128]{1,0:T(8,128)S(1)}, f32[16,128]{1,0:T(8,128)}, u32[]{:S(2)}) copy-start(f32[16,128]{1,0:T(8,128)} %constant.37.clone.refs_10_.tw_s) | copy-start | bytes 24580
  0.0 32.1 %copy-start.9 = (f32[16,128]{1,0:T(8,128)S(1)}, f32[16,128]{1,0:T(8,128)}, u32[]{:S(2)}) copy-start(f32[16,128]{1,0:T(8,128)} %constant.36.clone.refs_9_.tw_c) | copy-start | bytes 24580
  0.9 6.9 %collective-permute-start = (bf16[16,256]{1,0:T(8,128)(2,1)S(1)}, bf16[16,256]{1,0:T(8,128)(2,1)S(1)}, u32[]{:S(2)}, u32[]{:S(2)}) collective-permute-start(bf16[16,256]{1,0:T(8,128)(2,1)S(1)} %bitcast.30), channel_id=1, source_target_pairs={{0,8},{8,16},{16,24},{1,9},{9,17},{17,25},{2,10},{10,18},{18,26},{... | collective-permute-start | bytes 24584 | tf_op jit(solution)/shard_map/ppermute | solution.py:541
  5.8 5.5 %collective-permute-start.1 = (bf16[16,256]{1,0:T(8,128)(2,1)S(1)}, bf16[16,256]{1,0:T(8,128)(2,1)S(1)}, u32[]{:S(2)}, u32[]{:S(2)}) collective-permute-start(bf16[16,256]{1,0:T(8,128)(2,1)S(1)} %bitcast.31), channel_id=1, source_target_pairs={{8,0},{16,8},{24,16},{9,1},{17,9},{25,17},{10,2},{18,10},{26,18},{... | collective-permute-start | bytes 24584 | tf_op jit(solution)/shard_map/ppermute | solution.py:542
  11.4 1.6 %copy-start = (bf16[16,256,256]{2,1,0:T(8,128)(2,1)S(1)}, bf16[16,256,256]{2,1,0:T(8,128)(2,1)}, u32[]{:S(2)}) copy-start(bf16[16,256,256]{2,1,0:T(8,128)(2,1)} %feat.1) | copy-start | bytes 6291460
  12.9 0.9 copy-start.7
  13.8 0.7 copy-start.10
  14.6 0.7 copy-start.11
  15.3 0.7 copy-start.13
  15.9 16.2 %copy-start.3 = (bf16[768,256]{1,0:T(8,128)(2,1)S(1)}, bf16[768,256]{1,0:T(8,128)(2,1)}, u32[]{:S(2)}) copy-start(bf16[768,256]{1,0:T(8,128)(2,1)} %constant.35.clone.refs_8_) | copy-start | bytes 1179652
  18.2 22.4 %copy-start.12 = (f32[3]{0:T(128)S(1)}, f32[3]{0:T(128)}, u32[]{:S(2)}) copy-start(f32[3]{0:T(128)} %wave.1) | copy-start | bytes 40
  18.3 7.2 %collective-permute-start.8 = (bf16[208,128]{1,0:T(8,128)(2,1)S(1)}, bf16[208,128]{1,0:T(8,128)(2,1)S(1)}, u32[]{:S(2)}, u32[]{:S(2)}) collective-permute-start(bf16[208,128]{1,0:T(8,128)(2,1)S(1)} %get-tuple-element.7), channel_id=1, source_target_pairs={{0,7},{1,6},{2,5},{3,4},{4,3},{5,2},{6,1},{7,0},{8,15},{9,14},{10,... | collective-permute-start | bytes 159752 | tf_op jit(solution)/shard_map/ppermute | solution.py:548
  19.9 6.5 %collective-permute-start.7 = (bf16[208,128]{1,0:T(8,128)(2,1)S(1)}, bf16[208,128]{1,0:T(8,128)(2,1)S(1)}, u32[]{:S(2)}, u32[]{:S(2)}) collective-permute-start(bf16[208,128]{1,0:T(8,128)(2,1)S(1)} %get-tuple-element.8), channel_id=1, source_target_pairs={{0,6},{1,7},{2,4},{3,5},{4,2},{5,3},{6,0},{7,1},{8,14},{9,15},{10,... | collective-permute-start | bytes 159752 | tf_op jit(solution)/shard_map/ppermute | solution.py:548
  22.0 7.7 %collective-permute-start.6 = (bf16[208,128]{1,0:T(8,128)(2,1)S(1)}, bf16[208,128]{1,0:T(8,128)(2,1)S(1)}, u32[]{:S(2)}, u32[]{:S(2)}) collective-permute-start(bf16[208,128]{1,0:T(8,128)(2,1)S(1)} %get-tuple-element.9), channel_id=1, source_target_pairs={{0,5},{1,4},{2,7},{3,6},{4,1},{5,0},{6,3},{7,2},{8,13},{9,12},{10,... | collective-permute-start | bytes 159752 | tf_op jit(solution)/shard_map/ppermute | solution.py:548
  22.4 9.2 %collective-permute-start.5 = (bf16[208,128]{1,0:T(8,128)(2,1)S(1)}, bf16[208,128]{1,0:T(8,128)(2,1)S(1)}, u32[]{:S(2)}, u32[]{:S(2)}) collective-permute-start(bf16[208,128]{1,0:T(8,128)(2,1)S(1)} %get-tuple-element.10), channel_id=1, source_target_pairs={{0,4},{1,5},{2,6},{3,7},{4,0},{5,1},{6,2},{7,3},{8,12},{9,13},{10,... | collective-permute-start | bytes 159752 | tf_op jit(solution)/shard_map/ppermute | solution.py:548
  24.6 7.0 %collective-permute-start.4 = (bf16[208,128]{1,0:T(8,128)(2,1)S(1)}, bf16[208,128]{1,0:T(8,128)(2,1)S(1)}, u32[]{:S(2)}, u32[]{:S(2)}) collective-permute-start(bf16[208,128]{1,0:T(8,128)(2,1)S(1)} %get-tuple-element.11), channel_id=1, source_target_pairs={{0,3},{1,2},{2,1},{3,0},{4,7},{5,6},{6,5},{7,4},{8,11},{9,10},{10,... | collective-permute-start | bytes 159752 | tf_op jit(solution)/shard_map/ppermute | solution.py:548
  25.5 6.6 %collective-permute-start.3 = (bf16[208,128]{1,0:T(8,128)(2,1)S(1)}, bf16[208,128]{1,0:T(8,128)(2,1)S(1)}, u32[]{:S(2)}, u32[]{:S(2)}) collective-permute-start(bf16[208,128]{1,0:T(8,128)(2,1)S(1)} %get-tuple-element.12), channel_id=1, source_target_pairs={{0,2},{1,3},{2,0},{3,1},{4,6},{5,7},{6,4},{7,5},{8,10},{9,11},{10,... | collective-permute-start | bytes 159752 | tf_op jit(solution)/shard_map/ppermute | solution.py:548
  26.4 5.7 %collective-permute-start.2 = (bf16[208,128]{1,0:T(8,128)(2,1)S(1)}, bf16[208,128]{1,0:T(8,128)(2,1)S(1)}, u32[]{:S(2)}, u32[]{:S(2)}) collective-permute-start(bf16[208,128]{1,0:T(8,128)(2,1)S(1)} %get-tuple-element.13), channel_id=1, source_target_pairs={{0,1},{1,0},{2,3},{3,2},{4,5},{5,4},{6,7},{7,6},{8,9},{9,8},{10,11... | collective-permute-start | bytes 159752 | tf_op jit(solution)/shard_map/ppermute | solution.py:548
  32.2 29.8 %copy-start.1 = (bf16[256,768]{1,0:T(8,128)(2,1)S(1)}, bf16[256,768]{1,0:T(8,128)(2,1)}, u32[]{:S(2)}) copy-start(bf16[256,768]{1,0:T(8,128)(2,1)} %constant.39.clone.inverse) | copy-start | bytes 1179652
  32.2 29.8 %copy-start.2 = (bf16[256,768]{1,0:T(8,128)(2,1)S(1)}, bf16[256,768]{1,0:T(8,128)(2,1)}, u32[]{:S(2)}) copy-start(bf16[256,768]{1,0:T(8,128)(2,1)} %constant.38.clone.forward) | copy-start | bytes 1179652
  32.2 29.8 %copy-start.5 = (f32[4,128,128]{2,1,0:T(8,128)S(1)}, f32[4,128,128]{2,1,0:T(8,128)}, u32[]{:S(2)}) copy-start(f32[4,128,128]{2,1,0:T(8,128)} %constant.41.clone.tw_s) | copy-start | bytes 786436
  35.3 26.6 %all-to-all-start = ((bf16[32,96,128]{2,1,0:T(8,128)(2,1)}), bf16[32,96,128]{2,1,0:T(8,128)(2,1)S(1)}, u32[]{:S(2)}, u32[]{:S(2)}) async-start(bf16[32,96,128]{2,1,0:T(8,128)(2,1)} %forward_y.1), calls=%async_computation | async-start | bytes 1572864 | tf_op jit(solution)/shard_map/all_to_all | solution.py:551
  61.9 1.0 %copy-start.6 = (f32[4,128,128]{2,1,0:T(8,128)S(1)}, f32[4,128,128]{2,1,0:T(8,128)}, u32[]{:S(2)}) copy-start(f32[4,128,128]{2,1,0:T(8,128)} %constant.40.clone.tw_c) | copy-start | bytes 786436
  62.9 27.7 %copy-start.4 = (bf16[768,256]{1,0:T(8,128)(2,1)S(1)}, bf16[768,256]{1,0:T(8,128)(2,1)}, u32[]{:S(2)}) copy-start(bf16[768,256]{1,0:T(8,128)(2,1)} %constant.42.clone.matrix) | copy-start | bytes 1179652

commit v2 on v1

--- a/solution.py
+++ b/solution.py
@@ -15,7 +15,7 @@
 HALF = 128
 CODE = 124.0
 TINY = 1.2e-38
-VMEM_LIMIT = 20 * 1024 * 1024
+VMEM_LIMIT = 10 * 1024 * 1024
 
 
 def split_np(table):
@@ -162,25 +162,99 @@
     return 16 * color + 8 * part
 
 
-def head_kernel(colors, chans, band, place, feat, above, below, taps, expand, spread, masks, bias, *rest):
-    out, table = rest
+def prepare_kernel(colors, chans, feat, weight, bias, tile, first_edge, second_edge, table, ring_table, bias_rows, edge, taps, bias_in, sems):
+    step = 16
+    rows = feat.shape[1]
+    copies = fetch(
+        [
+            pltpu.make_async_copy(weight, taps, sems.at[0]),
+            pltpu.make_async_copy(bias, bias_in, sems.at[1]),
+            pltpu.make_async_copy(feat.at[:, pl.ds(0, step), :], edge.at[0], sems.at[2]),
+            pltpu.make_async_copy(feat.at[:, pl.ds(rows - step, step), :], edge.at[1], sems.at[3]),
+        ]
+        + [
+            pltpu.make_async_copy(feat.at[pl.ds(i * (chans // 8), chans // 8)], tile.at[pl.ds(i * (chans // 8), chans // 8)], sems.at[4 + i])
+            for i in range(8)
+        ]
+    )
+    copies[0].wait()
+    wide = chans * step
+    c_of = lax.broadcasted_iota(jnp.int32, (chans, wide), 1) // step
+    spread = (c_of == lax.broadcasted_iota(jnp.int32, (chans, wide), 0)).astype(F32).astype(BF16)
+    x_in = lax.broadcasted_iota(jnp.int32, (step + 8, wide), 1) % step
+    row = lax.broadcasted_iota(jnp.int32, (step + 8, wide), 0)
+    masks = []
+    for u in range(3):
+        main = (row < step) & (x_in - row + 1 == u)
+        if u == 0:
+            main = main | ((row == step) & (x_in == step - 1))
+        if u == 2:
+            main = main | ((row == step + 7) & (x_in == 0))
+        masks.append(main)
+    sub = lax.broadcasted_iota(jnp.int32, (8, chans), 0)
+    for o in range(colors):
+        spreads = [dot(taps[o, u], spread) for u in range(3)]
+        small = [taps[o, u].astype(F32) for u in range(3)]
+        for v in range(3):
+            total = jnp.zeros((step + 8, wide), F32)
+            for u in range(3):
+                total = total + jnp.where(masks[u], spreads[u][v : v + 1], 0.0)
+            g = v * colors + o
+            table[g * step : (g + 1) * step, :] = total[:step].astype(BF16)
+            start = 3 * colors * step + 8 * g
+            table[start : start + 8, :] = total[step:].astype(BF16)
+            ring_table[0, 8 * g : 8 * g + 8, :] = jnp.where(sub == 0, small[0][v : v + 1], 0.0).astype(BF16)
+            ring_table[1, 8 * g : 8 * g + 8, :] = jnp.where(sub == 7, small[2][v : v + 1], 0.0).astype(BF16)
+    copies[1].wait()
+    for o in range(colors):
+        bias_rows[o : o + 1, :] = jnp.full((1, TILE), bias_in[o], F32)
+    copies[2].wait()
+    copies[3].wait()
+    top = edge[0].astype(F32)[:, 0, :]
+    bottom = edge[1].astype(F32)[:, step - 1, :]
+    even = lax.axis_index("row") % 2 == 0
+    first_edge[...] = jnp.where(even, bottom, top).astype(BF16)
+    second_edge[...] = jnp.where(even, top, bottom).astype(BF16)
+    for copy in copies[4:]:
+        copy.wait()
+
+
+def prepare(features, conv_weight, bias):
+    chans, rows, cols = features.shape
+    colors = bias.shape[0]
+    weight = conv_weight.transpose(0, 2, 3, 1)
+    hbm = pl.BlockSpec(memory_space=pltpu.HBM)
+    vm = pl.BlockSpec(memory_space=pltpu.VMEM)
+    return pl.pallas_call(
+        partial(prepare_kernel, colors, chans),
+        out_shape=[
+            pltpu.VMEM(features.shape, BF16),
+            pltpu.VMEM((chans, cols), BF16),
+            pltpu.VMEM((chans, cols), BF16),
+            pltpu.VMEM((3 * colors * 24, chans * 16), BF16),
+            pltpu.VMEM((2, 3 * colors * 8, chans), BF16),
+            pltpu.VMEM((colors, TILE), F32),
+        ],
+        in_specs=[hbm] * 3,
+        out_specs=[vm] * 6,
+        scratch_shapes=[
+            pltpu.VMEM((2, chans, 16, cols), BF16),
+            pltpu.VMEM(weight.shape, BF16),
+            pltpu.SMEM(bias.shape, F32),
+            pltpu.SemaphoreType.DMA((12,)),
+        ],
+        compiler_params=pltpu.CompilerParams(vmem_limit_bytes=VMEM_LIMIT),
+        name="prepare",
+    )(*(pltpu.with_memory_space_constraint(x, pltpu.HBM) for x in (features, weight, bias)))
+
+
+def head_kernel(colors, chans, band, feat, first_halo, second_halo, table, ring_table, bias, out):
     peers = out.shape[0]
     step = 16
     per = band // step
     groups = 3 * colors
     main_rows = groups * step
-    me = place[0]
-    for v in range(3):
-        total = None
-        for u in range(3):
-            tall_taps = dot(expand[...], taps[u, v]).astype(BF16)
-            part = dot(tall_taps, spread[...]) * masks[u].astype(F32)
-            total = part if total is None else total + part
-        main = colors * step
-        table[v * main : (v + 1) * main, :] = total[:main].astype(BF16)
-        ring = colors * 8
-        start = main_rows + v * ring
-        table[start : start + ring, :] = total[main:].astype(BF16)
+    me = lax.axis_index("col")
 
     lane = lax.broadcasted_iota(jnp.int32, (1, TILE), 1)
     lane_half = lax.broadcasted_iota(jnp.int32, (1, HALF), 1)
@@ -189,10 +263,6 @@
 
     first, last = sub == 0, sub == 7
 
-    def outside(u, source):
-        pieces = [dot(expand[colors * step :, :], taps[u, v]).astype(BF16) for v in range(3)]
-        return [dot(piece, source) for piece in pieces]
-
     def ring_of(block):
         return [block[v * 8 * colors : (v + 1) * 8 * colors] for v in range(3)]
 
@@ -201,8 +271,12 @@
 
     prods = [None] * (peers * per)
     rings = [None] * (peers * per + 2)
-    rings[0] = outside(0, above[...])
-    rings[-1] = outside(2, below[...])
+    even = lax.axis_index("row") % 2 == 0
+    one, two = first_halo[...].astype(F32), second_halo[...].astype(F32)
+    above = jnp.where(even, two, one).astype(BF16)
+    below = jnp.where(even, one, two).astype(BF16)
+    rings[0] = ring_of(dot(ring_table[0], above))
+    rings[-1] = ring_of(dot(ring_table[1], below))
 
     def multiply(j):
         for i in range(j * per, (j + 1) * per):
@@ -225,7 +299,7 @@
                     q.append(jnp.concatenate([top, bottom], 0))
                 r0 = pltpu.roll(q[0], 1, 1)
                 r2 = pltpu.roll(q[2], TILE - 1, 1)
-                own = q[1] + jnp.where(lane == 0, 0.0, r0) + jnp.where(lane == TILE - 1, 0.0, r2) + bias[o]
+                own = q[1] + jnp.where(lane == 0, 0.0, r0) + jnp.where(lane == TILE - 1, 0.0, r2) + bias[o : o + 1, :]
                 code = jnp.exp2(CODE * jnp.tanh(own)).astype(BF16)
                 row = o * band + i * step
                 for h in range(2):
@@ -252,51 +326,26 @@
         finish(j)
 
 
-def head_tables(colors, chans):
-    step = 16
-    rows = colors * (step + 8)
-    expand = np.zeros((rows, colors), np.float32)
-    masks = np.zeros((3, rows, chans * step), np.float32)
-    spread = np.zeros((chans, chans * step), np.float32)
-    x_in = np.tile(np.arange(step), chans)
-    for c in range(chans):
-        spread[c, c * step : (c + 1) * step] = 1
-    for o in range(colors):
-        for xo in range(step):
-            row = o * step + xo
-            expand[row, o] = 1
-            for u in range(3):
-                masks[u, row] = x_in - xo + 1 == u
-        base = colors * step + 8 * o
-        expand[base, o] = 1
-        expand[base + 7, o] = 1
-        masks[0, base] = x_in == step - 1
-        masks[2, base + 7] = x_in == 0
-    return tuple(x.astype(jnp.bfloat16) for x in (expand, spread, masks))
-
-
-def head(features, above, below, taps, bias, place, band, peers):
+def head(prepared, above, below, band, peers):
+    features, table, ring_table, bias = prepared
     chans, rows, cols = features.shape
     colors = bias.shape[0]
-    expand, spread, masks = head_tables(colors, chans)
     vm = pl.BlockSpec(memory_space=pltpu.VMEM)
-    sm = pl.BlockSpec(memory_space=pltpu.SMEM)
     return pl.pallas_call(
         partial(head_kernel, colors, chans, band),
-        out_shape=jax.ShapeDtypeStruct((peers, 2 * colors * band + 16, HALF), BF16),
-        in_specs=[sm] + [vm] * 7 + [sm],
+        out_shape=pltpu.VMEM((peers, 2 * colors * band + 16, HALF), BF16),
+        in_specs=[vm] * 6,
         out_specs=vm,
-        scratch_shapes=[pltpu.VMEM((3 * colors * 24, chans * 16), BF16)],
         compiler_params=pltpu.CompilerParams(vmem_limit_bytes=VMEM_LIMIT),
         name="conv_head",
-    )(place, features, above, below, taps, jnp.asarray(expand), jnp.asarray(spread), jnp.asarray(masks), bias)
-
-
-def forward_y_kernel(colors, band, parts, place, *refs):
+    )(features, above, below, table, ring_table, bias)
+
+
+def forward_y_kernel(colors, band, parts, *refs):
     peers = len(refs) - 6
     matrix, tw_c, tw_s, out, coded, left = refs[peers:]
     for k in range(peers):
-        coded[place[0] ^ k] = refs[k][...]
+        coded[lax.axis_index("col") ^ k] = refs[k][...]
     step = 16
     lane = lax.broadcasted_iota(jnp.int32, (1, HALF), 1)
     for o in range(colors):
@@ -339,7 +388,7 @@
                 out[parts * k + q, o * band : (o + 1) * band, :] = code[k * band : (k + 1) * band, q * width : (q + 1) * width]
 
 
-def forward_y(blocks, place, colors, band, parts):
+def forward_y(blocks, colors, band, parts):
     peers = len(blocks)
     tw_c, tw_s = dft_np(2 * peers, HALF, peers * TILE)
     vm = pl.BlockSpec(memory_space=pltpu.VMEM)
@@ -347,8 +396,8 @@
     matrix = tall(interleaved(complex_np(-1), parts))
     return pl.pallas_call(
         partial(forward_y_kernel, colors, band, parts),
-        out_shape=jax.ShapeDtypeStruct((2 * peers * parts, colors * band, TILE // parts), BF16),
-        in_specs=[sm] + [vm] * (peers + 3),
+        out_shape=pltpu.VMEM((2 * peers * parts, colors * band, TILE // parts), BF16),
+        in_specs=[vm] * (peers + 3),
         out_specs=vm,
         scratch_shapes=[
             pltpu.VMEM((peers,) + blocks[0].shape, BF16),
@@ -356,52 +405,66 @@
         ],
         compiler_params=pltpu.CompilerParams(vmem_limit_bytes=VMEM_LIMIT),
         name="forward_y",
-    )(place, *blocks, jnp.asarray(matrix), jnp.asarray(tw_c, F32), jnp.asarray(tw_s, F32))
-
-
-def transfer_kernel(sizes, position, wave, travel, out):
+    )(*blocks, jnp.asarray(matrix), jnp.asarray(tw_c, F32), jnp.asarray(tw_s, F32))
+
+
+def transfer_kernel(sizes, wave, travel, out):
     height, width, parts, inner, block = sizes
     color, k = pl.program_id(0), pl.program_id(1)
-    k0 = position[0] // parts
-    q = position[0] % parts
+    position = lax.axis_index("row") * lax.axis_size("col") + lax.axis_index("col")
+    k0 = position // parts
+    q = position % parts
     shape = out.shape[3:]
     m = lax.broadcasted_iota(jnp.int32, shape, 0)
     lane = lax.broadcasted_iota(jnp.int32, shape, 1)
     kx = 2 * k + lane // block + (height // HALF) * m
     ky = k0 + inner * (block * q + lane % block)
-    sx = jnp.where(kx < height // 2, kx, kx - height).astype(F32) / height
-    sy = jnp.where(ky < width // 2, ky, ky - width).astype(F32) / width
-    f2 = sx * sx + sy * sy
-    a = wave[color]
-    turns = travel[0] * f2 / (a + jnp.sqrt(a * a - f2))
-    turns = turns - jnp.round(turns)
-    c, s = sincos_half(2.0 * turns)
-    out[0, 0, 0] = c * (1.0 / height)
-    out[0, 0, 1] = s * (1.0 / height)
-
-
-def transfer(position, inv_wavelength, distance, sizes):
+
+    @pl.when(color < wave.shape[0])
+    def _():
+        sx = jnp.where(kx < height // 2, kx, kx - height).astype(F32) / height
+        sy = jnp.where(ky < width // 2, ky, ky - width).astype(F32) / width
+        f2 = sx * sx + sy * sy
+        a = wave[jnp.minimum(color, wave.shape[0] - 1)]
+        turns = travel[0] * f2 / (a + jnp.sqrt(a * a - f2))
+        turns = turns - jnp.round(turns)
+        c, s = sincos_half(2.0 * turns)
+        out[0, 0, 0] = c * (1.0 / height)
+        out[0, 0, 1] = s * (1.0 / height)
+
+    @pl.when(color == wave.shape[0])
+    def _():
+        turns = ((2 * k + lane // block) * m).astype(F32) * (1.0 / height)
+        c, s = sincos_half(2.0 * (turns - jnp.round(turns)))
+        out[0, 0, 0] = c
+        out[0, 0, 1] = s
+
+
+def transfer(inv_wavelength, distance, sizes):
     height, width, parts, inner, block = sizes
     colors = inv_wavelength.shape[0]
     sm = pl.BlockSpec(memory_space=pltpu.SMEM)
     n = height // TILE
     return pl.pallas_call(
         partial(transfer_kernel, sizes),
-        grid=(colors, n),
-        out_shape=jax.ShapeDtypeStruct((colors, n, 2, HALF, 2 * block), F32),
-        in_specs=[sm] * 3,
+        grid=(colors + 1, n),
+        out_shape=jax.ShapeDtypeStruct((colors + 1, n, 2, HALF, 2 * block), F32),
+        in_specs=[sm] * 2,
         out_specs=pl.BlockSpec((1, 1, 2, HALF, 2 * block), lambda c, k: (c, k, 0, 0, 0)),
         compiler_params=pltpu.CompilerParams(vmem_limit_bytes=VMEM_LIMIT),
         name="transfer",
-    )(position, inv_wavelength, distance)
-
-
-def middle_kernel(coded, tables, forward, inverse, tw_c, tw_s, out, right):
-    for color in range(tables.shape[0]):
-        middle_color(coded.at[:, color], tables.at[color], forward, inverse, tw_c, tw_s, out.at[:, color], right.at[color])
-
-
-def middle_color(coded, table, forward, inverse, tw_c, tw_s, out, right):
+    )(inv_wavelength, distance)
+
+
+def middle_kernel(coded, tables, matrix, out, right):
+    colors = out.shape[1]
+    for color in range(colors):
+        middle_color(
+            coded.at[:, color], tables.at[color], matrix, tables.at[colors], out.at[:, color], right.at[color]
+        )
+
+
+def middle_color(coded, table, matrix, twiddles, out, right):
     n = table.shape[0]
     width = coded.shape[-1]
     block = width // 2
@@ -413,8 +476,8 @@
     turn_c = [jnp.where(left, 1.0, math.cos(math.pi * a / n)) for a in range(n)]
     turn_s = [jnp.where(left, 0.0, math.sin(math.pi * a / n)) for a in range(n)]
 
-    def put(k, rows, z):
-        for part, x in enumerate((z.re, z.im)):
+    def put(k, rows, z, order):
+        for part, x in zip(order, (z.re, z.im)):
             high, low = split(x)
             for j, value in enumerate((high, high, low)):
                 to = (2 * j + part) * HALF
@@ -433,21 +496,21 @@
                 z = z.times(turn_c[a], -turn_s[a])
             items.append(z)
         for k, z in enumerate(small_dft(items, -1)):
-            put(k, rows, z.times(tw_c[k, rows, :], -tw_s[k, rows, :]))
-    acc = dot(forward[...], right[...])
+            put(k, rows, z.times(twiddles[k, 0, rows, :], -twiddles[k, 1, rows, :]), (0, 1))
+    acc = dot(matrix[...], right[...])
     for k in range(n):
         cols = slice(k * width, (k + 1) * width)
         z = Pair(acc[:HALF, cols], acc[HALF:, cols])
-        put(k, slice(0, HALF), z.times(table[k, 0], -table[k, 1]))
-    acc = dot(inverse[...], right[...])
+        put(k, slice(0, HALF), z.times(table[k, 0], -table[k, 1]), (1, 0))
+    acc = dot(matrix[...], right[...])
     for i in range(HALF // step):
         s, r = divmod(i * step, band)
         rows = slice(i * step, (i + 1) * step)
         items = []
         for k in range(n):
             cols = slice(k * width, (k + 1) * width)
-            z = Pair(acc[rows, cols], acc[HALF + rows.start : HALF + rows.stop, cols])
-            items.append(z.times(tw_c[k, rows, :], tw_s[k, rows, :]))
+            z = Pair(acc[HALF + rows.start : HALF + rows.stop, cols], acc[rows, cols])
+            items.append(z.times(twiddles[k, 0, rows, :], twiddles[k, 1, rows, :]))
         for a, z in enumerate(small_dft(items, 1)):
             if a:
                 z = z.times(turn_c[a], turn_s[a])
@@ -460,20 +523,17 @@
 def middle(coded, table):
     groups, colors, band, width = coded.shape
     n = table.shape[1]
-    tw_c, tw_s = dft_np(2 * n, HALF, 2 * n * HALF)
-    tw_c, tw_s = (np.repeat(x.reshape(n, 2, HALF).transpose(0, 2, 1), width // 2, 2) for x in (tw_c, tw_s))
     vm = pl.BlockSpec(memory_space=pltpu.VMEM)
     forward = wide(complex_np(-1).T)
-    inverse = wide(complex_np(1).T)
     return pl.pallas_call(
         middle_kernel,
         out_shape=jax.ShapeDtypeStruct(coded.shape, BF16),
-        in_specs=[vm] * 6,
+        in_specs=[vm] * 3,
         out_specs=vm,
         scratch_shapes=[pltpu.VMEM((colors, 3 * TILE, n * width), BF16)],
         compiler_params=pltpu.CompilerParams(vmem_limit_bytes=VMEM_LIMIT),
         name="middle_x",
-    )(coded, table, jnp.asarray(forward), jnp.asarray(inverse), jnp.asarray(tw_c, F32), jnp.asarray(tw_s, F32))
+    )(*(pltpu.with_memory_space_constraint(x, pltpu.VMEM) for x in (coded, table, jnp.asarray(forward))))
 
 
 def inverse_y_kernel(parts, coded, matrix, tw_c, tw_s, target, left, out, sems):
@@ -535,19 +595,17 @@
     width = tile_cols * mesh_cols
     block = width // groups
     parts = mesh_rows // 2
-    position = (lax.axis_index("row") * mesh_cols + lax.axis_index("col")).astype(jnp.int32)
-    up = [(i, i + 1) for i in range(mesh_rows - 1)]
-    down = [(j, i) for i, j in up]
-    above = lax.ppermute(features[:, tile_rows - 1, :], "row", up)
-    below = lax.ppermute(features[:, 0, :], "row", down)
-    taps = conv_weight.transpose(2, 3, 0, 1)
-    place = lax.axis_index("col").astype(jnp.int32)[None]
-    bands = head(features, above, below, taps, bias, place, band, mesh_cols)
-    blocks = [bands[0]]
-    for k in range(1, mesh_cols):
-        blocks.append(lax.ppermute(bands[k], "col", [(i, i ^ k) for i in range(mesh_cols)]))
-    spectrum = forward_y(blocks, place, colors, band, parts)
-    table = transfer(position[None], inv_wavelength, distance, (height, width, parts, 2 * mesh_cols, block))
+    tile, edge_one, edge_two, *prepared = prepare(features, conv_weight, bias)
+    halos = []
+    for start, edge in ((0, edge_one), (1, edge_two)):
+        pairs = [(i, i + 1) for i in range(start, mesh_rows - 1, 2)]
+        halos.append(lax.ppermute(edge, "row", pairs + [(j, i) for i, j in pairs]))
+    bands = head((tile, *prepared), *halos, band, mesh_cols)
+    blocks = [bands[0]] * mesh_cols
+    for k in range(mesh_cols - 1, 0, -1):
+        blocks[k] = lax.ppermute(bands[k], "col", [(i, i ^ k) for i in range(mesh_cols)])
+    spectrum = forward_y(blocks, colors, band, parts)
+    table = transfer(inv_wavelength, distance, (height, width, parts, 2 * mesh_cols, block))
     spectrum = lax.all_to_all(spectrum, ("row", "col"), split_axis=0, concat_axis=0, tiled=True)
     back = middle(spectrum.reshape(groups, colors, band, 2 * block), table)
     back = lax.all_to_all(back, ("row", "col"), split_axis=0, concat_axis=0, tiled=True)

time: 93.5 us -> 86.7 us (0.927)
  local copies, waits for them, and re-layouts: 7.22 us -> 0.07 us
  waiting for transfers between devices: 27.9 us -> 25.1 us
  starting transfers between devices: 19.4 us -> 21.6 us
  Pallas kernels: 13.7 us -> 14.9 us
    unnamed x31 -> x12, local copies, waits for them, and re-layouts: 6.26 us -> 0.03 us
    all_to_all x1, starting transfers between devices: 4.63 us -> 9.2 us  [per_device(): lax.all_to_all(spectrum, ('row', 'col'), split_axis=0, concat_axis=0, til...]
    ppermute x2, waiting for transfers between devices: 3.53 us -> 0.98 us  [per_device(): halos.append(lax.ppermute(edge, 'row', pairs + [(j, i) for i, j in pairs]))]
    ppermute x2, starting transfers between devices: 6.13 us -> 3.65 us  [per_device(): halos.append(lax.ppermute(edge, 'row', pairs + [(j, i) for i, j in pairs]))]
    pallas_call x2 -> x3, Pallas kernels: 4.45 us -> 5.7 us  [the longest x1 2.76 us: transfer(): pl.pallas_call(partial(transfer_kernel, sizes), grid=(colors + 1, n), out...]
  transfers between devices with their start and end apart: 10 -> 10, of which waited for: 5 -> 4; matrix products, arithmetic and copies ran while one was open for 1% -> 0% of each run, Pallas kernels for 2% -> 3%
where the time goes in v2:
time: 86.7 us; the launch traced here: 86.5 us
  waiting for transfers between devices  25.1 us (29%)
  blocking collectives  24 us (28%)
  starting transfers between devices  21.6 us (25%)
  Pallas kernels  14.9 us (17%)
    all_to_all x1, blocking collectives, per_device(): lax.all_to_all(back, ('row', 'col'), split_axis=0, concat_axis=0, tiled=T...  24 us
    all_to_all x1, waiting for transfers between devices, per_device(): lax.all_to_all(spectrum, ('row', 'col'), split_axis=0, concat_axis=0, til...  18.5 us
    all_to_all x1, starting transfers between devices, per_device(): lax.all_to_all(spectrum, ('row', 'col'), split_axis=0, concat_axis=0, til...  9.2 us
    ppermute x7, starting transfers between devices, per_device(): lax.ppermute(bands[k], 'col', [(i, i ^ k) for i in range(mesh_cols)])  8.78 us
    ppermute x7, waiting for transfers between devices, per_device(): lax.ppermute(bands[k], 'col', [(i, i ^ k) for i in range(mesh_cols)])  5.56 us
    pallas_call x1, Pallas kernels, middle(): pl.pallas_call(middle_kernel, out_shape=jax.ShapeDtypeStruct(coded.shape,...  3.72 us
    ppermute x2, starting transfers between devices, per_device(): halos.append(lax.ppermute(edge, 'row', pairs + [(j, i) for i, j in pairs]))  3.65 us
    pallas_call x1, Pallas kernels, forward_y(): pl.pallas_call(partial(forward_y_kernel, colors, band, parts), out_shape=...  3.13 us
  transfers between devices with their start and end apart: 10, of which 4 were waited for; matrix products, arithmetic and copies ran while one was open for 0% of the time, Pallas kernels for 3%

profile of v2, /device:TPU:0, one launch (start us, length us, event | category | flops | bytes accessed | tf_op | source)
XLA Modules:
  0.0 86.5 jit_solution(11406261230182724084)
XLA Ops:
  0.0 1.8 %prepare.1 = (bf16[16,256,256]{2,1,0:T(8,128)(2,1)S(1)}, bf16[16,256]{1,0:T(8,128)(2,1)S(1)}, bf16[16,256]{1,0:T(8,128)(2,1)S(1)}, bf16[216,256]{1,0:T(8,128)(2,...) custom-call(bf16[16,256,256]{2,1,0:T(8,128)(2,1)} %feat.1, bf16[3,3,3,16]{3,2,1,0:T(4,128)(2,1)} %bitcast.19, ...), custom_call_target="tpu_custom_call" | custom-call | tf_op jit(solution)/shard_map/prepare/pallas_call | solution.py:228
  1.8 0.0 copy-start
  1.8 0.0 copy-start.3
  1.8 0.0 copy-start.4
  1.8 3.0 %collective-permute-start = (bf16[16,256]{1,0:T(8,128)(2,1)S(1)}, bf16[16,256]{1,0:T(8,128)(2,1)S(1)}, u32[]{:S(2)}, u32[]{:S(2)}) collective-permute-start(bf16[16,256]{1,0:T(8,128)(2,1)S(1)} %get-tuple-element.12), channel_id=1, source_target_pairs={{0,8},{16,24},{8,0},{24,16},{1,9},{17,25},{9,1},{25,17},{2,10},{18... | collective-permute-start | bytes 24584 | tf_op jit(solution)/shard_map/ppermute | solution.py:602
  4.8 0.6 collective-permute-start.1
  5.5 1.0 %collective-permute-done.first_halo = bf16[16,256]{1,0:T(8,128)(2,1)S(1)} collective-permute-done((bf16[16,256]{1,0:T(8,128)(2,1)S(1)}, bf16[16,256]{1,0:T(8,128)(2,1)S(1)}, u32[]{:S(2)}, u32[]{:S(2)}) %collective-permute-start) | collective-permute-done | bytes 8224 | tf_op jit(solution)/shard_map/ppermute | solution.py:602
  6.4 0.0 collective-permute-done.1.second_halo
  6.4 1.2 %conv_head.1 = bf16[8,208,128]{2,1,0:T(8,128)(2,1)S(1)} custom-call(bf16[16,256,256]{2,1,0:T(8,128)(2,1)S(1)} %get-tuple-element.11.feat, bf16[16,256]{1,0:T(8,128)(2,1)S(1)} %collective-permute-done.first_halo, bf16[16,256]{1,0:T(8,128)(2,1)S(1)} %collective-permute-done.1.second_halo, bf16[216,256]{1,0:T(8,128)(2,1)S(1)} %get-tuple-element.14.table, ...), custom_call_target="tpu_custom_call" | custom-call | tf_op jit(solution)/shard_map/conv_head/pallas_call | solution.py:334
  7.6 0.0 copy-start.5
  7.7 0.1 collective-permute-start.2
  7.8 2.2 %collective-permute-start.3 = (bf16[208,128]{1,0:T(8,128)(2,1)S(1)}, bf16[208,128]{1,0:T(8,128)(2,1)S(1)}, u32[]{:S(2)}, u32[]{:S(2)}) collective-permute-start(bf16[208,128]{1,0:T(8,128)(2,1)S(1)} %get-tuple-element.22), channel_id=1, source_target_pairs={{0,2},{1,3},{2,0},{3,1},{4,6},{5,7},{6,4},{7,5},{8,10},{9,11},{10,... | collective-permute-start | bytes 159752 | tf_op jit(solution)/shard_map/ppermute | solution.py:606
  9.9 0.1 collective-permute-start.4
  10.0 2.8 %collective-permute-start.5 = (bf16[208,128]{1,0:T(8,128)(2,1)S(1)}, bf16[208,128]{1,0:T(8,128)(2,1)S(1)}, u32[]{:S(2)}, u32[]{:S(2)}) collective-permute-start(bf16[208,128]{1,0:T(8,128)(2,1)S(1)} %get-tuple-element.20), channel_id=1, source_target_pairs={{0,4},{1,5},{2,6},{3,7},{4,0},{5,1},{6,2},{7,3},{8,12},{9,13},{10,... | collective-permute-start | bytes 159752 | tf_op jit(solution)/shard_map/ppermute | solution.py:606
  12.8 0.0 collective-permute-start.6
  12.8 0.0 collective-permute-done.2.refs_1_
  12.8 3.6 %collective-permute-start.7 = (bf16[208,128]{1,0:T(8,128)(2,1)S(1)}, bf16[208,128]{1,0:T(8,128)(2,1)S(1)}, u32[]{:S(2)}, u32[]{:S(2)}) collective-permute-start(bf16[208,128]{1,0:T(8,128)(2,1)S(1)} %get-tuple-element.18), channel_id=1, source_target_pairs={{0,6},{1,7},{2,4},{3,5},{4,2},{5,3},{6,0},{7,1},{8,14},{9,15},{10,... | collective-permute-start | bytes 159752 | tf_op jit(solution)/shard_map/ppermute | solution.py:606
  16.4 0.0 collective-permute-done.3.refs_2_
  16.4 0.1 collective-permute-start.8
  16.5 0.0 collective-permute-done.4.refs_3_
  16.5 0.0 collective-permute-done.5.refs_4_
  16.5 4.1 %collective-permute-done.6.refs_5_ = bf16[208,128]{1,0:T(8,128)(2,1)S(1)} collective-permute-done((bf16[208,128]{1,0:T(8,128)(2,1)S(1)}, bf16[208,128]{1,0:T(8,128)(2,1)S(1)}, u32[]{:S(2)}, u32[]{:S(2)}) %collective-permute-start.6) | collective-permute-done | bytes 53280 | tf_op jit(solution)/shard_map/ppermute | solution.py:606
  20.6 0.0 collective-permute-done.7.refs_6_
  20.6 1.4 %collective-permute-done.8.refs_7_ = bf16[208,128]{1,0:T(8,128)(2,1)S(1)} collective-permute-done((bf16[208,128]{1,0:T(8,128)(2,1)S(1)}, bf16[208,128]{1,0:T(8,128)(2,1)S(1)}, u32[]{:S(2)}, u32[]{:S(2)}) %collective-permute-start.8) | collective-permute-done | bytes 53280 | tf_op jit(solution)/shard_map/ppermute | solution.py:606
  22.0 0.0 copy-done
  22.0 0.0 copy-done.3
  22.1 0.0 copy-done.4
  22.1 3.1 %forward_y.1 = bf16[32,96,128]{2,1,0:T(8,128)(2,1)} custom-call(bf16[208,128]{1,0:T(8,128)(2,1)S(1)} %get-tuple-element.24.refs_0_, bf16[208,128]{1,0:T(8,128)(2,1)S(1)} %collective-permute-done.2.refs_1_, bf16[208,128]{1,0:T(8,128)(2,1)S(1)} %collective-permute-done.3.refs_2_, bf16[208,128]{1,0:T(8,128)(2,1)S(1)} %collective-permute-done.4.refs_3_, ...), custom_call_target="tpu_custom_call" | custom-call | tf_op jit(solution)/shard_map/forward_y/pallas_call | solution.py:397
  25.2 0.0 copy-start.2
  25.2 9.2 %all-to-all-start = ((bf16[32,96,128]{2,1,0:T(8,128)(2,1)}), bf16[32,96,128]{2,1,0:T(8,128)(2,1)S(1)}, u32[]{:S(2)}, u32[]{:S(2)}) async-start(bf16[32,96,128]{2,1,0:T(8,128)(2,1)} %forward_y.1), calls=%async_computation | async-start | bytes 1572864 | tf_op jit(solution)/shard_map/all_to_all | solution.py:609
  35.0 0.0 copy-done.5
  35.0 2.8 %transfer.1.tables = f32[4,4,2,128,128]{4,3,2,1,0:T(8,128)S(1)} custom-call(f32[3]{0:T(128)S(1)} %copy-done.5, f32[1]{0:T(128)S(6)} %copy.13.travel), custom_call_target="tpu_custom_call" | custom-call | tf_op jit(solution)/shard_map/transfer/pallas_call | solution.py:448
  37.8 18.5 %all-to-all-done = bf16[32,96,128]{2,1,0:T(8,128)(2,1)S(1)} async-done(((bf16[32,96,128]{2,1,0:T(8,128)(2,1)}), bf16[32,96,128]{2,1,0:T(8,128)(2,1)S(1)}, u32[]{:S(2)}, u32[]{:S(2)}) %all-to-all-start) | async-done | bytes 786464 | tf_op jit(solution)/shard_map/all_to_all | solution.py:609
  56.4 0.0 copy-done.2
  56.4 0.0 copy-start.1
  56.4 3.7 %middle_x.1 = bf16[32,3,32,128]{3,2,1,0:T(8,128)(2,1)S(1)} custom-call(bf16[32,3,32,128]{3,2,1,0:T(8,128)(2,1)S(1)} %bitcast.18, f32[4,4,2,128,128]{4,3,2,1,0:T(8,128)S(1)} %transfer.1.tables, bf16[256,768]{1,0:T(8,128)(2,1)S(1)} %copy-done.2), custom_call_target="tpu_custom_call" | custom-call | tf_op jit(solution)/shard_map/middle_x/pallas_call | solution.py:528
  60.1 24.0 %all_to_all.10.coded = bf16[32,3,32,128]{3,2,1,0:T(8,128)(2,1)S(1)} all-to-all(bf16[32,3,32,128]{3,2,1,0:T(8,128)(2,1)S(1)} %middle_x.1), channel_id=1, replica_groups=mesh['row'=4,'col'=8] {'row','col'}, dimensions={0} | all-to-all | bytes 1572864 | tf_op jit(solution)/shard_map/all_to_all | solution.py:611
  84.1 0.0 copy-done.1
  84.1 2.4 %inverse_y.1 = bf16[3,2,32,2048]{3,2,1,0:T(8,128)(2,1)} custom-call(bf16[32,3,32,128]{3,2,1,0:T(8,128)(2,1)S(1)} %all_to_all.10.coded, bf16[768,256]{1,0:T(8,128)(2,1)S(1)} %copy-done.1, f32[16,128]{1,0:T(8,128)S(1)} %copy-done.3, f32[16,128]{1,0:T(8,128)S(1)} %copy-done.4), custom_call_target="tpu_custom_call" | custom-call | tf_op jit(solution)/shard_map/inverse_y/pallas_call | solution.py:572
  (1 shorter events, 0.0 us)
Async XLA Ops:
  1.8 20.3 %copy-start = (bf16[768,256]{1,0:T(8,128)(2,1)S(1)}, bf16[768,256]{1,0:T(8,128)(2,1)}, u32[]{:S(2)}) copy-start(bf16[768,256]{1,0:T(8,128)(2,1)} %constant.10.clone.refs_8_) | copy-start | bytes 1179652
  1.8 20.3 %copy-start.3 = (f32[16,128]{1,0:T(8,128)S(1)}, f32[16,128]{1,0:T(8,128)}, u32[]{:S(2)}) copy-start(f32[16,128]{1,0:T(8,128)} %constant.11.clone.refs_9_.tw_c) | copy-start | bytes 24580
  1.8 20.3 %copy-start.4 = (f32[16,128]{1,0:T(8,128)S(1)}, f32[16,128]{1,0:T(8,128)}, u32[]{:S(2)}) copy-start(f32[16,128]{1,0:T(8,128)} %constant.12.clone.refs_10_.tw_s) | copy-start | bytes 24580
  1.8 4.6 %collective-permute-start = (bf16[16,256]{1,0:T(8,128)(2,1)S(1)}, bf16[16,256]{1,0:T(8,128)(2,1)S(1)}, u32[]{:S(2)}, u32[]{:S(2)}) collective-permute-start(bf16[16,256]{1,0:T(8,128)(2,1)S(1)} %get-tuple-element.12), channel_id=1, source_target_pairs={{0,8},{16,24},{8,0},{24,16},{1,9},{17,25},{9,1},{25,17},{2,10},{18... | collective-permute-start | bytes 24584 | tf_op jit(solution)/shard_map/ppermute | solution.py:602
  4.8 1.6 %collective-permute-start.1 = (bf16[16,256]{1,0:T(8,128)(2,1)S(1)}, bf16[16,256]{1,0:T(8,128)(2,1)S(1)}, u32[]{:S(2)}, u32[]{:S(2)}) collective-permute-start(bf16[16,256]{1,0:T(8,128)(2,1)S(1)} %get-tuple-element.13), channel_id=1, source_target_pairs={{8,16},{16,8},{9,17},{17,9},{10,18},{18,10},{11,19},{19,11},{12,20... | collective-permute-start | bytes 24584 | tf_op jit(solution)/shard_map/ppermute | solution.py:602
  7.6 27.4 %copy-start.5 = (f32[3]{0:T(128)S(1)}, f32[3]{0:T(128)}, u32[]{:S(2)}) copy-start(f32[3]{0:T(128)} %wave.1) | copy-start | bytes 40
  7.7 5.1 %collective-permute-start.2 = (bf16[208,128]{1,0:T(8,128)(2,1)S(1)}, bf16[208,128]{1,0:T(8,128)(2,1)S(1)}, u32[]{:S(2)}, u32[]{:S(2)}) collective-permute-start(bf16[208,128]{1,0:T(8,128)(2,1)S(1)} %get-tuple-element.23), channel_id=1, source_target_pairs={{0,1},{1,0},{2,3},{3,2},{4,5},{5,4},{6,7},{7,6},{8,9},{9,8},{10,11... | collective-permute-start | bytes 159752 | tf_op jit(solution)/shard_map/ppermute | solution.py:606
  7.8 8.6 %collective-permute-start.3 = (bf16[208,128]{1,0:T(8,128)(2,1)S(1)}, bf16[208,128]{1,0:T(8,128)(2,1)S(1)}, u32[]{:S(2)}, u32[]{:S(2)}) collective-permute-start(bf16[208,128]{1,0:T(8,128)(2,1)S(1)} %get-tuple-element.22), channel_id=1, source_target_pairs={{0,2},{1,3},{2,0},{3,1},{4,6},{5,7},{6,4},{7,5},{8,10},{9,11},{10,... | collective-permute-start | bytes 159752 | tf_op jit(solution)/shard_map/ppermute | solution.py:606
  9.9 6.5 %collective-permute-start.4 = (bf16[208,128]{1,0:T(8,128)(2,1)S(1)}, bf16[208,128]{1,0:T(8,128)(2,1)S(1)}, u32[]{:S(2)}, u32[]{:S(2)}) collective-permute-start(bf16[208,128]{1,0:T(8,128)(2,1)S(1)} %get-tuple-element.21), channel_id=1, source_target_pairs={{0,3},{1,2},{2,1},{3,0},{4,7},{5,6},{6,5},{7,4},{8,11},{9,10},{10,... | collective-permute-start | bytes 159752 | tf_op jit(solution)/shard_map/ppermute | solution.py:606
  10.0 6.5 %collective-permute-start.5 = (bf16[208,128]{1,0:T(8,128)(2,1)S(1)}, bf16[208,128]{1,0:T(8,128)(2,1)S(1)}, u32[]{:S(2)}, u32[]{:S(2)}) collective-permute-start(bf16[208,128]{1,0:T(8,128)(2,1)S(1)} %get-tuple-element.20), channel_id=1, source_target_pairs={{0,4},{1,5},{2,6},{3,7},{4,0},{5,1},{6,2},{7,3},{8,12},{9,13},{10,... | collective-permute-start | bytes 159752 | tf_op jit(solution)/shard_map/ppermute | solution.py:606
  12.8 7.9 %collective-permute-start.6 = (bf16[208,128]{1,0:T(8,128)(2,1)S(1)}, bf16[208,128]{1,0:T(8,128)(2,1)S(1)}, u32[]{:S(2)}, u32[]{:S(2)}) collective-permute-start(bf16[208,128]{1,0:T(8,128)(2,1)S(1)} %get-tuple-element.19), channel_id=1, source_target_pairs={{0,5},{1,4},{2,7},{3,6},{4,1},{5,0},{6,3},{7,2},{8,13},{9,12},{10,... | collective-permute-start | bytes 159752 | tf_op jit(solution)/shard_map/ppermute | solution.py:606
  12.8 7.9 %collective-permute-start.7 = (bf16[208,128]{1,0:T(8,128)(2,1)S(1)}, bf16[208,128]{1,0:T(8,128)(2,1)S(1)}, u32[]{:S(2)}, u32[]{:S(2)}) collective-permute-start(bf16[208,128]{1,0:T(8,128)(2,1)S(1)} %get-tuple-element.18), channel_id=1, source_target_pairs={{0,6},{1,7},{2,4},{3,5},{4,2},{5,3},{6,0},{7,1},{8,14},{9,15},{10,... | collective-permute-start | bytes 159752 | tf_op jit(solution)/shard_map/ppermute | solution.py:606
  16.4 5.7 %collective-permute-start.8 = (bf16[208,128]{1,0:T(8,128)(2,1)S(1)}, bf16[208,128]{1,0:T(8,128)(2,1)S(1)}, u32[]{:S(2)}, u32[]{:S(2)}) collective-permute-start(bf16[208,128]{1,0:T(8,128)(2,1)S(1)} %get-tuple-element.17), channel_id=1, source_target_pairs={{0,7},{1,6},{2,5},{3,4},{4,3},{5,2},{6,1},{7,0},{8,15},{9,14},{10,... | collective-permute-start | bytes 159752 | tf_op jit(solution)/shard_map/ppermute | solution.py:606
  25.2 31.2 %copy-start.2 = (bf16[256,768]{1,0:T(8,128)(2,1)S(1)}, bf16[256,768]{1,0:T(8,128)(2,1)}, u32[]{:S(2)}) copy-start(bf16[256,768]{1,0:T(8,128)(2,1)} %constant.13.clone.matrix) | copy-start | bytes 1179652
  25.2 31.2 %all-to-all-start = ((bf16[32,96,128]{2,1,0:T(8,128)(2,1)}), bf16[32,96,128]{2,1,0:T(8,128)(2,1)S(1)}, u32[]{:S(2)}, u32[]{:S(2)}) async-start(bf16[32,96,128]{2,1,0:T(8,128)(2,1)} %forward_y.1), calls=%async_computation | async-start | bytes 1572864 | tf_op jit(solution)/shard_map/all_to_all | solution.py:609
  56.4 27.7 %copy-start.1 = (bf16[768,256]{1,0:T(8,128)(2,1)S(1)}, bf16[768,256]{1,0:T(8,128)(2,1)}, u32[]{:S(2)}) copy-start(bf16[768,256]{1,0:T(8,128)(2,1)} %constant.14.clone.matrix) | copy-start | bytes 1179652

commit v3 on v2

--- a/solution.py
+++ b/solution.py
@@ -248,7 +248,7 @@
     )(*(pltpu.with_memory_space_constraint(x, pltpu.HBM) for x in (features, weight, bias)))
 
 
-def head_kernel(colors, chans, band, feat, first_halo, second_halo, table, ring_table, bias, out):
+def head_kernel(colors, chans, band, second_halo, first_halo, feat, table, ring_table, bias, out):
     peers = out.shape[0]
     step = 16
     per = band // step
@@ -326,7 +326,7 @@
         finish(j)
 
 
-def head(prepared, above, below, band, peers):
+def head(prepared, second_halo, first_halo, band, peers):
     features, table, ring_table, bias = prepared
     chans, rows, cols = features.shape
     colors = bias.shape[0]
@@ -338,14 +338,18 @@
         out_specs=vm,
         compiler_params=pltpu.CompilerParams(vmem_limit_bytes=VMEM_LIMIT),
         name="conv_head",
-    )(features, above, below, table, ring_table, bias)
+    )(second_halo, first_halo, features, table, ring_table, bias)
+
+
+def sending_order(peers):
+    return [*range(peers - 2, 0, -2), *range(peers - 1, 0, -2), 0]
 
 
 def forward_y_kernel(colors, band, parts, *refs):
     peers = len(refs) - 6
     matrix, tw_c, tw_s, out, coded, left = refs[peers:]
-    for k in range(peers):
-        coded[lax.axis_index("col") ^ k] = refs[k][...]
+    for i, k in enumerate(sending_order(peers)):
+        coded[lax.axis_index("col") ^ k] = refs[i][...]
     step = 16
     lane = lax.broadcasted_iota(jnp.int32, (1, HALF), 1)
     for o in range(colors):
@@ -405,7 +409,7 @@
         ],
         compiler_params=pltpu.CompilerParams(vmem_limit_bytes=VMEM_LIMIT),
         name="forward_y",
-    )(*blocks, jnp.asarray(matrix), jnp.asarray(tw_c, F32), jnp.asarray(tw_s, F32))
+    )(*(blocks[k] for k in sending_order(peers)), jnp.asarray(matrix), jnp.asarray(tw_c, F32), jnp.asarray(tw_s, F32))
 
 
 def transfer_kernel(sizes, wave, travel, out):
@@ -597,7 +601,7 @@
     parts = mesh_rows // 2
     tile, edge_one, edge_two, *prepared = prepare(features, conv_weight, bias)
     halos = []
-    for start, edge in ((0, edge_one), (1, edge_two)):
+    for start, edge in ((1, edge_two), (0, edge_one)):
         pairs = [(i, i + 1) for i in range(start, mesh_rows - 1, 2)]
         halos.append(lax.ppermute(edge, "row", pairs + [(j, i) for i, j in pairs]))
     bands = head((tile, *prepared), *halos, band, mesh_cols)

time: 86.7 us -> 83.1 us (0.958)
  starting transfers between devices: 21.6 us -> 18.4 us
    all_to_all x1, starting transfers between devices: 9.2 us -> 3.53 us  [per_device(): lax.all_to_all(spectrum, ('row', 'col'), split_axis=0, concat_axis=0, til...]
    ppermute x2, starting transfers between devices: 3.65 us -> 6.53 us  [per_device(): halos.append(lax.ppermute(edge, 'row', pairs + [(j, i) for i, j in pairs]))]
    ppermute x7, waiting for transfers between devices: 5.56 us -> 4.45 us  [per_device(): lax.ppermute(bands[k], 'col', [(i, i ^ k) for i in range(mesh_cols)])]
  transfers between devices with their start and end apart: 10 -> 10, of which waited for: 4 -> 5; matrix products, arithmetic and copies ran while one was open for 0% -> 0% of each run, Pallas kernels for 3% -> 3%
where the time goes in v3:
time: 83.1 us; the launch traced here: 82.8 us
  waiting for transfers between devices  24.6 us (30%)
  blocking collectives  24 us (29%)
  starting transfers between devices  18.4 us (22%)
  Pallas kernels  15 us (18%)
    all_to_all x1, blocking collectives, per_device(): lax.all_to_all(back, ('row', 'col'), split_axis=0, concat_axis=0, tiled=T...  24 us
    all_to_all x1, waiting for transfers between devices, per_device(): lax.all_to_all(spectrum, ('row', 'col'), split_axis=0, concat_axis=0, til...  18.5 us
    ppermute x7, starting transfers between devices, per_device(): lax.ppermute(bands[k], 'col', [(i, i ^ k) for i in range(mesh_cols)])  8.34 us
    ppermute x2, starting transfers between devices, per_device(): halos.append(lax.ppermute(edge, 'row', pairs + [(j, i) for i, j in pairs]))  6.53 us
    ppermute x7, waiting for transfers between devices, per_device(): lax.ppermute(bands[k], 'col', [(i, i ^ k) for i in range(mesh_cols)])  4.45 us
    pallas_call x1, Pallas kernels, middle(): pl.pallas_call(middle_kernel, out_shape=jax.ShapeDtypeStruct(coded.shape,...  3.72 us
    all_to_all x1, starting transfers between devices, per_device(): lax.all_to_all(spectrum, ('row', 'col'), split_axis=0, concat_axis=0, til...  3.53 us
    pallas_call x1, Pallas kernels, forward_y(): pl.pallas_call(partial(forward_y_kernel, colors, band, parts), out_shape=...  3.13 us
  transfers between devices with their start and end apart: 10, of which 5 were waited for; matrix products, arithmetic and copies ran while one was open for 0% of the time, Pallas kernels for 3%

profile of v3, /device:TPU:0, one launch (start us, length us, event | category | flops | bytes accessed | tf_op | source)
XLA Modules:
  0.0 82.8 jit_solution(15691206795583332763)
XLA Ops:
  0.0 1.8 %prepare.1 = (bf16[16,256,256]{2,1,0:T(8,128)(2,1)S(1)}, bf16[16,256]{1,0:T(8,128)(2,1)S(1)}, bf16[16,256]{1,0:T(8,128)(2,1)S(1)}, bf16[216,256]{1,0:T(8,128)(2,...) custom-call(bf16[16,256,256]{2,1,0:T(8,128)(2,1)} %feat.1, bf16[3,3,3,16]{3,2,1,0:T(4,128)(2,1)} %bitcast.19, ...), custom_call_target="tpu_custom_call" | custom-call | tf_op jit(solution)/shard_map/prepare/pallas_call | solution.py:228
  1.8 0.0 copy-start
  1.8 0.0 copy-start.3
  1.8 0.0 copy-start.4
  1.8 0.8 collective-permute-start
  2.6 5.7 %collective-permute-start.1 = (bf16[16,256]{1,0:T(8,128)(2,1)S(1)}, bf16[16,256]{1,0:T(8,128)(2,1)S(1)}, u32[]{:S(2)}, u32[]{:S(2)}) collective-permute-start(bf16[16,256]{1,0:T(8,128)(2,1)S(1)} %get-tuple-element.12), channel_id=1, source_target_pairs={{0,8},{16,24},{8,0},{24,16},{1,9},{17,25},{9,1},{25,17},{2,10},{18... | collective-permute-start | bytes 24584 | tf_op jit(solution)/shard_map/ppermute | solution.py:606
  8.3 0.0 collective-permute-done.second_halo
  8.3 1.6 %collective-permute-done.1.first_halo = bf16[16,256]{1,0:T(8,128)(2,1)S(1)} collective-permute-done((bf16[16,256]{1,0:T(8,128)(2,1)S(1)}, bf16[16,256]{1,0:T(8,128)(2,1)S(1)}, u32[]{:S(2)}, u32[]{:S(2)}) %collective-permute-start.1) | collective-permute-done | bytes 8224 | tf_op jit(solution)/shard_map/ppermute | solution.py:606
  10.0 1.2 %conv_head.1 = bf16[8,208,128]{2,1,0:T(8,128)(2,1)S(1)} custom-call(bf16[16,256]{1,0:T(8,128)(2,1)S(1)} %collective-permute-done.second_halo, bf16[16,256]{1,0:T(8,128)(2,1)S(1)} %collective-permute-done.1.first_halo, bf16[16,256,256]{2,1,0:T(8,128)(2,1)S(1)} %get-tuple-element.13.feat, bf16[216,256]{1,0:T(8,128)(2,1)S(1)} %get-tuple-element.14.table, ...), custom_call_target="tpu_custom_call" | custom-call | tf_op jit(solution)/shard_map/conv_head/pallas_call | solution.py:334
  11.2 0.0 copy-start.5
  11.2 3.7 %collective-permute-start.2 = (bf16[208,128]{1,0:T(8,128)(2,1)S(1)}, bf16[208,128]{1,0:T(8,128)(2,1)S(1)}, u32[]{:S(2)}, u32[]{:S(2)}) collective-permute-start(bf16[208,128]{1,0:T(8,128)(2,1)S(1)} %get-tuple-element.24), channel_id=1, source_target_pairs={{0,6},{1,7},{2,4},{3,5},{4,2},{5,3},{6,0},{7,1},{8,14},{9,15},{10,... | collective-permute-start | bytes 159752 | tf_op jit(solution)/shard_map/ppermute | solution.py:610
  14.9 0.0 collective-permute-start.3
  14.9 0.8 collective-permute-start.4
  15.7 1.1 %collective-permute-start.5 = (bf16[208,128]{1,0:T(8,128)(2,1)S(1)}, bf16[208,128]{1,0:T(8,128)(2,1)S(1)}, u32[]{:S(2)}, u32[]{:S(2)}) collective-permute-start(bf16[208,128]{1,0:T(8,128)(2,1)S(1)} %get-tuple-element.21), channel_id=1, source_target_pairs={{0,7},{1,6},{2,5},{3,4},{4,3},{5,2},{6,1},{7,0},{8,15},{9,14},{10,... | collective-permute-start | bytes 159752 | tf_op jit(solution)/shard_map/ppermute | solution.py:610
  16.7 1.4 %collective-permute-start.6 = (bf16[208,128]{1,0:T(8,128)(2,1)S(1)}, bf16[208,128]{1,0:T(8,128)(2,1)S(1)}, u32[]{:S(2)}, u32[]{:S(2)}) collective-permute-start(bf16[208,128]{1,0:T(8,128)(2,1)S(1)} %get-tuple-element.20), channel_id=1, source_target_pairs={{0,5},{1,4},{2,7},{3,6},{4,1},{5,0},{6,3},{7,2},{8,13},{9,12},{10,... | collective-permute-start | bytes 159752 | tf_op jit(solution)/shard_map/ppermute | solution.py:610
  18.1 0.0 collective-permute-done.2.refs_0_
  18.1 1.5 %collective-permute-start.7 = (bf16[208,128]{1,0:T(8,128)(2,1)S(1)}, bf16[208,128]{1,0:T(8,128)(2,1)S(1)}, u32[]{:S(2)}, u32[]{:S(2)}) collective-permute-start(bf16[208,128]{1,0:T(8,128)(2,1)S(1)} %get-tuple-element.19), channel_id=1, source_target_pairs={{0,3},{1,2},{2,1},{3,0},{4,7},{5,6},{6,5},{7,4},{8,11},{9,10},{10,... | collective-permute-start | bytes 159752 | tf_op jit(solution)/shard_map/ppermute | solution.py:610
  19.6 0.9 %collective-permute-done.3.refs_1_ = bf16[208,128]{1,0:T(8,128)(2,1)S(1)} collective-permute-done((bf16[208,128]{1,0:T(8,128)(2,1)S(1)}, bf16[208,128]{1,0:T(8,128)(2,1)S(1)}, u32[]{:S(2)}, u32[]{:S(2)}) %collective-permute-start.3) | collective-permute-done | bytes 53280 | tf_op jit(solution)/shard_map/ppermute | solution.py:610
  20.5 0.0 collective-permute-start.8
  20.5 0.0 collective-permute-done.4.refs_2_
  20.5 0.8 %collective-permute-done.5.refs_3_ = bf16[208,128]{1,0:T(8,128)(2,1)S(1)} collective-permute-done((bf16[208,128]{1,0:T(8,128)(2,1)S(1)}, bf16[208,128]{1,0:T(8,128)(2,1)S(1)}, u32[]{:S(2)}, u32[]{:S(2)}) %collective-permute-start.5) | collective-permute-done | bytes 53280 | tf_op jit(solution)/shard_map/ppermute | solution.py:610
  21.3 2.7 %collective-permute-done.6.refs_4_ = bf16[208,128]{1,0:T(8,128)(2,1)S(1)} collective-permute-done((bf16[208,128]{1,0:T(8,128)(2,1)S(1)}, bf16[208,128]{1,0:T(8,128)(2,1)S(1)}, u32[]{:S(2)}, u32[]{:S(2)}) %collective-permute-start.6) | collective-permute-done | bytes 53280 | tf_op jit(solution)/shard_map/ppermute | solution.py:610
  24.0 0.0 collective-permute-done.7.refs_5_
  24.0 0.0 collective-permute-done.8.refs_6_
  24.0 0.0 copy-done
  24.0 0.0 copy-done.3
  24.0 0.0 copy-done.4
  24.0 3.1 %forward_y.1 = bf16[32,96,128]{2,1,0:T(8,128)(2,1)} custom-call(bf16[208,128]{1,0:T(8,128)(2,1)S(1)} %collective-permute-done.2.refs_0_, bf16[208,128]{1,0:T(8,128)(2,1)S(1)} %collective-permute-done.3.refs_1_, bf16[208,128]{1,0:T(8,128)(2,1)S(1)} %collective-permute-done.4.refs_2_, bf16[208,128]{1,0:T(8,128)(2,1)S(1)} %collective-permute-done.5.refs_3_, ...), custom_call_target="tpu_custom_call" | custom-call | tf_op jit(solution)/shard_map/forward_y/pallas_call | solution.py:401
  27.2 0.0 copy-start.2
  27.2 3.5 %all-to-all-start = ((bf16[32,96,128]{2,1,0:T(8,128)(2,1)}), bf16[32,96,128]{2,1,0:T(8,128)(2,1)S(1)}, u32[]{:S(2)}, u32[]{:S(2)}) async-start(bf16[32,96,128]{2,1,0:T(8,128)(2,1)} %forward_y.1), calls=%async_computation | async-start | bytes 1572864 | tf_op jit(solution)/shard_map/all_to_all | solution.py:613
  31.4 0.0 copy-done.5
  31.4 2.8 %transfer.1.tables = f32[4,4,2,128,128]{4,3,2,1,0:T(8,128)S(1)} custom-call(f32[3]{0:T(128)S(1)} %copy-done.5, f32[1]{0:T(128)S(6)} %copy.13.travel), custom_call_target="tpu_custom_call" | custom-call | tf_op jit(solution)/shard_map/transfer/pallas_call | solution.py:452
  34.1 18.5 %all-to-all-done = bf16[32,96,128]{2,1,0:T(8,128)(2,1)S(1)} async-done(((bf16[32,96,128]{2,1,0:T(8,128)(2,1)}), bf16[32,96,128]{2,1,0:T(8,128)(2,1)S(1)}, u32[]{:S(2)}, u32[]{:S(2)}) %all-to-all-start) | async-done | bytes 786464 | tf_op jit(solution)/shard_map/all_to_all | solution.py:613
  52.7 0.0 copy-done.2
  52.7 0.0 copy-start.1
  52.7 3.7 %middle_x.1 = bf16[32,3,32,128]{3,2,1,0:T(8,128)(2,1)S(1)} custom-call(bf16[32,3,32,128]{3,2,1,0:T(8,128)(2,1)S(1)} %bitcast.18, f32[4,4,2,128,128]{4,3,2,1,0:T(8,128)S(1)} %transfer.1.tables, bf16[256,768]{1,0:T(8,128)(2,1)S(1)} %copy-done.2), custom_call_target="tpu_custom_call" | custom-call | tf_op jit(solution)/shard_map/middle_x/pallas_call | solution.py:532
  56.4 24.0 %all_to_all.10.coded = bf16[32,3,32,128]{3,2,1,0:T(8,128)(2,1)S(1)} all-to-all(bf16[32,3,32,128]{3,2,1,0:T(8,128)(2,1)S(1)} %middle_x.1), channel_id=1, replica_groups=mesh['row'=4,'col'=8] {'row','col'}, dimensions={0} | all-to-all | bytes 1572864 | tf_op jit(solution)/shard_map/all_to_all | solution.py:615
  80.4 0.0 copy-done.1
  80.4 2.4 %inverse_y.1 = bf16[3,2,32,2048]{3,2,1,0:T(8,128)(2,1)} custom-call(bf16[32,3,32,128]{3,2,1,0:T(8,128)(2,1)S(1)} %all_to_all.10.coded, bf16[768,256]{1,0:T(8,128)(2,1)S(1)} %copy-done.1, f32[16,128]{1,0:T(8,128)S(1)} %copy-done.3, f32[16,128]{1,0:T(8,128)S(1)} %copy-done.4), custom_call_target="tpu_custom_call" | custom-call | tf_op jit(solution)/shard_map/inverse_y/pallas_call | solution.py:576
  (1 shorter events, 0.0 us)
Async XLA Ops:
  1.8 22.3 %copy-start = (bf16[768,256]{1,0:T(8,128)(2,1)S(1)}, bf16[768,256]{1,0:T(8,128)(2,1)}, u32[]{:S(2)}) copy-start(bf16[768,256]{1,0:T(8,128)(2,1)} %constant.10.clone.refs_8_) | copy-start | bytes 1179652
  1.8 22.3 %copy-start.3 = (f32[16,128]{1,0:T(8,128)S(1)}, f32[16,128]{1,0:T(8,128)}, u32[]{:S(2)}) copy-start(f32[16,128]{1,0:T(8,128)} %constant.11.clone.refs_9_.tw_c) | copy-start | bytes 24580
  1.8 22.3 %copy-start.4 = (f32[16,128]{1,0:T(8,128)S(1)}, f32[16,128]{1,0:T(8,128)}, u32[]{:S(2)}) copy-start(f32[16,128]{1,0:T(8,128)} %constant.12.clone.refs_10_.tw_s) | copy-start | bytes 24580
  1.8 6.5 %collective-permute-start = (bf16[16,256]{1,0:T(8,128)(2,1)S(1)}, bf16[16,256]{1,0:T(8,128)(2,1)S(1)}, u32[]{:S(2)}, u32[]{:S(2)}) collective-permute-start(bf16[16,256]{1,0:T(8,128)(2,1)S(1)} %get-tuple-element.11), channel_id=1, source_target_pairs={{8,16},{16,8},{9,17},{17,9},{10,18},{18,10},{11,19},{19,11},{12,20... | collective-permute-start | bytes 24584 | tf_op jit(solution)/shard_map/ppermute | solution.py:606
  2.6 7.4 %collective-permute-start.1 = (bf16[16,256]{1,0:T(8,128)(2,1)S(1)}, bf16[16,256]{1,0:T(8,128)(2,1)S(1)}, u32[]{:S(2)}, u32[]{:S(2)}) collective-permute-start(bf16[16,256]{1,0:T(8,128)(2,1)S(1)} %get-tuple-element.12), channel_id=1, source_target_pairs={{0,8},{16,24},{8,0},{24,16},{1,9},{17,25},{9,1},{25,17},{2,10},{18... | collective-permute-start | bytes 24584 | tf_op jit(solution)/shard_map/ppermute | solution.py:606
  11.2 20.2 %copy-start.5 = (f32[3]{0:T(128)S(1)}, f32[3]{0:T(128)}, u32[]{:S(2)}) copy-start(f32[3]{0:T(128)} %wave.1) | copy-start | bytes 40
  11.2 6.9 %collective-permute-start.2 = (bf16[208,128]{1,0:T(8,128)(2,1)S(1)}, bf16[208,128]{1,0:T(8,128)(2,1)S(1)}, u32[]{:S(2)}, u32[]{:S(2)}) collective-permute-start(bf16[208,128]{1,0:T(8,128)(2,1)S(1)} %get-tuple-element.24), channel_id=1, source_target_pairs={{0,6},{1,7},{2,4},{3,5},{4,2},{5,3},{6,0},{7,1},{8,14},{9,15},{10,... | collective-permute-start | bytes 159752 | tf_op jit(solution)/shard_map/ppermute | solution.py:610
  14.9 5.6 %collective-permute-start.3 = (bf16[208,128]{1,0:T(8,128)(2,1)S(1)}, bf16[208,128]{1,0:T(8,128)(2,1)S(1)}, u32[]{:S(2)}, u32[]{:S(2)}) collective-permute-start(bf16[208,128]{1,0:T(8,128)(2,1)S(1)} %get-tuple-element.23), channel_id=1, source_target_pairs={{0,4},{1,5},{2,6},{3,7},{4,0},{5,1},{6,2},{7,3},{8,12},{9,13},{10,... | collective-permute-start | bytes 159752 | tf_op jit(solution)/shard_map/ppermute | solution.py:610
  14.9 5.6 %collective-permute-start.4 = (bf16[208,128]{1,0:T(8,128)(2,1)S(1)}, bf16[208,128]{1,0:T(8,128)(2,1)S(1)}, u32[]{:S(2)}, u32[]{:S(2)}) collective-permute-start(bf16[208,128]{1,0:T(8,128)(2,1)S(1)} %get-tuple-element.22), channel_id=1, source_target_pairs={{0,2},{1,3},{2,0},{3,1},{4,6},{5,7},{6,4},{7,5},{8,10},{9,11},{10,... | collective-permute-start | bytes 159752 | tf_op jit(solution)/shard_map/ppermute | solution.py:610
  15.7 5.7 %collective-permute-start.5 = (bf16[208,128]{1,0:T(8,128)(2,1)S(1)}, bf16[208,128]{1,0:T(8,128)(2,1)S(1)}, u32[]{:S(2)}, u32[]{:S(2)}) collective-permute-start(bf16[208,128]{1,0:T(8,128)(2,1)S(1)} %get-tuple-element.21), channel_id=1, source_target_pairs={{0,7},{1,6},{2,5},{3,4},{4,3},{5,2},{6,1},{7,0},{8,15},{9,14},{10,... | collective-permute-start | bytes 159752 | tf_op jit(solution)/shard_map/ppermute | solution.py:610
  16.7 7.3 %collective-permute-start.6 = (bf16[208,128]{1,0:T(8,128)(2,1)S(1)}, bf16[208,128]{1,0:T(8,128)(2,1)S(1)}, u32[]{:S(2)}, u32[]{:S(2)}) collective-permute-start(bf16[208,128]{1,0:T(8,128)(2,1)S(1)} %get-tuple-element.20), channel_id=1, source_target_pairs={{0,5},{1,4},{2,7},{3,6},{4,1},{5,0},{6,3},{7,2},{8,13},{9,12},{10,... | collective-permute-start | bytes 159752 | tf_op jit(solution)/shard_map/ppermute | solution.py:610
  18.1 5.9 %collective-permute-start.7 = (bf16[208,128]{1,0:T(8,128)(2,1)S(1)}, bf16[208,128]{1,0:T(8,128)(2,1)S(1)}, u32[]{:S(2)}, u32[]{:S(2)}) collective-permute-start(bf16[208,128]{1,0:T(8,128)(2,1)S(1)} %get-tuple-element.19), channel_id=1, source_target_pairs={{0,3},{1,2},{2,1},{3,0},{4,7},{5,6},{6,5},{7,4},{8,11},{9,10},{10,... | collective-permute-start | bytes 159752 | tf_op jit(solution)/shard_map/ppermute | solution.py:610
  20.5 3.5 %collective-permute-start.8 = (bf16[208,128]{1,0:T(8,128)(2,1)S(1)}, bf16[208,128]{1,0:T(8,128)(2,1)S(1)}, u32[]{:S(2)}, u32[]{:S(2)}) collective-permute-start(bf16[208,128]{1,0:T(8,128)(2,1)S(1)} %get-tuple-element.18), channel_id=1, source_target_pairs={{0,1},{1,0},{2,3},{3,2},{4,5},{5,4},{6,7},{7,6},{8,9},{9,8},{10,11... | collective-permute-start | bytes 159752 | tf_op jit(solution)/shard_map/ppermute | solution.py:610
  27.2 25.5 %copy-start.2 = (bf16[256,768]{1,0:T(8,128)(2,1)S(1)}, bf16[256,768]{1,0:T(8,128)(2,1)}, u32[]{:S(2)}) copy-start(bf16[256,768]{1,0:T(8,128)(2,1)} %constant.13.clone.matrix) | copy-start | bytes 1179652
  27.2 25.5 %all-to-all-start = ((bf16[32,96,128]{2,1,0:T(8,128)(2,1)}), bf16[32,96,128]{2,1,0:T(8,128)(2,1)S(1)}, u32[]{:S(2)}, u32[]{:S(2)}) async-start(bf16[32,96,128]{2,1,0:T(8,128)(2,1)} %forward_y.1), calls=%async_computation | async-start | bytes 1572864 | tf_op jit(solution)/shard_map/all_to_all | solution.py:613
  52.7 27.7 %copy-start.1 = (bf16[768,256]{1,0:T(8,128)(2,1)S(1)}, bf16[768,256]{1,0:T(8,128)(2,1)}, u32[]{:S(2)}) copy-start(bf16[768,256]{1,0:T(8,128)(2,1)} %constant.14.clone.matrix) | copy-start | bytes 1179652

commit v4 on v3

--- a/solution.py
+++ b/solution.py
@@ -162,18 +162,47 @@
     return 16 * color + 8 * part
 
 
-def prepare_kernel(colors, chans, feat, weight, bias, tile, first_edge, second_edge, table, ring_table, bias_rows, edge, taps, bias_in, sems):
+def edges_kernel(feat, first_edge, second_edge, edge, sems):
     step = 16
     rows = feat.shape[1]
     copies = fetch(
         [
+            pltpu.make_async_copy(feat.at[:, pl.ds(0, step), :], edge.at[0], sems.at[0]),
+            pltpu.make_async_copy(feat.at[:, pl.ds(rows - step, step), :], edge.at[1], sems.at[1]),
+        ]
+    )
+    for copy in copies:
+        copy.wait()
+    top = edge[0].astype(F32)[:, 0, :]
+    bottom = edge[1].astype(F32)[:, step - 1, :]
+    even = lax.axis_index("row") % 2 == 0
+    first_edge[...] = jnp.where(even, bottom, top).astype(BF16)
+    second_edge[...] = jnp.where(even, top, bottom).astype(BF16)
+
+
+def edges(features):
+    chans, rows, cols = features.shape
+    vm = pl.BlockSpec(memory_space=pltpu.VMEM)
+    return pl.pallas_call(
+        edges_kernel,
+        out_shape=[pltpu.VMEM((chans, cols), BF16)] * 2,
+        in_specs=[pl.BlockSpec(memory_space=pltpu.HBM)],
+        out_specs=[vm] * 2,
+        scratch_shapes=[pltpu.VMEM((2, chans, 16, cols), BF16), pltpu.SemaphoreType.DMA((2,))],
+        compiler_params=pltpu.CompilerParams(vmem_limit_bytes=VMEM_LIMIT),
+        name="edges",
+    )(pltpu.with_memory_space_constraint(features, pltpu.HBM))
+
+
+def prepare_kernel(colors, chans, feat, weight, bias, tile, table, ring_table, bias_rows, taps, bias_in, sems):
+    step = 16
+    copies = fetch(
+        [
             pltpu.make_async_copy(weight, taps, sems.at[0]),
             pltpu.make_async_copy(bias, bias_in, sems.at[1]),
-            pltpu.make_async_copy(feat.at[:, pl.ds(0, step), :], edge.at[0], sems.at[2]),
-            pltpu.make_async_copy(feat.at[:, pl.ds(rows - step, step), :], edge.at[1], sems.at[3]),
         ]
         + [
-            pltpu.make_async_copy(feat.at[pl.ds(i * (chans // 8), chans // 8)], tile.at[pl.ds(i * (chans // 8), chans // 8)], sems.at[4 + i])
+            pltpu.make_async_copy(feat.at[pl.ds(i * (chans // 8), chans // 8)], tile.at[pl.ds(i * (chans // 8), chans // 8)], sems.at[2 + i])
             for i in range(8)
         ]
     )
@@ -208,14 +237,7 @@
     copies[1].wait()
     for o in range(colors):
         bias_rows[o : o + 1, :] = jnp.full((1, TILE), bias_in[o], F32)
-    copies[2].wait()
-    copies[3].wait()
-    top = edge[0].astype(F32)[:, 0, :]
-    bottom = edge[1].astype(F32)[:, step - 1, :]
-    even = lax.axis_index("row") % 2 == 0
-    first_edge[...] = jnp.where(even, bottom, top).astype(BF16)
-    second_edge[...] = jnp.where(even, top, bottom).astype(BF16)
-    for copy in copies[4:]:
+    for copy in copies[2:]:
         copy.wait()
 
 
@@ -229,19 +251,16 @@
         partial(prepare_kernel, colors, chans),
         out_shape=[
             pltpu.VMEM(features.shape, BF16),
-            pltpu.VMEM((chans, cols), BF16),
-            pltpu.VMEM((chans, cols), BF16),
             pltpu.VMEM((3 * colors * 24, chans * 16), BF16),
             pltpu.VMEM((2, 3 * colors * 8, chans), BF16),
             pltpu.VMEM((colors, TILE), F32),
         ],
         in_specs=[hbm] * 3,
-        out_specs=[vm] * 6,
+        out_specs=[vm] * 4,
         scratch_shapes=[
-            pltpu.VMEM((2, chans, 16, cols), BF16),
             pltpu.VMEM(weight.shape, BF16),
             pltpu.SMEM(bias.shape, F32),
-            pltpu.SemaphoreType.DMA((12,)),
+            pltpu.SemaphoreType.DMA((10,)),
         ],
         compiler_params=pltpu.CompilerParams(vmem_limit_bytes=VMEM_LIMIT),
         name="prepare",
@@ -346,13 +365,15 @@
 
 
 def forward_y_kernel(colors, band, parts, *refs):
-    peers = len(refs) - 6
-    matrix, tw_c, tw_s, out, coded, left = refs[peers:]
+    peers = len(refs) - 7
+    matrix, tw_c, tw_s, _, out, coded, left = refs[peers:]
     for i, k in enumerate(sending_order(peers)):
         coded[lax.axis_index("col") ^ k] = refs[i][...]
     step = 16
     lane = lax.broadcasted_iota(jnp.int32, (1, HALF), 1)
-    for o in range(colors):
+    width = TILE // parts
+
+    def spread(o):
         for r in range(0, band, step):
             edge = []
             for p in range(peers):
@@ -384,15 +405,27 @@
                     for j, value in enumerate((high, low, high)):
                         to = slice((2 * j + part) * HALF, (2 * j + part + 1) * HALF)
                         left[o, k, r : r + step, to] = value
-        width = TILE // parts
-        acc = dot(left[o].reshape(2 * peers * band, 3 * TILE), matrix[...])
+
+    def multiply(o):
+        return dot(left[o].reshape(2 * peers * band, 3 * TILE), matrix[...])
+
+    def store(o, acc):
         code = encode(acc)
         for k in range(2 * peers):
             for q in range(parts):
                 out[parts * k + q, o * band : (o + 1) * band, :] = code[k * band : (k + 1) * band, q * width : (q + 1) * width]
 
-
-def forward_y(blocks, colors, band, parts):
+    held = None
+    for o in range(colors):
+        spread(o)
+        acc = multiply(o)
+        if held is not None:
+            store(o - 1, held)
+        held = acc
+    store(colors - 1, held)
+
+
+def forward_y(blocks, colors, band, parts, table):
     peers = len(blocks)
     tw_c, tw_s = dft_np(2 * peers, HALF, peers * TILE)
     vm = pl.BlockSpec(memory_space=pltpu.VMEM)
@@ -401,7 +434,7 @@
     return pl.pallas_call(
         partial(forward_y_kernel, colors, band, parts),
         out_shape=pltpu.VMEM((2 * peers * parts, colors * band, TILE // parts), BF16),
-        in_specs=[vm] * (peers + 3),
+        in_specs=[vm] * (peers + 3) + [pl.BlockSpec(memory_space=pl.ANY)],
         out_specs=vm,
         scratch_shapes=[
             pltpu.VMEM((peers,) + blocks[0].shape, BF16),
@@ -409,39 +442,39 @@
         ],
         compiler_params=pltpu.CompilerParams(vmem_limit_bytes=VMEM_LIMIT),
         name="forward_y",
-    )(*(blocks[k] for k in sending_order(peers)), jnp.asarray(matrix), jnp.asarray(tw_c, F32), jnp.asarray(tw_s, F32))
+    )(*(blocks[k] for k in sending_order(peers)), jnp.asarray(matrix), jnp.asarray(tw_c, F32), jnp.asarray(tw_s, F32), table)
 
 
 def transfer_kernel(sizes, wave, travel, out):
     height, width, parts, inner, block = sizes
-    color, k = pl.program_id(0), pl.program_id(1)
     position = lax.axis_index("row") * lax.axis_size("col") + lax.axis_index("col")
     k0 = position // parts
     q = position % parts
-    shape = out.shape[3:]
-    m = lax.broadcasted_iota(jnp.int32, shape, 0)
+    colors, n = out.shape[0] - 1, out.shape[1]
+    shape = (HALF // 4, out.shape[4])
     lane = lax.broadcasted_iota(jnp.int32, shape, 1)
-    kx = 2 * k + lane // block + (height // HALF) * m
     ky = k0 + inner * (block * q + lane % block)
-
-    @pl.when(color < wave.shape[0])
-    def _():
-        sx = jnp.where(kx < height // 2, kx, kx - height).astype(F32) / height
-        sy = jnp.where(ky < width // 2, ky, ky - width).astype(F32) / width
-        f2 = sx * sx + sy * sy
-        a = wave[jnp.minimum(color, wave.shape[0] - 1)]
-        turns = travel[0] * f2 / (a + jnp.sqrt(a * a - f2))
-        turns = turns - jnp.round(turns)
-        c, s = sincos_half(2.0 * turns)
-        out[0, 0, 0] = c * (1.0 / height)
-        out[0, 0, 1] = s * (1.0 / height)
-
-    @pl.when(color == wave.shape[0])
-    def _():
-        turns = ((2 * k + lane // block) * m).astype(F32) * (1.0 / height)
-        c, s = sincos_half(2.0 * (turns - jnp.round(turns)))
-        out[0, 0, 0] = c
-        out[0, 0, 1] = s
+    sy = jnp.where(ky < width // 2, ky, ky - width).astype(F32) * (1.0 / width)
+    sy2 = sy * sy
+    for k in range(n):
+        for i in range(4):
+            rows = slice(i * HALF // 4, (i + 1) * HALF // 4)
+            m = lax.broadcasted_iota(jnp.int32, shape, 0) + i * HALF // 4
+            half = 2 * k + lane // block
+            kx = half + (height // HALF) * m
+            sx = jnp.where(kx < height // 2, kx, kx - height).astype(F32) * (1.0 / height)
+            f2 = sx * sx + sy2
+            for color in range(colors):
+                a = wave[color]
+                turns = travel[0] * f2 / (a + jnp.sqrt(a * a - f2))
+                turns = turns - jnp.round(turns)
+                c, s = sincos_half(turns, 5, 2.0)
+                out[color, k, 0, rows, :] = c * (1.0 / height)
+                out[color, k, 1, rows, :] = s * (1.0 / height)
+            turns = (half * m).astype(F32) * (1.0 / height)
+            c, s = sincos_half(turns - jnp.round(turns), 5, 2.0)
+            out[colors, k, 0, rows, :] = c
+            out[colors, k, 1, rows, :] = s
 
 
 def transfer(inv_wavelength, distance, sizes):
@@ -451,77 +484,88 @@
     n = height // TILE
     return pl.pallas_call(
         partial(transfer_kernel, sizes),
-        grid=(colors + 1, n),
-        out_shape=jax.ShapeDtypeStruct((colors + 1, n, 2, HALF, 2 * block), F32),
+        out_shape=pltpu.VMEM((colors + 1, n, 2, HALF, 2 * block), F32),
         in_specs=[sm] * 2,
-        out_specs=pl.BlockSpec((1, 1, 2, HALF, 2 * block), lambda c, k: (c, k, 0, 0, 0)),
+        out_specs=pl.BlockSpec(memory_space=pltpu.VMEM),
         compiler_params=pltpu.CompilerParams(vmem_limit_bytes=VMEM_LIMIT),
         name="transfer",
     )(inv_wavelength, distance)
 
 
-def middle_kernel(coded, tables, matrix, out, right):
-    colors = out.shape[1]
-    for color in range(colors):
-        middle_color(
-            coded.at[:, color], tables.at[color], matrix, tables.at[colors], out.at[:, color], right.at[color]
-        )
-
-
-def middle_color(coded, table, matrix, twiddles, out, right):
-    n = table.shape[0]
+def middle_kernel(coded, tables, matrix, out, before, after):
+    colors, n = out.shape[1], tables.shape[1]
     width = coded.shape[-1]
     block = width // 2
     per = coded.shape[0] // (2 * n)
-    band = coded.shape[1]
+    band = coded.shape[2]
+    twiddles = tables.at[colors]
     lane = lax.broadcasted_iota(jnp.int32, (1, width), 1)
     left = lane < block
     step = 16
     turn_c = [jnp.where(left, 1.0, math.cos(math.pi * a / n)) for a in range(n)]
     turn_s = [jnp.where(left, 0.0, math.sin(math.pi * a / n)) for a in range(n)]
 
-    def put(k, rows, z, order):
+    def put(right, k, rows, z, order):
         for part, x in zip(order, (z.re, z.im)):
             high, low = split(x)
             for j, value in enumerate((high, high, low)):
                 to = (2 * j + part) * HALF
                 right[to + rows.start : to + rows.stop, k * width : (k + 1) * width] = value
 
-    for i in range(HALF // step):
-        s, r = divmod(i * step, band)
-        rows = slice(i * step, (i + 1) * step)
-        items = []
-        for a in range(n):
-            x = decode(coded[per * a + s, r : r + step, :])
-            y = decode(coded[per * (a + n) + s, r : r + step, :])
-            u, v = x + y, x - y
-            z = Pair(jnp.where(left, u, lane_shift(v, block)), jnp.where(left, lane_shift(u, block), v))
-            if a:
-                z = z.times(turn_c[a], -turn_s[a])
-            items.append(z)
-        for k, z in enumerate(small_dft(items, -1)):
-            put(k, rows, z.times(twiddles[k, 0, rows, :], -twiddles[k, 1, rows, :]), (0, 1))
-    acc = dot(matrix[...], right[...])
-    for k in range(n):
-        cols = slice(k * width, (k + 1) * width)
-        z = Pair(acc[:HALF, cols], acc[HALF:, cols])
-        put(k, slice(0, HALF), z.times(table[k, 0], -table[k, 1]), (1, 0))
-    acc = dot(matrix[...], right[...])
-    for i in range(HALF // step):
-        s, r = divmod(i * step, band)
-        rows = slice(i * step, (i + 1) * step)
-        items = []
+    def spread(color):
+        for i in range(HALF // step):
+            s, r = divmod(i * step, band)
+            rows = slice(i * step, (i + 1) * step)
+            items = []
+            for a in range(n):
+                x = decode(coded[per * a + s, color, r : r + step, :])
+                y = decode(coded[per * (a + n) + s, color, r : r + step, :])
+                u, v = x + y, x - y
+                z = Pair(jnp.where(left, u, lane_shift(v, block)), jnp.where(left, lane_shift(u, block), v))
+                if a:
+                    z = z.times(turn_c[a], -turn_s[a])
+                items.append(z)
+            for k, z in enumerate(small_dft(items, -1)):
+                put(before.at[color], k, rows, z.times(twiddles[k, 0, rows, :], -twiddles[k, 1, rows, :]), (0, 1))
+
+    def multiply(right, color):
+        return dot(matrix[...], right[color])
+
+    def filtered(color, acc):
         for k in range(n):
             cols = slice(k * width, (k + 1) * width)
-            z = Pair(acc[HALF + rows.start : HALF + rows.stop, cols], acc[rows, cols])
-            items.append(z.times(twiddles[k, 0, rows, :], twiddles[k, 1, rows, :]))
-        for a, z in enumerate(small_dft(items, 1)):
-            if a:
-                z = z.times(turn_c[a], turn_s[a])
-            u = jnp.where(left, z.re, lane_shift(z.im, block))
-            v = jnp.where(left, lane_shift(z.re, block), z.im)
-            out[per * a + s, r : r + step, :] = encode(u + v)
-            out[per * (a + n) + s, r : r + step, :] = encode(u - v)
+            for i in range(HALF // step):
+                rows = slice(i * step, (i + 1) * step)
+                z = Pair(acc[rows, cols], acc[HALF + rows.start : HALF + rows.stop, cols])
+                put(after.at[color], k, rows, z.times(tables[color, k, 0, rows, :], -tables[color, k, 1, rows, :]), (1, 0))
+
+    def store(color, acc):
+        for i in range(HALF // step):
+            s, r = divmod(i * step, band)
+            rows = slice(i * step, (i + 1) * step)
+            items = []
+            for k in range(n):
+                cols = slice(k * width, (k + 1) * width)
+                z = Pair(acc[HALF + rows.start : HALF + rows.stop, cols], acc[rows, cols])
+                items.append(z.times(twiddles[k, 0, rows, :], twiddles[k, 1, rows, :]))
+            for a, z in enumerate(small_dft(items, 1)):
+                if a:
+                    z = z.times(turn_c[a], turn_s[a])
+                u = jnp.where(left, z.re, lane_shift(z.im, block))
+                v = jnp.where(left, lane_shift(z.re, block), z.im)
+                out[per * a + s, color, r : r + step, :] = encode(u + v)
+                out[per * (a + n) + s, color, r : r + step, :] = encode(u - v)
+
+    ahead, back = {}, {}
+    for tick in range(colors + 2):
+        if tick < colors:
+            spread(tick)
+            ahead[tick] = multiply(before, tick)
+        if 0 <= tick - 1 < colors:
+            filtered(tick - 1, ahead.pop(tick - 1))
+            back[tick - 1] = multiply(after, tick - 1)
+        if tick >= 2:
+            store(tick - 2, back.pop(tick - 2))
 
 
 def middle(coded, table):
@@ -534,7 +578,7 @@
         out_shape=jax.ShapeDtypeStruct(coded.shape, BF16),
         in_specs=[vm] * 3,
         out_specs=vm,
-        scratch_shapes=[pltpu.VMEM((colors, 3 * TILE, n * width), BF16)],
+        scratch_shapes=[pltpu.VMEM((colors, 3 * TILE, n * width), BF16)] * 2,
         compiler_params=pltpu.CompilerParams(vmem_limit_bytes=VMEM_LIMIT),
         name="middle_x",
     )(*(pltpu.with_memory_space_constraint(x, pltpu.VMEM) for x in (coded, table, jnp.asarray(forward))))
@@ -546,13 +590,18 @@
     outs = []
     step = 16
     scale = 1.0 / (inner * HALF)
-    for o in range(colors):
+
+    def spread(o):
         for k in range(inner):
             for q in range(parts):
                 high, low = split(decode(coded[parts * k + q, o]))
                 for j, value in enumerate((high, low, high)):
                     left[o, k, :, j * TILE + q * width : j * TILE + (q + 1) * width] = value
-        acc = dot(left[o].reshape(inner * band, 3 * TILE), matrix[...])
+
+    def multiply(o):
+        return dot(left[o].reshape(inner * band, 3 * TILE), matrix[...])
+
+    def store(o, acc):
         for r in range(0, band, step):
             items = []
             for k in range(inner):
@@ -561,7 +610,16 @@
             for a, z in enumerate(small_dft(items, 1)):
                 out[o, 0, r : r + step, a * HALF : (a + 1) * HALF] = z.re.astype(BF16)
                 out[o, 1, r : r + step, a * HALF : (a + 1) * HALF] = z.im.astype(BF16)
-        outs += fetch([pltpu.make_async_copy(out.at[o], target.at[o], sems.at[o])])
+        outs.extend(fetch([pltpu.make_async_copy(out.at[o], target.at[o], sems.at[o])]))
+
+    held = None
+    for o in range(colors):
+        spread(o)
+        acc = multiply(o)
+        if held is not None:
+            store(o - 1, held)
+        held = acc
+    store(colors - 1, held)
     for copy in outs:
         copy.wait()
 
@@ -599,7 +657,8 @@
     width = tile_cols * mesh_cols
     block = width // groups
     parts = mesh_rows // 2
-    tile, edge_one, edge_two, *prepared = prepare(features, conv_weight, bias)
+    edge_one, edge_two = edges(features)
+    tile, *prepared = prepare(features, conv_weight, bias)
     halos = []
     for start, edge in ((1, edge_two), (0, edge_one)):
         pairs = [(i, i + 1) for i in range(start, mesh_rows - 1, 2)]
@@ -608,8 +667,8 @@
     blocks = [bands[0]] * mesh_cols
     for k in range(mesh_cols - 1, 0, -1):
         blocks[k] = lax.ppermute(bands[k], "col", [(i, i ^ k) for i in range(mesh_cols)])
-    spectrum = forward_y(blocks, colors, band, parts)
     table = transfer(inv_wavelength, distance, (height, width, parts, 2 * mesh_cols, block))
+    spectrum = forward_y(blocks, colors, band, parts, table)
     spectrum = lax.all_to_all(spectrum, ("row", "col"), split_axis=0, concat_axis=0, tiled=True)
     back = middle(spectrum.reshape(groups, colors, band, 2 * block), table)
     back = lax.all_to_all(back, ("row", "col"), split_axis=0, concat_axis=0, tiled=True)

time: 83.1 us -> 80.8 us (0.972)
  blocking collectives: 24 us -> 49.4 us
  waiting for transfers between devices: 24.6 us -> 2.12 us
  starting transfers between devices: 18.4 us -> 14.7 us
  Pallas kernels: 15 us -> 13.4 us
    all_to_all x0 -> x1, blocking collectives: none -> 25.4 us  [per_device(): lax.all_to_all(spectrum, ('row', 'col'), split_axis=0, concat_axis=0, til...]
    all_to_all x1 -> x0, waiting for transfers between devices: 18.5 us -> none  [per_device(): lax.all_to_all(spectrum, ('row', 'col'), split_axis=0, concat_axis=0, til...]
    all_to_all x1 -> x0, starting transfers between devices: 3.53 us -> none  [per_device(): lax.all_to_all(spectrum, ('row', 'col'), split_axis=0, concat_axis=0, til...]
    ppermute x7, waiting for transfers between devices: 4.45 us -> 2.11 us  [per_device(): lax.ppermute(bands[k], 'col', [(i, i ^ k) for i in range(mesh_cols)])]
    ppermute x2, waiting for transfers between devices: 1.63 us -> 0.01 us  [per_device(): halos.append(lax.ppermute(edge, 'row', pairs + [(j, i) for i, j in pairs]))]
    pallas_call x1, Pallas kernels: 3.13 us -> 2.25 us  [forward_y(): pl.pallas_call(partial(forward_y_kernel, colors, band, parts), out_shape=...]
    pallas_call x1 -> x2, Pallas kernels: 2.76 us -> 2.88 us  [the longest x1 1.83 us: transfer(): pl.pallas_call(partial(transfer_kernel, sizes), out_shape=pltpu.VMEM((col...]
  transfers between devices with their start and end apart: 10 -> 9, of which waited for: 5 -> 2; matrix products, arithmetic and copies ran while one was open for 0% -> 0% of each run, Pallas kernels for 3% -> 4%
where the time goes in v4:
time: 80.8 us; the launch traced here: 80.6 us
  blocking collectives  49.4 us (61%)
  starting transfers between devices  14.7 us (18%)
  Pallas kernels  13.4 us (17%)
  waiting for transfers between devices  2.12 us (3%)
  between operations  0.82 us (1%)
    all_to_all x1, blocking collectives, per_device(): lax.all_to_all(spectrum, ('row', 'col'), split_axis=0, concat_axis=0, til...  25.4 us
    all_to_all x1, blocking collectives, per_device(): lax.all_to_all(back, ('row', 'col'), split_axis=0, concat_axis=0, tiled=T...  24 us
    ppermute x7, starting transfers between devices, per_device(): lax.ppermute(bands[k], 'col', [(i, i ^ k) for i in range(mesh_cols)])  8.34 us
    ppermute x2, starting transfers between devices, per_device(): halos.append(lax.ppermute(edge, 'row', pairs + [(j, i) for i, j in pairs]))  6.4 us
    pallas_call x1, Pallas kernels, middle(): pl.pallas_call(middle_kernel, out_shape=jax.ShapeDtypeStruct(coded.shape,...  3.11 us
    pallas_call x1, Pallas kernels, inverse_y(): pl.pallas_call(partial(inverse_y_kernel, parts), out_shape=jax.ShapeDtype...  2.4 us
    pallas_call x1, Pallas kernels, forward_y(): pl.pallas_call(partial(forward_y_kernel, colors, band, parts), out_shape=...  2.25 us
    ppermute x7, waiting for transfers between devices, per_device(): lax.ppermute(bands[k], 'col', [(i, i ^ k) for i in range(mesh_cols)])  2.11 us
  transfers between devices with their start and end apart: 9, of which 2 were waited for; matrix products, arithmetic and copies ran while one was open for 0% of the time, Pallas kernels for 4%

profile of v4, /device:TPU:0, one launch (start us, length us, event | category | flops | bytes accessed | tf_op | source)
XLA Modules:
  0.0 80.6 jit_solution(1047420331023927509)
XLA Ops:
  0.0 1.0 %edges.1 = (bf16[16,256]{1,0:T(8,128)(2,1)S(1)}, bf16[16,256]{1,0:T(8,128)(2,1)S(1)}) custom-call(bf16[16,256,256]{2,1,0:T(8,128)(2,1)} %feat.3), custom_call_target="tpu_custom_call" | custom-call | tf_op jit(solution)/shard_map/edges/pallas_call | solution.py:186
  1.1 0.7 collective-permute-start
  1.7 5.7 %collective-permute-start.1 = (bf16[16,256]{1,0:T(8,128)(2,1)S(1)}, bf16[16,256]{1,0:T(8,128)(2,1)S(1)}, u32[]{:S(2)}, u32[]{:S(2)}) collective-permute-start(bf16[16,256]{1,0:T(8,128)(2,1)S(1)} %get-tuple-element.12), channel_id=1, source_target_pairs={{0,8},{16,24},{8,0},{24,16},{1,9},{17,25},{9,1},{25,17},{2,10},{18... | collective-permute-start | bytes 24584 | tf_op jit(solution)/shard_map/ppermute | solution.py:665
  7.5 1.6 %prepare.1 = (bf16[16,256,256]{2,1,0:T(8,128)(2,1)S(1)}, bf16[216,256]{1,0:T(8,128)(2,1)S(1)}, bf16[2,72,16]{2,1,0:T(8,128)(2,1)S(1)}, f32[3,256]{1,0:T(4,128)S(1)}) custom-call(bf16[16,256,256]{2,1,0:T(8,128)(2,1)} %feat.3, bf16[3,3,3,16]{3,2,1,0:T(4,128)(2,1)} %bitcast.19, f32[3]{0:T(128)} %bias.1), custom_call_target="tpu_custom_call" | custom-call | tf_op jit(solution)/shard_map/prepare/pallas_call | solution.py:250
  9.1 0.0 copy-start.5
  9.1 0.0 collective-permute-done.second_halo
  9.1 0.0 collective-permute-done.1.first_halo
  9.1 1.2 %conv_head.1 = bf16[8,208,128]{2,1,0:T(8,128)(2,1)S(1)} custom-call(bf16[16,256]{1,0:T(8,128)(2,1)S(1)} %collective-permute-done.second_halo, bf16[16,256]{1,0:T(8,128)(2,1)S(1)} %collective-permute-done.1.first_halo, bf16[16,256,256]{2,1,0:T(8,128)(2,1)S(1)} %get-tuple-element.13.feat, bf16[216,256]{1,0:T(8,128)(2,1)S(1)} %get-tuple-element.14.table, ...), custom_call_target="tpu_custom_call" | custom-call | tf_op jit(solution)/shard_map/conv_head/pallas_call | solution.py:353
  10.3 0.0 copy-start
  10.3 0.0 copy-start.3
  10.3 0.0 copy-start.4
  10.4 3.7 %collective-permute-start.2 = (bf16[208,128]{1,0:T(8,128)(2,1)S(1)}, bf16[208,128]{1,0:T(8,128)(2,1)S(1)}, u32[]{:S(2)}, u32[]{:S(2)}) collective-permute-start(bf16[208,128]{1,0:T(8,128)(2,1)S(1)} %get-tuple-element.24), channel_id=1, source_target_pairs={{0,6},{1,7},{2,4},{3,5},{4,2},{5,3},{6,0},{7,1},{8,14},{9,15},{10,... | collective-permute-start | bytes 159752 | tf_op jit(solution)/shard_map/ppermute | solution.py:669
  14.0 0.0 collective-permute-start.3
  14.0 0.8 collective-permute-start.4
  14.8 1.6 %collective-permute-start.5 = (bf16[208,128]{1,0:T(8,128)(2,1)S(1)}, bf16[208,128]{1,0:T(8,128)(2,1)S(1)}, u32[]{:S(2)}, u32[]{:S(2)}) collective-permute-start(bf16[208,128]{1,0:T(8,128)(2,1)S(1)} %get-tuple-element.21), channel_id=1, source_target_pairs={{0,7},{1,6},{2,5},{3,4},{4,3},{5,2},{6,1},{7,0},{8,15},{9,14},{10,... | collective-permute-start | bytes 159752 | tf_op jit(solution)/shard_map/ppermute | solution.py:669
  16.5 0.8 collective-permute-start.6
  17.2 0.0 collective-permute-done.2.refs_0_
  17.2 1.5 %collective-permute-start.7 = (bf16[208,128]{1,0:T(8,128)(2,1)S(1)}, bf16[208,128]{1,0:T(8,128)(2,1)S(1)}, u32[]{:S(2)}, u32[]{:S(2)}) collective-permute-start(bf16[208,128]{1,0:T(8,128)(2,1)S(1)} %get-tuple-element.19), channel_id=1, source_target_pairs={{0,3},{1,2},{2,1},{3,0},{4,7},{5,6},{6,5},{7,4},{8,11},{9,10},{10,... | collective-permute-start | bytes 159752 | tf_op jit(solution)/shard_map/ppermute | solution.py:669
  18.7 0.9 %collective-permute-done.3.refs_1_ = bf16[208,128]{1,0:T(8,128)(2,1)S(1)} collective-permute-done((bf16[208,128]{1,0:T(8,128)(2,1)S(1)}, bf16[208,128]{1,0:T(8,128)(2,1)S(1)}, u32[]{:S(2)}, u32[]{:S(2)}) %collective-permute-start.3) | collective-permute-done | bytes 53280 | tf_op jit(solution)/shard_map/ppermute | solution.py:669
  19.6 0.0 collective-permute-start.8
  20.3 0.0 copy-done.5
  20.3 1.8 %transfer.1.refs_11_.tables = f32[4,4,2,128,128]{4,3,2,1,0:T(8,128)S(1)} custom-call(f32[3]{0:T(128)S(1)} %copy-done.5, f32[1]{0:T(128)S(6)} %copy.13.travel), custom_call_target="tpu_custom_call" | custom-call | tf_op jit(solution)/shard_map/transfer/pallas_call | solution.py:485
  22.1 0.0 collective-permute-done.4.refs_2_
  22.1 0.0 collective-permute-done.5.refs_3_
  22.2 1.2 %collective-permute-done.6.refs_4_ = bf16[208,128]{1,0:T(8,128)(2,1)S(1)} collective-permute-done((bf16[208,128]{1,0:T(8,128)(2,1)S(1)}, bf16[208,128]{1,0:T(8,128)(2,1)S(1)}, u32[]{:S(2)}, u32[]{:S(2)}) %collective-permute-start.6) | collective-permute-done | bytes 53280 | tf_op jit(solution)/shard_map/ppermute | solution.py:669
  23.3 0.0 collective-permute-done.7.refs_5_
  23.3 0.0 collective-permute-done.8.refs_6_
  23.3 0.0 copy-done
  23.3 0.0 copy-done.3
  23.4 0.0 copy-done.4
  23.4 0.0 copy-start.2
  23.4 2.3 %forward_y.1 = bf16[32,96,128]{2,1,0:T(8,128)(2,1)S(1)} custom-call(bf16[208,128]{1,0:T(8,128)(2,1)S(1)} %collective-permute-done.2.refs_0_, bf16[208,128]{1,0:T(8,128)(2,1)S(1)} %collective-permute-done.3.refs_1_, bf16[208,128]{1,0:T(8,128)(2,1)S(1)} %collective-permute-done.4.refs_2_, bf16[208,128]{1,0:T(8,128)(2,1)S(1)} %collective-permute-done.5.refs_3_, ...), custom_call_target="tpu_custom_call" | custom-call | tf_op jit(solution)/shard_map/forward_y/pallas_call | solution.py:434
  25.6 25.4 %all_to_all.10 = bf16[32,96,128]{2,1,0:T(8,128)(2,1)S(1)} all-to-all(bf16[32,96,128]{2,1,0:T(8,128)(2,1)S(1)} %forward_y.1), channel_id=1, replica_groups=mesh['row'=4,'col'=8] {'row','col'}, dimensions={0} | all-to-all | bytes 1572864 | tf_op jit(solution)/shard_map/all_to_all | solution.py:672
  51.1 0.0 copy-done.2
  51.1 0.0 copy-start.1
  51.1 3.1 %middle_x.1 = bf16[32,3,32,128]{3,2,1,0:T(8,128)(2,1)S(1)} custom-call(bf16[32,3,32,128]{3,2,1,0:T(8,128)(2,1)S(1)} %bitcast.18, f32[4,4,2,128,128]{4,3,2,1,0:T(8,128)S(1)} %transfer.1.refs_11_.tables, bf16[256,768]{1,0:T(8,128)(2,1)S(1)} %copy-done.2), custom_call_target="tpu_custom_call" | custom-call | tf_op jit(solution)/shard_map/middle_x/pallas_call | solution.py:576
  54.2 24.0 %all_to_all.11.coded = bf16[32,3,32,128]{3,2,1,0:T(8,128)(2,1)S(1)} all-to-all(bf16[32,3,32,128]{3,2,1,0:T(8,128)(2,1)S(1)} %middle_x.1), channel_id=1, replica_groups=mesh['row'=4,'col'=8] {'row','col'}, dimensions={0} | all-to-all | bytes 1572864 | tf_op jit(solution)/shard_map/all_to_all | solution.py:674
  78.2 0.0 copy-done.1
  78.2 2.4 %inverse_y.1 = bf16[3,2,32,2048]{3,2,1,0:T(8,128)(2,1)} custom-call(bf16[32,3,32,128]{3,2,1,0:T(8,128)(2,1)S(1)} %all_to_all.11.coded, bf16[768,256]{1,0:T(8,128)(2,1)S(1)} %copy-done.1, f32[16,128]{1,0:T(8,128)S(1)} %copy-done.3, f32[16,128]{1,0:T(8,128)S(1)} %copy-done.4), custom_call_target="tpu_custom_call" | custom-call | tf_op jit(solution)/shard_map/inverse_y/pallas_call | solution.py:634
  (1 shorter events, 0.0 us)
Async XLA Ops:
  1.1 8.0 %collective-permute-start = (bf16[16,256]{1,0:T(8,128)(2,1)S(1)}, bf16[16,256]{1,0:T(8,128)(2,1)S(1)}, u32[]{:S(2)}, u32[]{:S(2)}) collective-permute-start(bf16[16,256]{1,0:T(8,128)(2,1)S(1)} %get-tuple-element.11), channel_id=1, source_target_pairs={{8,16},{16,8},{9,17},{17,9},{10,18},{18,10},{11,19},{19,11},{12,20... | collective-permute-start | bytes 24584 | tf_op jit(solution)/shard_map/ppermute | solution.py:665
  1.7 7.4 %collective-permute-start.1 = (bf16[16,256]{1,0:T(8,128)(2,1)S(1)}, bf16[16,256]{1,0:T(8,128)(2,1)S(1)}, u32[]{:S(2)}, u32[]{:S(2)}) collective-permute-start(bf16[16,256]{1,0:T(8,128)(2,1)S(1)} %get-tuple-element.12), channel_id=1, source_target_pairs={{0,8},{16,24},{8,0},{24,16},{1,9},{17,25},{9,1},{25,17},{2,10},{18... | collective-permute-start | bytes 24584 | tf_op jit(solution)/shard_map/ppermute | solution.py:665
  9.1 11.2 %copy-start.5 = (f32[3]{0:T(128)S(1)}, f32[3]{0:T(128)}, u32[]{:S(2)}) copy-start(f32[3]{0:T(128)} %wave.1) | copy-start | bytes 40
  10.3 13.1 %copy-start = (bf16[768,256]{1,0:T(8,128)(2,1)S(1)}, bf16[768,256]{1,0:T(8,128)(2,1)}, u32[]{:S(2)}) copy-start(bf16[768,256]{1,0:T(8,128)(2,1)} %constant.10.clone.refs_8_) | copy-start | bytes 1179652
  10.3 13.1 %copy-start.3 = (f32[16,128]{1,0:T(8,128)S(1)}, f32[16,128]{1,0:T(8,128)}, u32[]{:S(2)}) copy-start(f32[16,128]{1,0:T(8,128)} %constant.11.clone.refs_9_.tw_c) | copy-start | bytes 24580
  10.3 13.0 %copy-start.4 = (f32[16,128]{1,0:T(8,128)S(1)}, f32[16,128]{1,0:T(8,128)}, u32[]{:S(2)}) copy-start(f32[16,128]{1,0:T(8,128)} %constant.12.clone.refs_10_.tw_s) | copy-start | bytes 24580
  10.4 6.9 %collective-permute-start.2 = (bf16[208,128]{1,0:T(8,128)(2,1)S(1)}, bf16[208,128]{1,0:T(8,128)(2,1)S(1)}, u32[]{:S(2)}, u32[]{:S(2)}) collective-permute-start(bf16[208,128]{1,0:T(8,128)(2,1)S(1)} %get-tuple-element.24), channel_id=1, source_target_pairs={{0,6},{1,7},{2,4},{3,5},{4,2},{5,3},{6,0},{7,1},{8,14},{9,15},{10,... | collective-permute-start | bytes 159752 | tf_op jit(solution)/shard_map/ppermute | solution.py:669
  14.0 5.6 %collective-permute-start.3 = (bf16[208,128]{1,0:T(8,128)(2,1)S(1)}, bf16[208,128]{1,0:T(8,128)(2,1)S(1)}, u32[]{:S(2)}, u32[]{:S(2)}) collective-permute-start(bf16[208,128]{1,0:T(8,128)(2,1)S(1)} %get-tuple-element.23), channel_id=1, source_target_pairs={{0,4},{1,5},{2,6},{3,7},{4,0},{5,1},{6,2},{7,3},{8,12},{9,13},{10,... | collective-permute-start | bytes 159752 | tf_op jit(solution)/shard_map/ppermute | solution.py:669
  14.0 8.1 %collective-permute-start.4 = (bf16[208,128]{1,0:T(8,128)(2,1)S(1)}, bf16[208,128]{1,0:T(8,128)(2,1)S(1)}, u32[]{:S(2)}, u32[]{:S(2)}) collective-permute-start(bf16[208,128]{1,0:T(8,128)(2,1)S(1)} %get-tuple-element.22), channel_id=1, source_target_pairs={{0,2},{1,3},{2,0},{3,1},{4,6},{5,7},{6,4},{7,5},{8,10},{9,11},{10,... | collective-permute-start | bytes 159752 | tf_op jit(solution)/shard_map/ppermute | solution.py:669
  14.8 7.3 %collective-permute-start.5 = (bf16[208,128]{1,0:T(8,128)(2,1)S(1)}, bf16[208,128]{1,0:T(8,128)(2,1)S(1)}, u32[]{:S(2)}, u32[]{:S(2)}) collective-permute-start(bf16[208,128]{1,0:T(8,128)(2,1)S(1)} %get-tuple-element.21), channel_id=1, source_target_pairs={{0,7},{1,6},{2,5},{3,4},{4,3},{5,2},{6,1},{7,0},{8,15},{9,14},{10,... | collective-permute-start | bytes 159752 | tf_op jit(solution)/shard_map/ppermute | solution.py:669
  16.5 6.9 %collective-permute-start.6 = (bf16[208,128]{1,0:T(8,128)(2,1)S(1)}, bf16[208,128]{1,0:T(8,128)(2,1)S(1)}, u32[]{:S(2)}, u32[]{:S(2)}) collective-permute-start(bf16[208,128]{1,0:T(8,128)(2,1)S(1)} %get-tuple-element.20), channel_id=1, source_target_pairs={{0,5},{1,4},{2,7},{3,6},{4,1},{5,0},{6,3},{7,2},{8,13},{9,12},{10,... | collective-permute-start | bytes 159752 | tf_op jit(solution)/shard_map/ppermute | solution.py:669
  17.2 6.1 %collective-permute-start.7 = (bf16[208,128]{1,0:T(8,128)(2,1)S(1)}, bf16[208,128]{1,0:T(8,128)(2,1)S(1)}, u32[]{:S(2)}, u32[]{:S(2)}) collective-permute-start(bf16[208,128]{1,0:T(8,128)(2,1)S(1)} %get-tuple-element.19), channel_id=1, source_target_pairs={{0,3},{1,2},{2,1},{3,0},{4,7},{5,6},{6,5},{7,4},{8,11},{9,10},{10,... | collective-permute-start | bytes 159752 | tf_op jit(solution)/shard_map/ppermute | solution.py:669
  19.6 3.7 %collective-permute-start.8 = (bf16[208,128]{1,0:T(8,128)(2,1)S(1)}, bf16[208,128]{1,0:T(8,128)(2,1)S(1)}, u32[]{:S(2)}, u32[]{:S(2)}) collective-permute-start(bf16[208,128]{1,0:T(8,128)(2,1)S(1)} %get-tuple-element.18), channel_id=1, source_target_pairs={{0,1},{1,0},{2,3},{3,2},{4,5},{5,4},{6,7},{7,6},{8,9},{9,8},{10,11... | collective-permute-start | bytes 159752 | tf_op jit(solution)/shard_map/ppermute | solution.py:669
  23.4 27.7 %copy-start.2 = (bf16[256,768]{1,0:T(8,128)(2,1)S(1)}, bf16[256,768]{1,0:T(8,128)(2,1)}, u32[]{:S(2)}) copy-start(bf16[256,768]{1,0:T(8,128)(2,1)} %constant.13.clone.matrix) | copy-start | bytes 1179652
  51.1 27.1 %copy-start.1 = (bf16[768,256]{1,0:T(8,128)(2,1)S(1)}, bf16[768,256]{1,0:T(8,128)(2,1)}, u32[]{:S(2)}) copy-start(bf16[768,256]{1,0:T(8,128)(2,1)} %constant.14.clone.matrix) | copy-start | bytes 1179652

commit v5 on v4

--- a/solution.py
+++ b/solution.py
@@ -15,6 +15,7 @@
 HALF = 128
 CODE = 124.0
 TINY = 1.2e-38
+SHRINK = 2.0**-4
 VMEM_LIMIT = 10 * 1024 * 1024
 
 
@@ -77,12 +78,13 @@
 
 def encode(v):
     v2 = v * v
-    return (v2 * v2 * v).astype(BF16)
+    v4 = v2 * v2
+    return (v4 * v4 * v).astype(BF16)
 
 
 def decode(w):
     w = w.astype(F32)
-    return w * jnp.exp2(lax.log(jnp.maximum(jnp.abs(w), TINY)) * (-0.8 / math.log(2.0)))
+    return w * jnp.exp2(lax.log(jnp.maximum(jnp.abs(w), TINY)) * (-8.0 / 9.0 / math.log(2.0)))
 
 
 def fetch(copies):
@@ -469,8 +471,8 @@
                 turns = travel[0] * f2 / (a + jnp.sqrt(a * a - f2))
                 turns = turns - jnp.round(turns)
                 c, s = sincos_half(turns, 5, 2.0)
-                out[color, k, 0, rows, :] = c * (1.0 / height)
-                out[color, k, 1, rows, :] = s * (1.0 / height)
+                out[color, k, 0, rows, :] = c * (SHRINK / height)
+                out[color, k, 1, rows, :] = s * (SHRINK / height)
             turns = (half * m).astype(F32) * (1.0 / height)
             c, s = sincos_half(turns - jnp.round(turns), 5, 2.0)
             out[colors, k, 0, rows, :] = c
@@ -589,7 +591,7 @@
     colors, band, width = coded.shape[1], coded.shape[2], coded.shape[3]
     outs = []
     step = 16
-    scale = 1.0 / (inner * HALF)
+    scale = 1.0 / (SHRINK * inner * HALF)
 
     def spread(o):
         for k in range(inner):

time: 80.8 us -> 80.9 us (level)
  no operation moved by 1% of the time
where the time goes in v5:
time: 80.9 us; the launch traced here: 80.6 us
  blocking collectives  49.4 us (61%)
  starting transfers between devices  14.7 us (18%)
  Pallas kernels  13.4 us (17%)
  waiting for transfers between devices  2.12 us (3%)
  between operations  0.82 us (1%)
    all_to_all x1, blocking collectives, per_device(): lax.all_to_all(spectrum, ('row', 'col'), split_axis=0, concat_axis=0, til...  25.4 us
    all_to_all x1, blocking collectives, per_device(): lax.all_to_all(back, ('row', 'col'), split_axis=0, concat_axis=0, tiled=T...  24 us
    ppermute x7, starting transfers between devices, per_device(): lax.ppermute(bands[k], 'col', [(i, i ^ k) for i in range(mesh_cols)])  8.34 us
    ppermute x2, starting transfers between devices, per_device(): halos.append(lax.ppermute(edge, 'row', pairs + [(j, i) for i, j in pairs]))  6.4 us
    pallas_call x1, Pallas kernels, middle(): pl.pallas_call(middle_kernel, out_shape=jax.ShapeDtypeStruct(coded.shape,...  3.12 us
    pallas_call x1, Pallas kernels, inverse_y(): pl.pallas_call(partial(inverse_y_kernel, parts), out_shape=jax.ShapeDtype...  2.4 us
    pallas_call x1, Pallas kernels, forward_y(): pl.pallas_call(partial(forward_y_kernel, colors, band, parts), out_shape=...  2.26 us
    ppermute x7, waiting for transfers between devices, per_device(): lax.ppermute(bands[k], 'col', [(i, i ^ k) for i in range(mesh_cols)])  2.11 us
  transfers between devices with their start and end apart: 9, of which 2 were waited for; matrix products, arithmetic and copies ran while one was open for 0% of the time, Pallas kernels for 4%

profile of v5, /device:TPU:0, one launch (start us, length us, event | category | flops | bytes accessed | tf_op | source)
XLA Modules:
  0.0 80.6 jit_solution(2873174194002307486)
XLA Ops:
  0.0 1.0 %edges.1 = (bf16[16,256]{1,0:T(8,128)(2,1)S(1)}, bf16[16,256]{1,0:T(8,128)(2,1)S(1)}) custom-call(bf16[16,256,256]{2,1,0:T(8,128)(2,1)} %feat.3), custom_call_target="tpu_custom_call" | custom-call | tf_op jit(solution)/shard_map/edges/pallas_call | solution.py:188
  1.1 0.7 collective-permute-start
  1.7 5.7 %collective-permute-start.1 = (bf16[16,256]{1,0:T(8,128)(2,1)S(1)}, bf16[16,256]{1,0:T(8,128)(2,1)S(1)}, u32[]{:S(2)}, u32[]{:S(2)}) collective-permute-start(bf16[16,256]{1,0:T(8,128)(2,1)S(1)} %get-tuple-element.12), channel_id=1, source_target_pairs={{0,8},{16,24},{8,0},{24,16},{1,9},{17,25},{9,1},{25,17},{2,10},{18... | collective-permute-start | bytes 24584 | tf_op jit(solution)/shard_map/ppermute | solution.py:667
  7.5 1.6 %prepare.1 = (bf16[16,256,256]{2,1,0:T(8,128)(2,1)S(1)}, bf16[216,256]{1,0:T(8,128)(2,1)S(1)}, bf16[2,72,16]{2,1,0:T(8,128)(2,1)S(1)}, f32[3,256]{1,0:T(4,128)S(1)}) custom-call(bf16[16,256,256]{2,1,0:T(8,128)(2,1)} %feat.3, bf16[3,3,3,16]{3,2,1,0:T(4,128)(2,1)} %bitcast.19, f32[3]{0:T(128)} %bias.1), custom_call_target="tpu_custom_call" | custom-call | tf_op jit(solution)/shard_map/prepare/pallas_call | solution.py:252
  9.1 0.0 copy-start.5
  9.1 0.0 collective-permute-done.second_halo
  9.1 0.0 collective-permute-done.1.first_halo
  9.1 1.2 %conv_head.1 = bf16[8,208,128]{2,1,0:T(8,128)(2,1)S(1)} custom-call(bf16[16,256]{1,0:T(8,128)(2,1)S(1)} %collective-permute-done.second_halo, bf16[16,256]{1,0:T(8,128)(2,1)S(1)} %collective-permute-done.1.first_halo, bf16[16,256,256]{2,1,0:T(8,128)(2,1)S(1)} %get-tuple-element.13.feat, bf16[216,256]{1,0:T(8,128)(2,1)S(1)} %get-tuple-element.14.table, ...), custom_call_target="tpu_custom_call" | custom-call | tf_op jit(solution)/shard_map/conv_head/pallas_call | solution.py:355
  10.3 0.0 copy-start
  10.3 0.0 copy-start.3
  10.3 0.0 copy-start.4
  10.4 3.7 %collective-permute-start.2 = (bf16[208,128]{1,0:T(8,128)(2,1)S(1)}, bf16[208,128]{1,0:T(8,128)(2,1)S(1)}, u32[]{:S(2)}, u32[]{:S(2)}) collective-permute-start(bf16[208,128]{1,0:T(8,128)(2,1)S(1)} %get-tuple-element.24), channel_id=1, source_target_pairs={{0,6},{1,7},{2,4},{3,5},{4,2},{5,3},{6,0},{7,1},{8,14},{9,15},{10,... | collective-permute-start | bytes 159752 | tf_op jit(solution)/shard_map/ppermute | solution.py:671
  14.0 0.0 collective-permute-start.3
  14.0 0.8 collective-permute-start.4
  14.8 1.6 %collective-permute-start.5 = (bf16[208,128]{1,0:T(8,128)(2,1)S(1)}, bf16[208,128]{1,0:T(8,128)(2,1)S(1)}, u32[]{:S(2)}, u32[]{:S(2)}) collective-permute-start(bf16[208,128]{1,0:T(8,128)(2,1)S(1)} %get-tuple-element.21), channel_id=1, source_target_pairs={{0,7},{1,6},{2,5},{3,4},{4,3},{5,2},{6,1},{7,0},{8,15},{9,14},{10,... | collective-permute-start | bytes 159752 | tf_op jit(solution)/shard_map/ppermute | solution.py:671
  16.5 0.8 collective-permute-start.6
  17.2 0.0 collective-permute-done.2.refs_0_
  17.2 1.5 %collective-permute-start.7 = (bf16[208,128]{1,0:T(8,128)(2,1)S(1)}, bf16[208,128]{1,0:T(8,128)(2,1)S(1)}, u32[]{:S(2)}, u32[]{:S(2)}) collective-permute-start(bf16[208,128]{1,0:T(8,128)(2,1)S(1)} %get-tuple-element.19), channel_id=1, source_target_pairs={{0,3},{1,2},{2,1},{3,0},{4,7},{5,6},{6,5},{7,4},{8,11},{9,10},{10,... | collective-permute-start | bytes 159752 | tf_op jit(solution)/shard_map/ppermute | solution.py:671
  18.7 0.9 %collective-permute-done.3.refs_1_ = bf16[208,128]{1,0:T(8,128)(2,1)S(1)} collective-permute-done((bf16[208,128]{1,0:T(8,128)(2,1)S(1)}, bf16[208,128]{1,0:T(8,128)(2,1)S(1)}, u32[]{:S(2)}, u32[]{:S(2)}) %collective-permute-start.3) | collective-permute-done | bytes 53280 | tf_op jit(solution)/shard_map/ppermute | solution.py:671
  19.6 0.0 collective-permute-start.8
  20.3 0.0 copy-done.5
  20.3 1.8 %transfer.1.refs_11_.tables = f32[4,4,2,128,128]{4,3,2,1,0:T(8,128)S(1)} custom-call(f32[3]{0:T(128)S(1)} %copy-done.5, f32[1]{0:T(128)S(6)} %copy.13.travel), custom_call_target="tpu_custom_call" | custom-call | tf_op jit(solution)/shard_map/transfer/pallas_call | solution.py:487
  22.1 0.0 collective-permute-done.4.refs_2_
  22.1 0.0 collective-permute-done.5.refs_3_
  22.2 1.2 %collective-permute-done.6.refs_4_ = bf16[208,128]{1,0:T(8,128)(2,1)S(1)} collective-permute-done((bf16[208,128]{1,0:T(8,128)(2,1)S(1)}, bf16[208,128]{1,0:T(8,128)(2,1)S(1)}, u32[]{:S(2)}, u32[]{:S(2)}) %collective-permute-start.6) | collective-permute-done | bytes 53280 | tf_op jit(solution)/shard_map/ppermute | solution.py:671
  23.3 0.0 collective-permute-done.7.refs_5_
  23.3 0.0 collective-permute-done.8.refs_6_
  23.3 0.0 copy-done
  23.3 0.0 copy-done.3
  23.4 0.0 copy-done.4
  23.4 0.0 copy-start.2
  23.4 2.3 %forward_y.1 = bf16[32,96,128]{2,1,0:T(8,128)(2,1)S(1)} custom-call(bf16[208,128]{1,0:T(8,128)(2,1)S(1)} %collective-permute-done.2.refs_0_, bf16[208,128]{1,0:T(8,128)(2,1)S(1)} %collective-permute-done.3.refs_1_, bf16[208,128]{1,0:T(8,128)(2,1)S(1)} %collective-permute-done.4.refs_2_, bf16[208,128]{1,0:T(8,128)(2,1)S(1)} %collective-permute-done.5.refs_3_, ...), custom_call_target="tpu_custom_call" | custom-call | tf_op jit(solution)/shard_map/forward_y/pallas_call | solution.py:436
  25.6 25.4 %all_to_all.10 = bf16[32,96,128]{2,1,0:T(8,128)(2,1)S(1)} all-to-all(bf16[32,96,128]{2,1,0:T(8,128)(2,1)S(1)} %forward_y.1), channel_id=1, replica_groups=mesh['row'=4,'col'=8] {'row','col'}, dimensions={0} | all-to-all | bytes 1572864 | tf_op jit(solution)/shard_map/all_to_all | solution.py:674
  51.1 0.0 copy-done.2
  51.1 0.0 copy-start.1
  51.1 3.1 %middle_x.1 = bf16[32,3,32,128]{3,2,1,0:T(8,128)(2,1)S(1)} custom-call(bf16[32,3,32,128]{3,2,1,0:T(8,128)(2,1)S(1)} %bitcast.18, f32[4,4,2,128,128]{4,3,2,1,0:T(8,128)S(1)} %transfer.1.refs_11_.tables, bf16[256,768]{1,0:T(8,128)(2,1)S(1)} %copy-done.2), custom_call_target="tpu_custom_call" | custom-call | tf_op jit(solution)/shard_map/middle_x/pallas_call | solution.py:578
  54.2 24.0 %all_to_all.11.coded = bf16[32,3,32,128]{3,2,1,0:T(8,128)(2,1)S(1)} all-to-all(bf16[32,3,32,128]{3,2,1,0:T(8,128)(2,1)S(1)} %middle_x.1), channel_id=1, replica_groups=mesh['row'=4,'col'=8] {'row','col'}, dimensions={0} | all-to-all | bytes 1572864 | tf_op jit(solution)/shard_map/all_to_all | solution.py:676
  78.2 0.0 copy-done.1
  78.2 2.4 %inverse_y.1 = bf16[3,2,32,2048]{3,2,1,0:T(8,128)(2,1)} custom-call(bf16[32,3,32,128]{3,2,1,0:T(8,128)(2,1)S(1)} %all_to_all.11.coded, bf16[768,256]{1,0:T(8,128)(2,1)S(1)} %copy-done.1, f32[16,128]{1,0:T(8,128)S(1)} %copy-done.3, f32[16,128]{1,0:T(8,128)S(1)} %copy-done.4), custom_call_target="tpu_custom_call" | custom-call | tf_op jit(solution)/shard_map/inverse_y/pallas_call | solution.py:636
  (1 shorter events, 0.0 us)
Async XLA Ops:
  1.1 8.0 %collective-permute-start = (bf16[16,256]{1,0:T(8,128)(2,1)S(1)}, bf16[16,256]{1,0:T(8,128)(2,1)S(1)}, u32[]{:S(2)}, u32[]{:S(2)}) collective-permute-start(bf16[16,256]{1,0:T(8,128)(2,1)S(1)} %get-tuple-element.11), channel_id=1, source_target_pairs={{8,16},{16,8},{9,17},{17,9},{10,18},{18,10},{11,19},{19,11},{12,20... | collective-permute-start | bytes 24584 | tf_op jit(solution)/shard_map/ppermute | solution.py:667
  1.7 7.4 %collective-permute-start.1 = (bf16[16,256]{1,0:T(8,128)(2,1)S(1)}, bf16[16,256]{1,0:T(8,128)(2,1)S(1)}, u32[]{:S(2)}, u32[]{:S(2)}) collective-permute-start(bf16[16,256]{1,0:T(8,128)(2,1)S(1)} %get-tuple-element.12), channel_id=1, source_target_pairs={{0,8},{16,24},{8,0},{24,16},{1,9},{17,25},{9,1},{25,17},{2,10},{18... | collective-permute-start | bytes 24584 | tf_op jit(solution)/shard_map/ppermute | solution.py:667
  9.1 11.2 %copy-start.5 = (f32[3]{0:T(128)S(1)}, f32[3]{0:T(128)}, u32[]{:S(2)}) copy-start(f32[3]{0:T(128)} %wave.1) | copy-start | bytes 40
  10.3 13.1 %copy-start = (bf16[768,256]{1,0:T(8,128)(2,1)S(1)}, bf16[768,256]{1,0:T(8,128)(2,1)}, u32[]{:S(2)}) copy-start(bf16[768,256]{1,0:T(8,128)(2,1)} %constant.10.clone.refs_8_) | copy-start | bytes 1179652
  10.3 13.1 %copy-start.3 = (f32[16,128]{1,0:T(8,128)S(1)}, f32[16,128]{1,0:T(8,128)}, u32[]{:S(2)}) copy-start(f32[16,128]{1,0:T(8,128)} %constant.11.clone.refs_9_.tw_c) | copy-start | bytes 24580
  10.3 13.0 %copy-start.4 = (f32[16,128]{1,0:T(8,128)S(1)}, f32[16,128]{1,0:T(8,128)}, u32[]{:S(2)}) copy-start(f32[16,128]{1,0:T(8,128)} %constant.12.clone.refs_10_.tw_s) | copy-start | bytes 24580
  10.4 6.9 %collective-permute-start.2 = (bf16[208,128]{1,0:T(8,128)(2,1)S(1)}, bf16[208,128]{1,0:T(8,128)(2,1)S(1)}, u32[]{:S(2)}, u32[]{:S(2)}) collective-permute-start(bf16[208,128]{1,0:T(8,128)(2,1)S(1)} %get-tuple-element.24), channel_id=1, source_target_pairs={{0,6},{1,7},{2,4},{3,5},{4,2},{5,3},{6,0},{7,1},{8,14},{9,15},{10,... | collective-permute-start | bytes 159752 | tf_op jit(solution)/shard_map/ppermute | solution.py:671
  14.0 5.6 %collective-permute-start.3 = (bf16[208,128]{1,0:T(8,128)(2,1)S(1)}, bf16[208,128]{1,0:T(8,128)(2,1)S(1)}, u32[]{:S(2)}, u32[]{:S(2)}) collective-permute-start(bf16[208,128]{1,0:T(8,128)(2,1)S(1)} %get-tuple-element.23), channel_id=1, source_target_pairs={{0,4},{1,5},{2,6},{3,7},{4,0},{5,1},{6,2},{7,3},{8,12},{9,13},{10,... | collective-permute-start | bytes 159752 | tf_op jit(solution)/shard_map/ppermute | solution.py:671
  14.0 8.1 %collective-permute-start.4 = (bf16[208,128]{1,0:T(8,128)(2,1)S(1)}, bf16[208,128]{1,0:T(8,128)(2,1)S(1)}, u32[]{:S(2)}, u32[]{:S(2)}) collective-permute-start(bf16[208,128]{1,0:T(8,128)(2,1)S(1)} %get-tuple-element.22), channel_id=1, source_target_pairs={{0,2},{1,3},{2,0},{3,1},{4,6},{5,7},{6,4},{7,5},{8,10},{9,11},{10,... | collective-permute-start | bytes 159752 | tf_op jit(solution)/shard_map/ppermute | solution.py:671
  14.8 7.3 %collective-permute-start.5 = (bf16[208,128]{1,0:T(8,128)(2,1)S(1)}, bf16[208,128]{1,0:T(8,128)(2,1)S(1)}, u32[]{:S(2)}, u32[]{:S(2)}) collective-permute-start(bf16[208,128]{1,0:T(8,128)(2,1)S(1)} %get-tuple-element.21), channel_id=1, source_target_pairs={{0,7},{1,6},{2,5},{3,4},{4,3},{5,2},{6,1},{7,0},{8,15},{9,14},{10,... | collective-permute-start | bytes 159752 | tf_op jit(solution)/shard_map/ppermute | solution.py:671
  16.5 6.9 %collective-permute-start.6 = (bf16[208,128]{1,0:T(8,128)(2,1)S(1)}, bf16[208,128]{1,0:T(8,128)(2,1)S(1)}, u32[]{:S(2)}, u32[]{:S(2)}) collective-permute-start(bf16[208,128]{1,0:T(8,128)(2,1)S(1)} %get-tuple-element.20), channel_id=1, source_target_pairs={{0,5},{1,4},{2,7},{3,6},{4,1},{5,0},{6,3},{7,2},{8,13},{9,12},{10,... | collective-permute-start | bytes 159752 | tf_op jit(solution)/shard_map/ppermute | solution.py:671
  17.2 6.1 %collective-permute-start.7 = (bf16[208,128]{1,0:T(8,128)(2,1)S(1)}, bf16[208,128]{1,0:T(8,128)(2,1)S(1)}, u32[]{:S(2)}, u32[]{:S(2)}) collective-permute-start(bf16[208,128]{1,0:T(8,128)(2,1)S(1)} %get-tuple-element.19), channel_id=1, source_target_pairs={{0,3},{1,2},{2,1},{3,0},{4,7},{5,6},{6,5},{7,4},{8,11},{9,10},{10,... | collective-permute-start | bytes 159752 | tf_op jit(solution)/shard_map/ppermute | solution.py:671
  19.6 3.7 %collective-permute-start.8 = (bf16[208,128]{1,0:T(8,128)(2,1)S(1)}, bf16[208,128]{1,0:T(8,128)(2,1)S(1)}, u32[]{:S(2)}, u32[]{:S(2)}) collective-permute-start(bf16[208,128]{1,0:T(8,128)(2,1)S(1)} %get-tuple-element.18), channel_id=1, source_target_pairs={{0,1},{1,0},{2,3},{3,2},{4,5},{5,4},{6,7},{7,6},{8,9},{9,8},{10,11... | collective-permute-start | bytes 159752 | tf_op jit(solution)/shard_map/ppermute | solution.py:671
  23.4 27.7 %copy-start.2 = (bf16[256,768]{1,0:T(8,128)(2,1)S(1)}, bf16[256,768]{1,0:T(8,128)(2,1)}, u32[]{:S(2)}) copy-start(bf16[256,768]{1,0:T(8,128)(2,1)} %constant.13.clone.matrix) | copy-start | bytes 1179652
  51.1 27.1 %copy-start.1 = (bf16[768,256]{1,0:T(8,128)(2,1)S(1)}, bf16[768,256]{1,0:T(8,128)(2,1)}, u32[]{:S(2)}) copy-start(bf16[768,256]{1,0:T(8,128)(2,1)} %constant.14.clone.matrix) | copy-start | bytes 1179652

commit v6 on v5

--- a/solution.py
+++ b/solution.py
@@ -14,6 +14,7 @@
 TILE = 256
 HALF = 128
 CODE = 124.0
+LOG_CODE = CODE * math.log(2.0)
 TINY = 1.2e-38
 SHRINK = 2.0**-4
 VMEM_LIMIT = 10 * 1024 * 1024
@@ -70,10 +71,6 @@
         c = c * u + coef
     s2 = s + s
     return 1.0 - s2 * s, s2 * c
-
-
-def log2(x):
-    return lax.log(x) * (1.0 / math.log(2.0))
 
 
 def encode(v):
@@ -391,14 +388,14 @@
             for p in range(peers):
                 before = cross[p - 1] if p > 0 else zero
                 after = cross[p + 1] if p + 1 < peers else zero
-                fixed.append(CODE * jnp.tanh(edge[p] + jnp.where(lane < HALF // 2, before, after)))
+                fixed.append(LOG_CODE * jnp.tanh(edge[p] + jnp.where(lane < HALF // 2, before, after)))
             items = []
             for p in range(peers):
                 for h in range(2):
                     start = (h * colors + o) * band + r
-                    t = log2(coded[p, start : start + step, :].astype(F32))
+                    t = lax.log(coded[p, start : start + step, :].astype(F32))
                     t = jnp.where(lane == (HALF - 1) * h, fixed[p], t)
-                    items.append(Pair(*sincos_half(t, 4, 1.0 / CODE)))
+                    items.append(Pair(*sincos_half(t, 4, 1.0 / LOG_CODE)))
             for k, z in enumerate(small_dft(items, -1)):
                 if k:
                     z = z.times(tw_c[k : k + 1, :], -tw_s[k : k + 1, :])
@@ -470,7 +467,7 @@
                 a = wave[color]
                 turns = travel[0] * f2 / (a + jnp.sqrt(a * a - f2))
                 turns = turns - jnp.round(turns)
-                c, s = sincos_half(turns, 5, 2.0)
+                c, s = sincos_half(turns, 4, 2.0)
                 out[color, k, 0, rows, :] = c * (SHRINK / height)
                 out[color, k, 1, rows, :] = s * (SHRINK / height)
             turns = (half * m).astype(F32) * (1.0 / height)

time: 80.9 us -> 80.8 us (level)
  no operation moved by 1% of the time
where the time goes in v6:
time: 80.8 us; the launch traced here: 80.5 us
  blocking collectives  49.3 us (61%)
  starting transfers between devices  14.7 us (18%)
  Pallas kernels  13.3 us (16%)
  waiting for transfers between devices  2.22 us (3%)
  between operations  0.82 us (1%)
    all_to_all x1, blocking collectives, per_device(): lax.all_to_all(spectrum, ('row', 'col'), split_axis=0, concat_axis=0, til...  25.3 us
    all_to_all x1, blocking collectives, per_device(): lax.all_to_all(back, ('row', 'col'), split_axis=0, concat_axis=0, tiled=T...  24 us
    ppermute x7, starting transfers between devices, per_device(): lax.ppermute(bands[k], 'col', [(i, i ^ k) for i in range(mesh_cols)])  8.34 us
    ppermute x2, starting transfers between devices, per_device(): halos.append(lax.ppermute(edge, 'row', pairs + [(j, i) for i, j in pairs]))  6.4 us
    pallas_call x1, Pallas kernels, middle(): pl.pallas_call(middle_kernel, out_shape=jax.ShapeDtypeStruct(coded.shape,...  3.12 us
    pallas_call x1, Pallas kernels, inverse_y(): pl.pallas_call(partial(inverse_y_kernel, parts), out_shape=jax.ShapeDtype...  2.4 us
    pallas_call x1, Pallas kernels, forward_y(): pl.pallas_call(partial(forward_y_kernel, colors, band, parts), out_shape=...  2.25 us
    ppermute x7, waiting for transfers between devices, per_device(): lax.ppermute(bands[k], 'col', [(i, i ^ k) for i in range(mesh_cols)])  2.22 us
  transfers between devices with their start and end apart: 9, of which 2 were waited for; matrix products, arithmetic and copies ran while one was open for 0% of the time, Pallas kernels for 4%

profile of v6, /device:TPU:0, one launch (start us, length us, event | category | flops | bytes accessed | tf_op | source)
XLA Modules:
  0.0 80.5 jit_solution(17111159416425236781)
XLA Ops:
  0.0 1.0 %edges.1 = (bf16[16,256]{1,0:T(8,128)(2,1)S(1)}, bf16[16,256]{1,0:T(8,128)(2,1)S(1)}) custom-call(bf16[16,256,256]{2,1,0:T(8,128)(2,1)} %feat.3), custom_call_target="tpu_custom_call" | custom-call | tf_op jit(solution)/shard_map/edges/pallas_call | solution.py:185
  1.1 0.7 collective-permute-start
  1.7 5.7 %collective-permute-start.1 = (bf16[16,256]{1,0:T(8,128)(2,1)S(1)}, bf16[16,256]{1,0:T(8,128)(2,1)S(1)}, u32[]{:S(2)}, u32[]{:S(2)}) collective-permute-start(bf16[16,256]{1,0:T(8,128)(2,1)S(1)} %get-tuple-element.12), channel_id=1, source_target_pairs={{0,8},{16,24},{8,0},{24,16},{1,9},{17,25},{9,1},{25,17},{2,10},{18... | collective-permute-start | bytes 24584 | tf_op jit(solution)/shard_map/ppermute | solution.py:664
  7.5 1.6 %prepare.1 = (bf16[16,256,256]{2,1,0:T(8,128)(2,1)S(1)}, bf16[216,256]{1,0:T(8,128)(2,1)S(1)}, bf16[2,72,16]{2,1,0:T(8,128)(2,1)S(1)}, f32[3,256]{1,0:T(4,128)S(1)}) custom-call(bf16[16,256,256]{2,1,0:T(8,128)(2,1)} %feat.3, bf16[3,3,3,16]{3,2,1,0:T(4,128)(2,1)} %bitcast.19, f32[3]{0:T(128)} %bias.1), custom_call_target="tpu_custom_call" | custom-call | tf_op jit(solution)/shard_map/prepare/pallas_call | solution.py:249
  9.1 0.0 copy-start.5
  9.1 0.0 collective-permute-done.second_halo
  9.1 0.0 collective-permute-done.1.first_halo
  9.1 1.2 %conv_head.1 = bf16[8,208,128]{2,1,0:T(8,128)(2,1)S(1)} custom-call(bf16[16,256]{1,0:T(8,128)(2,1)S(1)} %collective-permute-done.second_halo, bf16[16,256]{1,0:T(8,128)(2,1)S(1)} %collective-permute-done.1.first_halo, bf16[16,256,256]{2,1,0:T(8,128)(2,1)S(1)} %get-tuple-element.13.feat, bf16[216,256]{1,0:T(8,128)(2,1)S(1)} %get-tuple-element.14.table, ...), custom_call_target="tpu_custom_call" | custom-call | tf_op jit(solution)/shard_map/conv_head/pallas_call | solution.py:352
  10.3 0.0 copy-start
  10.3 0.0 copy-start.3
  10.3 0.0 copy-start.4
  10.4 3.7 %collective-permute-start.2 = (bf16[208,128]{1,0:T(8,128)(2,1)S(1)}, bf16[208,128]{1,0:T(8,128)(2,1)S(1)}, u32[]{:S(2)}, u32[]{:S(2)}) collective-permute-start(bf16[208,128]{1,0:T(8,128)(2,1)S(1)} %get-tuple-element.24), channel_id=1, source_target_pairs={{0,6},{1,7},{2,4},{3,5},{4,2},{5,3},{6,0},{7,1},{8,14},{9,15},{10,... | collective-permute-start | bytes 159752 | tf_op jit(solution)/shard_map/ppermute | solution.py:668
  14.0 0.0 collective-permute-start.3
  14.0 0.8 collective-permute-start.4
  14.8 1.6 %collective-permute-start.5 = (bf16[208,128]{1,0:T(8,128)(2,1)S(1)}, bf16[208,128]{1,0:T(8,128)(2,1)S(1)}, u32[]{:S(2)}, u32[]{:S(2)}) collective-permute-start(bf16[208,128]{1,0:T(8,128)(2,1)S(1)} %get-tuple-element.21), channel_id=1, source_target_pairs={{0,7},{1,6},{2,5},{3,4},{4,3},{5,2},{6,1},{7,0},{8,15},{9,14},{10,... | collective-permute-start | bytes 159752 | tf_op jit(solution)/shard_map/ppermute | solution.py:668
  16.5 0.8 collective-permute-start.6
  17.2 0.0 collective-permute-done.2.refs_0_
  17.2 1.5 %collective-permute-start.7 = (bf16[208,128]{1,0:T(8,128)(2,1)S(1)}, bf16[208,128]{1,0:T(8,128)(2,1)S(1)}, u32[]{:S(2)}, u32[]{:S(2)}) collective-permute-start(bf16[208,128]{1,0:T(8,128)(2,1)S(1)} %get-tuple-element.19), channel_id=1, source_target_pairs={{0,3},{1,2},{2,1},{3,0},{4,7},{5,6},{6,5},{7,4},{8,11},{9,10},{10,... | collective-permute-start | bytes 159752 | tf_op jit(solution)/shard_map/ppermute | solution.py:668
  18.7 0.9 %collective-permute-done.3.refs_1_ = bf16[208,128]{1,0:T(8,128)(2,1)S(1)} collective-permute-done((bf16[208,128]{1,0:T(8,128)(2,1)S(1)}, bf16[208,128]{1,0:T(8,128)(2,1)S(1)}, u32[]{:S(2)}, u32[]{:S(2)}) %collective-permute-start.3) | collective-permute-done | bytes 53280 | tf_op jit(solution)/shard_map/ppermute | solution.py:668
  19.6 0.0 collective-permute-start.8
  20.3 0.0 copy-done.5
  20.3 1.7 %transfer.1.refs_11_.tables = f32[4,4,2,128,128]{4,3,2,1,0:T(8,128)S(1)} custom-call(f32[3]{0:T(128)S(1)} %copy-done.5, f32[1]{0:T(128)S(6)} %copy.13.travel), custom_call_target="tpu_custom_call" | custom-call | tf_op jit(solution)/shard_map/transfer/pallas_call | solution.py:484
  22.0 0.0 collective-permute-done.4.refs_2_
  22.0 0.0 collective-permute-done.5.refs_3_
  22.1 1.3 %collective-permute-done.6.refs_4_ = bf16[208,128]{1,0:T(8,128)(2,1)S(1)} collective-permute-done((bf16[208,128]{1,0:T(8,128)(2,1)S(1)}, bf16[208,128]{1,0:T(8,128)(2,1)S(1)}, u32[]{:S(2)}, u32[]{:S(2)}) %collective-permute-start.6) | collective-permute-done | bytes 53280 | tf_op jit(solution)/shard_map/ppermute | solution.py:668
  23.3 0.0 collective-permute-done.7.refs_5_
  23.3 0.0 collective-permute-done.8.refs_6_
  23.3 0.0 copy-done
  23.3 0.0 copy-done.3
  23.4 0.0 copy-done.4
  23.4 0.0 copy-start.2
  23.4 2.3 %forward_y.1 = bf16[32,96,128]{2,1,0:T(8,128)(2,1)S(1)} custom-call(bf16[208,128]{1,0:T(8,128)(2,1)S(1)} %collective-permute-done.2.refs_0_, bf16[208,128]{1,0:T(8,128)(2,1)S(1)} %collective-permute-done.3.refs_1_, bf16[208,128]{1,0:T(8,128)(2,1)S(1)} %collective-permute-done.4.refs_2_, bf16[208,128]{1,0:T(8,128)(2,1)S(1)} %collective-permute-done.5.refs_3_, ...), custom_call_target="tpu_custom_call" | custom-call | tf_op jit(solution)/shard_map/forward_y/pallas_call | solution.py:433
  25.6 25.3 %all_to_all.10 = bf16[32,96,128]{2,1,0:T(8,128)(2,1)S(1)} all-to-all(bf16[32,96,128]{2,1,0:T(8,128)(2,1)S(1)} %forward_y.1), channel_id=1, replica_groups=mesh['row'=4,'col'=8] {'row','col'}, dimensions={0} | all-to-all | bytes 1572864 | tf_op jit(solution)/shard_map/all_to_all | solution.py:671
  51.0 0.0 copy-done.2
  51.0 0.0 copy-start.1
  51.0 3.1 %middle_x.1 = bf16[32,3,32,128]{3,2,1,0:T(8,128)(2,1)S(1)} custom-call(bf16[32,3,32,128]{3,2,1,0:T(8,128)(2,1)S(1)} %bitcast.18, f32[4,4,2,128,128]{4,3,2,1,0:T(8,128)S(1)} %transfer.1.refs_11_.tables, bf16[256,768]{1,0:T(8,128)(2,1)S(1)} %copy-done.2), custom_call_target="tpu_custom_call" | custom-call | tf_op jit(solution)/shard_map/middle_x/pallas_call | solution.py:575
  54.1 24.0 %all_to_all.11.coded = bf16[32,3,32,128]{3,2,1,0:T(8,128)(2,1)S(1)} all-to-all(bf16[32,3,32,128]{3,2,1,0:T(8,128)(2,1)S(1)} %middle_x.1), channel_id=1, replica_groups=mesh['row'=4,'col'=8] {'row','col'}, dimensions={0} | all-to-all | bytes 1572864 | tf_op jit(solution)/shard_map/all_to_all | solution.py:673
  78.1 0.0 copy-done.1
  78.1 2.4 %inverse_y.1 = bf16[3,2,32,2048]{3,2,1,0:T(8,128)(2,1)} custom-call(bf16[32,3,32,128]{3,2,1,0:T(8,128)(2,1)S(1)} %all_to_all.11.coded, bf16[768,256]{1,0:T(8,128)(2,1)S(1)} %copy-done.1, f32[16,128]{1,0:T(8,128)S(1)} %copy-done.3, f32[16,128]{1,0:T(8,128)S(1)} %copy-done.4), custom_call_target="tpu_custom_call" | custom-call | tf_op jit(solution)/shard_map/inverse_y/pallas_call | solution.py:633
  (1 shorter events, 0.0 us)
Async XLA Ops:
  1.1 8.0 %collective-permute-start = (bf16[16,256]{1,0:T(8,128)(2,1)S(1)}, bf16[16,256]{1,0:T(8,128)(2,1)S(1)}, u32[]{:S(2)}, u32[]{:S(2)}) collective-permute-start(bf16[16,256]{1,0:T(8,128)(2,1)S(1)} %get-tuple-element.11), channel_id=1, source_target_pairs={{8,16},{16,8},{9,17},{17,9},{10,18},{18,10},{11,19},{19,11},{12,20... | collective-permute-start | bytes 24584 | tf_op jit(solution)/shard_map/ppermute | solution.py:664
  1.7 7.4 %collective-permute-start.1 = (bf16[16,256]{1,0:T(8,128)(2,1)S(1)}, bf16[16,256]{1,0:T(8,128)(2,1)S(1)}, u32[]{:S(2)}, u32[]{:S(2)}) collective-permute-start(bf16[16,256]{1,0:T(8,128)(2,1)S(1)} %get-tuple-element.12), channel_id=1, source_target_pairs={{0,8},{16,24},{8,0},{24,16},{1,9},{17,25},{9,1},{25,17},{2,10},{18... | collective-permute-start | bytes 24584 | tf_op jit(solution)/shard_map/ppermute | solution.py:664
  9.1 11.2 %copy-start.5 = (f32[3]{0:T(128)S(1)}, f32[3]{0:T(128)}, u32[]{:S(2)}) copy-start(f32[3]{0:T(128)} %wave.1) | copy-start | bytes 40
  10.3 13.1 %copy-start = (bf16[768,256]{1,0:T(8,128)(2,1)S(1)}, bf16[768,256]{1,0:T(8,128)(2,1)}, u32[]{:S(2)}) copy-start(bf16[768,256]{1,0:T(8,128)(2,1)} %constant.10.clone.refs_8_) | copy-start | bytes 1179652
  10.3 13.1 %copy-start.3 = (f32[16,128]{1,0:T(8,128)S(1)}, f32[16,128]{1,0:T(8,128)}, u32[]{:S(2)}) copy-start(f32[16,128]{1,0:T(8,128)} %constant.11.clone.refs_9_.tw_c) | copy-start | bytes 24580
  10.3 13.0 %copy-start.4 = (f32[16,128]{1,0:T(8,128)S(1)}, f32[16,128]{1,0:T(8,128)}, u32[]{:S(2)}) copy-start(f32[16,128]{1,0:T(8,128)} %constant.12.clone.refs_10_.tw_s) | copy-start | bytes 24580
  10.4 6.9 %collective-permute-start.2 = (bf16[208,128]{1,0:T(8,128)(2,1)S(1)}, bf16[208,128]{1,0:T(8,128)(2,1)S(1)}, u32[]{:S(2)}, u32[]{:S(2)}) collective-permute-start(bf16[208,128]{1,0:T(8,128)(2,1)S(1)} %get-tuple-element.24), channel_id=1, source_target_pairs={{0,6},{1,7},{2,4},{3,5},{4,2},{5,3},{6,0},{7,1},{8,14},{9,15},{10,... | collective-permute-start | bytes 159752 | tf_op jit(solution)/shard_map/ppermute | solution.py:668
  14.0 5.6 %collective-permute-start.3 = (bf16[208,128]{1,0:T(8,128)(2,1)S(1)}, bf16[208,128]{1,0:T(8,128)(2,1)S(1)}, u32[]{:S(2)}, u32[]{:S(2)}) collective-permute-start(bf16[208,128]{1,0:T(8,128)(2,1)S(1)} %get-tuple-element.23), channel_id=1, source_target_pairs={{0,4},{1,5},{2,6},{3,7},{4,0},{5,1},{6,2},{7,3},{8,12},{9,13},{10,... | collective-permute-start | bytes 159752 | tf_op jit(solution)/shard_map/ppermute | solution.py:668
  14.0 8.0 %collective-permute-start.4 = (bf16[208,128]{1,0:T(8,128)(2,1)S(1)}, bf16[208,128]{1,0:T(8,128)(2,1)S(1)}, u32[]{:S(2)}, u32[]{:S(2)}) collective-permute-start(bf16[208,128]{1,0:T(8,128)(2,1)S(1)} %get-tuple-element.22), channel_id=1, source_target_pairs={{0,2},{1,3},{2,0},{3,1},{4,6},{5,7},{6,4},{7,5},{8,10},{9,11},{10,... | collective-permute-start | bytes 159752 | tf_op jit(solution)/shard_map/ppermute | solution.py:668
  14.8 7.2 %collective-permute-start.5 = (bf16[208,128]{1,0:T(8,128)(2,1)S(1)}, bf16[208,128]{1,0:T(8,128)(2,1)S(1)}, u32[]{:S(2)}, u32[]{:S(2)}) collective-permute-start(bf16[208,128]{1,0:T(8,128)(2,1)S(1)} %get-tuple-element.21), channel_id=1, source_target_pairs={{0,7},{1,6},{2,5},{3,4},{4,3},{5,2},{6,1},{7,0},{8,15},{9,14},{10,... | collective-permute-start | bytes 159752 | tf_op jit(solution)/shard_map/ppermute | solution.py:668
  16.5 6.9 %collective-permute-start.6 = (bf16[208,128]{1,0:T(8,128)(2,1)S(1)}, bf16[208,128]{1,0:T(8,128)(2,1)S(1)}, u32[]{:S(2)}, u32[]{:S(2)}) collective-permute-start(bf16[208,128]{1,0:T(8,128)(2,1)S(1)} %get-tuple-element.20), channel_id=1, source_target_pairs={{0,5},{1,4},{2,7},{3,6},{4,1},{5,0},{6,3},{7,2},{8,13},{9,12},{10,... | collective-permute-start | bytes 159752 | tf_op jit(solution)/shard_map/ppermute | solution.py:668
  17.2 6.1 %collective-permute-start.7 = (bf16[208,128]{1,0:T(8,128)(2,1)S(1)}, bf16[208,128]{1,0:T(8,128)(2,1)S(1)}, u32[]{:S(2)}, u32[]{:S(2)}) collective-permute-start(bf16[208,128]{1,0:T(8,128)(2,1)S(1)} %get-tuple-element.19), channel_id=1, source_target_pairs={{0,3},{1,2},{2,1},{3,0},{4,7},{5,6},{6,5},{7,4},{8,11},{9,10},{10,... | collective-permute-start | bytes 159752 | tf_op jit(solution)/shard_map/ppermute | solution.py:668
  19.6 3.7 %collective-permute-start.8 = (bf16[208,128]{1,0:T(8,128)(2,1)S(1)}, bf16[208,128]{1,0:T(8,128)(2,1)S(1)}, u32[]{:S(2)}, u32[]{:S(2)}) collective-permute-start(bf16[208,128]{1,0:T(8,128)(2,1)S(1)} %get-tuple-element.18), channel_id=1, source_target_pairs={{0,1},{1,0},{2,3},{3,2},{4,5},{5,4},{6,7},{7,6},{8,9},{9,8},{10,11... | collective-permute-start | bytes 159752 | tf_op jit(solution)/shard_map/ppermute | solution.py:668
  23.4 27.6 %copy-start.2 = (bf16[256,768]{1,0:T(8,128)(2,1)S(1)}, bf16[256,768]{1,0:T(8,128)(2,1)}, u32[]{:S(2)}) copy-start(bf16[256,768]{1,0:T(8,128)(2,1)} %constant.13.clone.matrix) | copy-start | bytes 1179652
  51.0 27.1 %copy-start.1 = (bf16[768,256]{1,0:T(8,128)(2,1)S(1)}, bf16[768,256]{1,0:T(8,128)(2,1)}, u32[]{:S(2)}) copy-start(bf16[768,256]{1,0:T(8,128)(2,1)} %constant.14.clone.matrix) | copy-start | bytes 1179652

commit v7 on v6

--- a/solution.py
+++ b/solution.py
@@ -360,7 +360,9 @@
 
 
 def sending_order(peers):
-    return [*range(peers - 2, 0, -2), *range(peers - 1, 0, -2), 0]
+    half = peers // 2
+    chips = [half, *(k for k in range(peers - 2, 0, -2) if k != half)]
+    return [*chips, *(k + 1 for k in chips), 1, 0]
 
 
 def forward_y_kernel(colors, band, parts, *refs):

time: 80.8 us -> 80.7 us (level)
  transfers between devices with their start and end apart: 9 -> 9, of which waited for: 2 -> 3; matrix products, arithmetic and copies ran while one was open for 0% -> 0% of each run, Pallas kernels for 4% -> 4%
where the time goes in v7:
time: 80.7 us; the launch traced here: 80.5 us
  blocking collectives  49.1 us (61%)
  starting transfers between devices  14.5 us (18%)
  Pallas kernels  13.3 us (16%)
  waiting for transfers between devices  2.62 us (3%)
  between operations  0.81 us (1%)
    all_to_all x1, blocking collectives, per_device(): lax.all_to_all(spectrum, ('row', 'col'), split_axis=0, concat_axis=0, til...  25.1 us
    all_to_all x1, blocking collectives, per_device(): lax.all_to_all(back, ('row', 'col'), split_axis=0, concat_axis=0, tiled=T...  24 us
    ppermute x7, starting transfers between devices, per_device(): lax.ppermute(bands[k], 'col', [(i, i ^ k) for i in range(mesh_cols)])  8.11 us
    ppermute x2, starting transfers between devices, per_device(): halos.append(lax.ppermute(edge, 'row', pairs + [(j, i) for i, j in pairs]))  6.4 us
    pallas_call x1, Pallas kernels, middle(): pl.pallas_call(middle_kernel, out_shape=jax.ShapeDtypeStruct(coded.shape,...  3.12 us
    ppermute x7, waiting for transfers between devices, per_device(): lax.ppermute(bands[k], 'col', [(i, i ^ k) for i in range(mesh_cols)])  2.61 us
    pallas_call x1, Pallas kernels, inverse_y(): pl.pallas_call(partial(inverse_y_kernel, parts), out_shape=jax.ShapeDtype...  2.4 us
    pallas_call x1, Pallas kernels, forward_y(): pl.pallas_call(partial(forward_y_kernel, colors, band, parts), out_shape=...  2.26 us
  transfers between devices with their start and end apart: 9, of which 3 were waited for; matrix products, arithmetic and copies ran while one was open for 0% of the time, Pallas kernels for 4%

profile of v7, /device:TPU:0, one launch (start us, length us, event | category | flops | bytes accessed | tf_op | source)
XLA Modules:
  0.0 80.5 jit_solution(5591652956627056271)
XLA Ops:
  0.0 1.0 %edges.1 = (bf16[16,256]{1,0:T(8,128)(2,1)S(1)}, bf16[16,256]{1,0:T(8,128)(2,1)S(1)}) custom-call(bf16[16,256,256]{2,1,0:T(8,128)(2,1)} %feat.3), custom_call_target="tpu_custom_call" | custom-call | tf_op jit(solution)/shard_map/edges/pallas_call | solution.py:185
  1.1 0.7 collective-permute-start
  1.7 5.7 %collective-permute-start.1 = (bf16[16,256]{1,0:T(8,128)(2,1)S(1)}, bf16[16,256]{1,0:T(8,128)(2,1)S(1)}, u32[]{:S(2)}, u32[]{:S(2)}) collective-permute-start(bf16[16,256]{1,0:T(8,128)(2,1)S(1)} %get-tuple-element.12), channel_id=1, source_target_pairs={{0,8},{16,24},{8,0},{24,16},{1,9},{17,25},{9,1},{25,17},{2,10},{18... | collective-permute-start | bytes 24584 | tf_op jit(solution)/shard_map/ppermute | solution.py:666
  7.5 1.6 %prepare.1 = (bf16[16,256,256]{2,1,0:T(8,128)(2,1)S(1)}, bf16[216,256]{1,0:T(8,128)(2,1)S(1)}, bf16[2,72,16]{2,1,0:T(8,128)(2,1)S(1)}, f32[3,256]{1,0:T(4,128)S(1)}) custom-call(bf16[16,256,256]{2,1,0:T(8,128)(2,1)} %feat.3, bf16[3,3,3,16]{3,2,1,0:T(4,128)(2,1)} %bitcast.19, f32[3]{0:T(128)} %bias.1), custom_call_target="tpu_custom_call" | custom-call | tf_op jit(solution)/shard_map/prepare/pallas_call | solution.py:249
  9.1 0.0 copy-start.5
  9.1 0.0 collective-permute-done.second_halo
  9.1 0.0 collective-permute-done.1.first_halo
  9.1 1.2 %conv_head.1 = bf16[8,208,128]{2,1,0:T(8,128)(2,1)S(1)} custom-call(bf16[16,256]{1,0:T(8,128)(2,1)S(1)} %collective-permute-done.second_halo, bf16[16,256]{1,0:T(8,128)(2,1)S(1)} %collective-permute-done.1.first_halo, bf16[16,256,256]{2,1,0:T(8,128)(2,1)S(1)} %get-tuple-element.13.feat, bf16[216,256]{1,0:T(8,128)(2,1)S(1)} %get-tuple-element.14.table, ...), custom_call_target="tpu_custom_call" | custom-call | tf_op jit(solution)/shard_map/conv_head/pallas_call | solution.py:352
  10.3 0.0 copy-start
  10.3 0.0 copy-start.3
  10.3 0.0 copy-start.4
  10.4 2.7 %collective-permute-start.2 = (bf16[208,128]{1,0:T(8,128)(2,1)S(1)}, bf16[208,128]{1,0:T(8,128)(2,1)S(1)}, u32[]{:S(2)}, u32[]{:S(2)}) collective-permute-start(bf16[208,128]{1,0:T(8,128)(2,1)S(1)} %get-tuple-element.24), channel_id=1, source_target_pairs={{0,4},{1,5},{2,6},{3,7},{4,0},{5,1},{6,2},{7,3},{8,12},{9,13},{10,... | collective-permute-start | bytes 159752 | tf_op jit(solution)/shard_map/ppermute | solution.py:670
  13.0 1.3 %collective-permute-start.3 = (bf16[208,128]{1,0:T(8,128)(2,1)S(1)}, bf16[208,128]{1,0:T(8,128)(2,1)S(1)}, u32[]{:S(2)}, u32[]{:S(2)}) collective-permute-start(bf16[208,128]{1,0:T(8,128)(2,1)S(1)} %get-tuple-element.23), channel_id=1, source_target_pairs={{0,6},{1,7},{2,4},{3,5},{4,2},{5,3},{6,0},{7,1},{8,14},{9,15},{10,... | collective-permute-start | bytes 159752 | tf_op jit(solution)/shard_map/ppermute | solution.py:670
  14.4 0.2 collective-permute-start.4
  14.6 0.8 %collective-permute-start.5 = (bf16[208,128]{1,0:T(8,128)(2,1)S(1)}, bf16[208,128]{1,0:T(8,128)(2,1)S(1)}, u32[]{:S(2)}, u32[]{:S(2)}) collective-permute-start(bf16[208,128]{1,0:T(8,128)(2,1)S(1)} %get-tuple-element.21), channel_id=1, source_target_pairs={{0,5},{1,4},{2,7},{3,6},{4,1},{5,0},{6,3},{7,2},{8,13},{9,12},{10,... | collective-permute-start | bytes 159752 | tf_op jit(solution)/shard_map/ppermute | solution.py:670
  15.4 3.0 %collective-permute-start.6 = (bf16[208,128]{1,0:T(8,128)(2,1)S(1)}, bf16[208,128]{1,0:T(8,128)(2,1)S(1)}, u32[]{:S(2)}, u32[]{:S(2)}) collective-permute-start(bf16[208,128]{1,0:T(8,128)(2,1)S(1)} %get-tuple-element.20), channel_id=1, source_target_pairs={{0,7},{1,6},{2,5},{3,4},{4,3},{5,2},{6,1},{7,0},{8,15},{9,14},{10,... | collective-permute-start | bytes 159752 | tf_op jit(solution)/shard_map/ppermute | solution.py:670
  18.5 0.0 collective-permute-done.2.refs_0_
  18.5 0.0 collective-permute-start.7
  18.5 0.6 collective-permute-done.3.refs_1_
  19.1 0.0 collective-permute-start.8
  19.8 0.0 copy-done.5
  19.8 1.7 %transfer.1.refs_11_.tables = f32[4,4,2,128,128]{4,3,2,1,0:T(8,128)S(1)} custom-call(f32[3]{0:T(128)S(1)} %copy-done.5, f32[1]{0:T(128)S(6)} %copy.13.travel), custom_call_target="tpu_custom_call" | custom-call | tf_op jit(solution)/shard_map/transfer/pallas_call | solution.py:486
  21.5 0.0 collective-permute-done.4.refs_2_
  21.5 0.4 collective-permute-done.5.refs_3_
  21.9 0.0 collective-permute-done.6.refs_4_
  21.9 1.6 %collective-permute-done.7.refs_5_ = bf16[208,128]{1,0:T(8,128)(2,1)S(1)} collective-permute-done((bf16[208,128]{1,0:T(8,128)(2,1)S(1)}, bf16[208,128]{1,0:T(8,128)(2,1)S(1)}, u32[]{:S(2)}, u32[]{:S(2)}) %collective-permute-start.7) | collective-permute-done | bytes 53280 | tf_op jit(solution)/shard_map/ppermute | solution.py:670
  23.5 0.0 collective-permute-done.8.refs_6_
  23.5 0.0 copy-done
  23.5 0.0 copy-done.3
  23.5 0.0 copy-done.4
  23.5 0.0 copy-start.2
  23.5 2.3 %forward_y.1 = bf16[32,96,128]{2,1,0:T(8,128)(2,1)S(1)} custom-call(bf16[208,128]{1,0:T(8,128)(2,1)S(1)} %collective-permute-done.2.refs_0_, bf16[208,128]{1,0:T(8,128)(2,1)S(1)} %collective-permute-done.3.refs_1_, bf16[208,128]{1,0:T(8,128)(2,1)S(1)} %collective-permute-done.4.refs_2_, bf16[208,128]{1,0:T(8,128)(2,1)S(1)} %collective-permute-done.5.refs_3_, ...), custom_call_target="tpu_custom_call" | custom-call | tf_op jit(solution)/shard_map/forward_y/pallas_call | solution.py:435
  25.8 25.1 %all_to_all.10 = bf16[32,96,128]{2,1,0:T(8,128)(2,1)S(1)} all-to-all(bf16[32,96,128]{2,1,0:T(8,128)(2,1)S(1)} %forward_y.1), channel_id=1, replica_groups=mesh['row'=4,'col'=8] {'row','col'}, dimensions={0} | all-to-all | bytes 1572864 | tf_op jit(solution)/shard_map/all_to_all | solution.py:673
  50.9 0.0 copy-done.2
  50.9 0.0 copy-start.1
  50.9 3.1 %middle_x.1 = bf16[32,3,32,128]{3,2,1,0:T(8,128)(2,1)S(1)} custom-call(bf16[32,3,32,128]{3,2,1,0:T(8,128)(2,1)S(1)} %bitcast.18, f32[4,4,2,128,128]{4,3,2,1,0:T(8,128)S(1)} %transfer.1.refs_11_.tables, bf16[256,768]{1,0:T(8,128)(2,1)S(1)} %copy-done.2), custom_call_target="tpu_custom_call" | custom-call | tf_op jit(solution)/shard_map/middle_x/pallas_call | solution.py:577
  54.1 24.0 %all_to_all.11.coded = bf16[32,3,32,128]{3,2,1,0:T(8,128)(2,1)S(1)} all-to-all(bf16[32,3,32,128]{3,2,1,0:T(8,128)(2,1)S(1)} %middle_x.1), channel_id=1, replica_groups=mesh['row'=4,'col'=8] {'row','col'}, dimensions={0} | all-to-all | bytes 1572864 | tf_op jit(solution)/shard_map/all_to_all | solution.py:675
  78.1 0.0 copy-done.1
  78.1 2.4 %inverse_y.1 = bf16[3,2,32,2048]{3,2,1,0:T(8,128)(2,1)} custom-call(bf16[32,3,32,128]{3,2,1,0:T(8,128)(2,1)S(1)} %all_to_all.11.coded, bf16[768,256]{1,0:T(8,128)(2,1)S(1)} %copy-done.1, f32[16,128]{1,0:T(8,128)S(1)} %copy-done.3, f32[16,128]{1,0:T(8,128)S(1)} %copy-done.4), custom_call_target="tpu_custom_call" | custom-call | tf_op jit(solution)/shard_map/inverse_y/pallas_call | solution.py:635
  (1 shorter events, 0.0 us)
Async XLA Ops:
  1.1 8.0 %collective-permute-start = (bf16[16,256]{1,0:T(8,128)(2,1)S(1)}, bf16[16,256]{1,0:T(8,128)(2,1)S(1)}, u32[]{:S(2)}, u32[]{:S(2)}) collective-permute-start(bf16[16,256]{1,0:T(8,128)(2,1)S(1)} %get-tuple-element.11), channel_id=1, source_target_pairs={{8,16},{16,8},{9,17},{17,9},{10,18},{18,10},{11,19},{19,11},{12,20... | collective-permute-start | bytes 24584 | tf_op jit(solution)/shard_map/ppermute | solution.py:666
  1.7 7.4 %collective-permute-start.1 = (bf16[16,256]{1,0:T(8,128)(2,1)S(1)}, bf16[16,256]{1,0:T(8,128)(2,1)S(1)}, u32[]{:S(2)}, u32[]{:S(2)}) collective-permute-start(bf16[16,256]{1,0:T(8,128)(2,1)S(1)} %get-tuple-element.12), channel_id=1, source_target_pairs={{0,8},{16,24},{8,0},{24,16},{1,9},{17,25},{9,1},{25,17},{2,10},{18... | collective-permute-start | bytes 24584 | tf_op jit(solution)/shard_map/ppermute | solution.py:666
  9.1 10.7 %copy-start.5 = (f32[3]{0:T(128)S(1)}, f32[3]{0:T(128)}, u32[]{:S(2)}) copy-start(f32[3]{0:T(128)} %wave.1) | copy-start | bytes 40
  10.3 13.2 %copy-start = (bf16[768,256]{1,0:T(8,128)(2,1)S(1)}, bf16[768,256]{1,0:T(8,128)(2,1)}, u32[]{:S(2)}) copy-start(bf16[768,256]{1,0:T(8,128)(2,1)} %constant.10.clone.refs_8_) | copy-start | bytes 1179652
  10.3 13.2 %copy-start.3 = (f32[16,128]{1,0:T(8,128)S(1)}, f32[16,128]{1,0:T(8,128)}, u32[]{:S(2)}) copy-start(f32[16,128]{1,0:T(8,128)} %constant.11.clone.refs_9_.tw_c) | copy-start | bytes 24580
  10.3 13.2 %copy-start.4 = (f32[16,128]{1,0:T(8,128)S(1)}, f32[16,128]{1,0:T(8,128)}, u32[]{:S(2)}) copy-start(f32[16,128]{1,0:T(8,128)} %constant.12.clone.refs_10_.tw_s) | copy-start | bytes 24580
  10.4 8.1 %collective-permute-start.2 = (bf16[208,128]{1,0:T(8,128)(2,1)S(1)}, bf16[208,128]{1,0:T(8,128)(2,1)S(1)}, u32[]{:S(2)}, u32[]{:S(2)}) collective-permute-start(bf16[208,128]{1,0:T(8,128)(2,1)S(1)} %get-tuple-element.24), channel_id=1, source_target_pairs={{0,4},{1,5},{2,6},{3,7},{4,0},{5,1},{6,2},{7,3},{8,12},{9,13},{10,... | collective-permute-start | bytes 159752 | tf_op jit(solution)/shard_map/ppermute | solution.py:670
  13.0 6.1 %collective-permute-start.3 = (bf16[208,128]{1,0:T(8,128)(2,1)S(1)}, bf16[208,128]{1,0:T(8,128)(2,1)S(1)}, u32[]{:S(2)}, u32[]{:S(2)}) collective-permute-start(bf16[208,128]{1,0:T(8,128)(2,1)S(1)} %get-tuple-element.23), channel_id=1, source_target_pairs={{0,6},{1,7},{2,4},{3,5},{4,2},{5,3},{6,0},{7,1},{8,14},{9,15},{10,... | collective-permute-start | bytes 159752 | tf_op jit(solution)/shard_map/ppermute | solution.py:670
  14.4 7.1 %collective-permute-start.4 = (bf16[208,128]{1,0:T(8,128)(2,1)S(1)}, bf16[208,128]{1,0:T(8,128)(2,1)S(1)}, u32[]{:S(2)}, u32[]{:S(2)}) collective-permute-start(bf16[208,128]{1,0:T(8,128)(2,1)S(1)} %get-tuple-element.22), channel_id=1, source_target_pairs={{0,2},{1,3},{2,0},{3,1},{4,6},{5,7},{6,4},{7,5},{8,10},{9,11},{10,... | collective-permute-start | bytes 159752 | tf_op jit(solution)/shard_map/ppermute | solution.py:670
  14.6 7.3 %collective-permute-start.5 = (bf16[208,128]{1,0:T(8,128)(2,1)S(1)}, bf16[208,128]{1,0:T(8,128)(2,1)S(1)}, u32[]{:S(2)}, u32[]{:S(2)}) collective-permute-start(bf16[208,128]{1,0:T(8,128)(2,1)S(1)} %get-tuple-element.21), channel_id=1, source_target_pairs={{0,5},{1,4},{2,7},{3,6},{4,1},{5,0},{6,3},{7,2},{8,13},{9,12},{10,... | collective-permute-start | bytes 159752 | tf_op jit(solution)/shard_map/ppermute | solution.py:670
  15.4 6.5 %collective-permute-start.6 = (bf16[208,128]{1,0:T(8,128)(2,1)S(1)}, bf16[208,128]{1,0:T(8,128)(2,1)S(1)}, u32[]{:S(2)}, u32[]{:S(2)}) collective-permute-start(bf16[208,128]{1,0:T(8,128)(2,1)S(1)} %get-tuple-element.20), channel_id=1, source_target_pairs={{0,7},{1,6},{2,5},{3,4},{4,3},{5,2},{6,1},{7,0},{8,15},{9,14},{10,... | collective-permute-start | bytes 159752 | tf_op jit(solution)/shard_map/ppermute | solution.py:670
  18.5 5.0 %collective-permute-start.7 = (bf16[208,128]{1,0:T(8,128)(2,1)S(1)}, bf16[208,128]{1,0:T(8,128)(2,1)S(1)}, u32[]{:S(2)}, u32[]{:S(2)}) collective-permute-start(bf16[208,128]{1,0:T(8,128)(2,1)S(1)} %get-tuple-element.19), channel_id=1, source_target_pairs={{0,3},{1,2},{2,1},{3,0},{4,7},{5,6},{6,5},{7,4},{8,11},{9,10},{10,... | collective-permute-start | bytes 159752 | tf_op jit(solution)/shard_map/ppermute | solution.py:670
  19.1 4.4 %collective-permute-start.8 = (bf16[208,128]{1,0:T(8,128)(2,1)S(1)}, bf16[208,128]{1,0:T(8,128)(2,1)S(1)}, u32[]{:S(2)}, u32[]{:S(2)}) collective-permute-start(bf16[208,128]{1,0:T(8,128)(2,1)S(1)} %get-tuple-element.18), channel_id=1, source_target_pairs={{0,1},{1,0},{2,3},{3,2},{4,5},{5,4},{6,7},{7,6},{8,9},{9,8},{10,11... | collective-permute-start | bytes 159752 | tf_op jit(solution)/shard_map/ppermute | solution.py:670
  23.5 27.4 %copy-start.2 = (bf16[256,768]{1,0:T(8,128)(2,1)S(1)}, bf16[256,768]{1,0:T(8,128)(2,1)}, u32[]{:S(2)}) copy-start(bf16[256,768]{1,0:T(8,128)(2,1)} %constant.13.clone.matrix) | copy-start | bytes 1179652
  50.9 27.1 %copy-start.1 = (bf16[768,256]{1,0:T(8,128)(2,1)S(1)}, bf16[768,256]{1,0:T(8,128)(2,1)}, u32[]{:S(2)}) copy-start(bf16[768,256]{1,0:T(8,128)(2,1)} %constant.14.clone.matrix) | copy-start | bytes 1179652

commit v8 on v5

--- a/solution.py
+++ b/solution.py
@@ -591,7 +591,6 @@
     colors, band, width = coded.shape[1], coded.shape[2], coded.shape[3]
     outs = []
     step = 16
-    scale = 1.0 / (SHRINK * inner * HALF)
 
     def spread(o):
         for k in range(inner):
@@ -608,7 +607,7 @@
             items = []
             for k in range(inner):
                 z = acc[k * band + r : k * band + r + step]
-                items.append(Pair(z[:, :HALF], z[:, HALF:]).times(tw_c[k : k + 1, :] * scale, tw_s[k : k + 1, :] * scale))
+                items.append(Pair(z[:, :HALF], z[:, HALF:]).times(tw_c[k : k + 1, :], tw_s[k : k + 1, :]))
             for a, z in enumerate(small_dft(items, 1)):
                 out[o, 0, r : r + step, a * HALF : (a + 1) * HALF] = z.re.astype(BF16)
                 out[o, 1, r : r + step, a * HALF : (a + 1) * HALF] = z.im.astype(BF16)
@@ -629,7 +628,7 @@
 def inverse_y(coded, parts):
     groups, colors, band, width = coded.shape
     inner = groups // parts
-    tw_c, tw_s = dft_np(inner, HALF, inner * HALF)
+    tw_c, tw_s = (x / (SHRINK * inner * HALF) for x in dft_np(inner, HALF, inner * HALF))
     matrix = tall(np.ascontiguousarray(interleaved(complex_np(1).T.copy(), parts).T))
     hbm = pl.BlockSpec(memory_space=pltpu.HBM)
     vm = pl.BlockSpec(memory_space=pltpu.VMEM)

time: 80.9 us -> 80.9 us (level)
  no operation moved by 1% of the time
where the time goes in v8:
time: 80.9 us; the launch traced here: 80.6 us
  blocking collectives  49.4 us (61%)
  starting transfers between devices  14.7 us (18%)
  Pallas kernels  13.4 us (17%)
  waiting for transfers between devices  2.12 us (3%)
  between operations  0.83 us (1%)
    all_to_all x1, blocking collectives, per_device(): lax.all_to_all(spectrum, ('row', 'col'), split_axis=0, concat_axis=0, til...  25.4 us
    all_to_all x1, blocking collectives, per_device(): lax.all_to_all(back, ('row', 'col'), split_axis=0, concat_axis=0, tiled=T...  24 us
    ppermute x7, starting transfers between devices, per_device(): lax.ppermute(bands[k], 'col', [(i, i ^ k) for i in range(mesh_cols)])  8.34 us
    ppermute x2, starting transfers between devices, per_device(): halos.append(lax.ppermute(edge, 'row', pairs + [(j, i) for i, j in pairs]))  6.4 us
    pallas_call x1, Pallas kernels, middle(): pl.pallas_call(middle_kernel, out_shape=jax.ShapeDtypeStruct(coded.shape,...  3.13 us
    pallas_call x1, Pallas kernels, inverse_y(): pl.pallas_call(partial(inverse_y_kernel, parts), out_shape=jax.ShapeDtype...  2.39 us
    pallas_call x1, Pallas kernels, forward_y(): pl.pallas_call(partial(forward_y_kernel, colors, band, parts), out_shape=...  2.26 us
    ppermute x7, waiting for transfers between devices, per_device(): lax.ppermute(bands[k], 'col', [(i, i ^ k) for i in range(mesh_cols)])  2.11 us
  transfers between devices with their start and end apart: 9, of which 2 were waited for; matrix products, arithmetic and copies ran while one was open for 0% of the time, Pallas kernels for 4%

profile of v8, /device:TPU:0, one launch (start us, length us, event | category | flops | bytes accessed | tf_op | source)
XLA Modules:
  0.0 80.6 jit_solution(1985424009405488253)
XLA Ops:
  0.0 1.0 %edges.1 = (bf16[16,256]{1,0:T(8,128)(2,1)S(1)}, bf16[16,256]{1,0:T(8,128)(2,1)S(1)}) custom-call(bf16[16,256,256]{2,1,0:T(8,128)(2,1)} %feat.3), custom_call_target="tpu_custom_call" | custom-call | tf_op jit(solution)/shard_map/edges/pallas_call | solution.py:188
  1.1 0.7 collective-permute-start
  1.7 5.7 %collective-permute-start.1 = (bf16[16,256]{1,0:T(8,128)(2,1)S(1)}, bf16[16,256]{1,0:T(8,128)(2,1)S(1)}, u32[]{:S(2)}, u32[]{:S(2)}) collective-permute-start(bf16[16,256]{1,0:T(8,128)(2,1)S(1)} %get-tuple-element.12), channel_id=1, source_target_pairs={{0,8},{16,24},{8,0},{24,16},{1,9},{17,25},{9,1},{25,17},{2,10},{18... | collective-permute-start | bytes 24584 | tf_op jit(solution)/shard_map/ppermute | solution.py:666
  7.5 1.6 %prepare.1 = (bf16[16,256,256]{2,1,0:T(8,128)(2,1)S(1)}, bf16[216,256]{1,0:T(8,128)(2,1)S(1)}, bf16[2,72,16]{2,1,0:T(8,128)(2,1)S(1)}, f32[3,256]{1,0:T(4,128)S(1)}) custom-call(bf16[16,256,256]{2,1,0:T(8,128)(2,1)} %feat.3, bf16[3,3,3,16]{3,2,1,0:T(4,128)(2,1)} %bitcast.19, f32[3]{0:T(128)} %bias.1), custom_call_target="tpu_custom_call" | custom-call | tf_op jit(solution)/shard_map/prepare/pallas_call | solution.py:252
  9.1 0.0 copy-start.7
  9.1 0.0 collective-permute-done.second_halo
  9.1 0.0 collective-permute-done.1.first_halo
  9.1 1.2 %conv_head.1 = bf16[8,208,128]{2,1,0:T(8,128)(2,1)S(1)} custom-call(bf16[16,256]{1,0:T(8,128)(2,1)S(1)} %collective-permute-done.second_halo, bf16[16,256]{1,0:T(8,128)(2,1)S(1)} %collective-permute-done.1.first_halo, bf16[16,256,256]{2,1,0:T(8,128)(2,1)S(1)} %get-tuple-element.13.feat, bf16[216,256]{1,0:T(8,128)(2,1)S(1)} %get-tuple-element.14.table, ...), custom_call_target="tpu_custom_call" | custom-call | tf_op jit(solution)/shard_map/conv_head/pallas_call | solution.py:355
  10.3 0.0 copy-start
  10.3 0.0 copy-start.5
  10.3 0.0 copy-start.6
  10.4 3.7 %collective-permute-start.2 = (bf16[208,128]{1,0:T(8,128)(2,1)S(1)}, bf16[208,128]{1,0:T(8,128)(2,1)S(1)}, u32[]{:S(2)}, u32[]{:S(2)}) collective-permute-start(bf16[208,128]{1,0:T(8,128)(2,1)S(1)} %get-tuple-element.24), channel_id=1, source_target_pairs={{0,6},{1,7},{2,4},{3,5},{4,2},{5,3},{6,0},{7,1},{8,14},{9,15},{10,... | collective-permute-start | bytes 159752 | tf_op jit(solution)/shard_map/ppermute | solution.py:670
  14.0 0.0 collective-permute-start.3
  14.0 0.8 collective-permute-start.4
  14.8 1.6 %collective-permute-start.5 = (bf16[208,128]{1,0:T(8,128)(2,1)S(1)}, bf16[208,128]{1,0:T(8,128)(2,1)S(1)}, u32[]{:S(2)}, u32[]{:S(2)}) collective-permute-start(bf16[208,128]{1,0:T(8,128)(2,1)S(1)} %get-tuple-element.21), channel_id=1, source_target_pairs={{0,7},{1,6},{2,5},{3,4},{4,3},{5,2},{6,1},{7,0},{8,15},{9,14},{10,... | collective-permute-start | bytes 159752 | tf_op jit(solution)/shard_map/ppermute | solution.py:670
  16.5 0.8 collective-permute-start.6
  17.2 0.0 collective-permute-done.2.refs_0_
  17.2 1.5 %collective-permute-start.7 = (bf16[208,128]{1,0:T(8,128)(2,1)S(1)}, bf16[208,128]{1,0:T(8,128)(2,1)S(1)}, u32[]{:S(2)}, u32[]{:S(2)}) collective-permute-start(bf16[208,128]{1,0:T(8,128)(2,1)S(1)} %get-tuple-element.19), channel_id=1, source_target_pairs={{0,3},{1,2},{2,1},{3,0},{4,7},{5,6},{6,5},{7,4},{8,11},{9,10},{10,... | collective-permute-start | bytes 159752 | tf_op jit(solution)/shard_map/ppermute | solution.py:670
  18.7 0.9 %collective-permute-done.3.refs_1_ = bf16[208,128]{1,0:T(8,128)(2,1)S(1)} collective-permute-done((bf16[208,128]{1,0:T(8,128)(2,1)S(1)}, bf16[208,128]{1,0:T(8,128)(2,1)S(1)}, u32[]{:S(2)}, u32[]{:S(2)}) %collective-permute-start.3) | collective-permute-done | bytes 53280 | tf_op jit(solution)/shard_map/ppermute | solution.py:670
  19.6 0.0 collective-permute-start.8
  20.3 0.0 copy-done.7
  20.3 1.8 %transfer.1.refs_11_.tables = f32[4,4,2,128,128]{4,3,2,1,0:T(8,128)S(1)} custom-call(f32[3]{0:T(128)S(1)} %copy-done.7, f32[1]{0:T(128)S(6)} %copy.13.travel), custom_call_target="tpu_custom_call" | custom-call | tf_op jit(solution)/shard_map/transfer/pallas_call | solution.py:487
  22.1 0.0 collective-permute-done.4.refs_2_
  22.1 0.0 collective-permute-done.5.refs_3_
  22.2 1.2 %collective-permute-done.6.refs_4_ = bf16[208,128]{1,0:T(8,128)(2,1)S(1)} collective-permute-done((bf16[208,128]{1,0:T(8,128)(2,1)S(1)}, bf16[208,128]{1,0:T(8,128)(2,1)S(1)}, u32[]{:S(2)}, u32[]{:S(2)}) %collective-permute-start.6) | collective-permute-done | bytes 53280 | tf_op jit(solution)/shard_map/ppermute | solution.py:670
  23.3 0.0 collective-permute-done.7.refs_5_
  23.3 0.0 collective-permute-done.8.refs_6_
  23.3 0.0 copy-done
  23.3 0.0 copy-done.5
  23.4 0.0 copy-done.6
  23.4 0.0 copy-start.2
  23.4 2.3 %forward_y.1 = bf16[32,96,128]{2,1,0:T(8,128)(2,1)S(1)} custom-call(bf16[208,128]{1,0:T(8,128)(2,1)S(1)} %collective-permute-done.2.refs_0_, bf16[208,128]{1,0:T(8,128)(2,1)S(1)} %collective-permute-done.3.refs_1_, bf16[208,128]{1,0:T(8,128)(2,1)S(1)} %collective-permute-done.4.refs_2_, bf16[208,128]{1,0:T(8,128)(2,1)S(1)} %collective-permute-done.5.refs_3_, ...), custom_call_target="tpu_custom_call" | custom-call | tf_op jit(solution)/shard_map/forward_y/pallas_call | solution.py:436
  25.6 25.4 %all_to_all.10 = bf16[32,96,128]{2,1,0:T(8,128)(2,1)S(1)} all-to-all(bf16[32,96,128]{2,1,0:T(8,128)(2,1)S(1)} %forward_y.1), channel_id=1, replica_groups=mesh['row'=4,'col'=8] {'row','col'}, dimensions={0} | all-to-all | bytes 1572864 | tf_op jit(solution)/shard_map/all_to_all | solution.py:673
  51.1 0.0 copy-done.2
  51.1 0.0 copy-start.1
  51.1 0.0 copy-start.3
  51.1 0.0 copy-start.4
  51.1 3.1 %middle_x.1 = bf16[32,3,32,128]{3,2,1,0:T(8,128)(2,1)S(1)} custom-call(bf16[32,3,32,128]{3,2,1,0:T(8,128)(2,1)S(1)} %bitcast.18, f32[4,4,2,128,128]{4,3,2,1,0:T(8,128)S(1)} %transfer.1.refs_11_.tables, bf16[256,768]{1,0:T(8,128)(2,1)S(1)} %copy-done.2), custom_call_target="tpu_custom_call" | custom-call | tf_op jit(solution)/shard_map/middle_x/pallas_call | solution.py:578
  54.2 24.0 %all_to_all.11.coded = bf16[32,3,32,128]{3,2,1,0:T(8,128)(2,1)S(1)} all-to-all(bf16[32,3,32,128]{3,2,1,0:T(8,128)(2,1)S(1)} %middle_x.1), channel_id=1, replica_groups=mesh['row'=4,'col'=8] {'row','col'}, dimensions={0} | all-to-all | bytes 1572864 | tf_op jit(solution)/shard_map/all_to_all | solution.py:675
  78.2 0.0 copy-done.1
  78.2 0.0 copy-done.3
  78.2 0.0 copy-done.4
  78.2 2.4 %inverse_y.1 = bf16[3,2,32,2048]{3,2,1,0:T(8,128)(2,1)} custom-call(bf16[32,3,32,128]{3,2,1,0:T(8,128)(2,1)S(1)} %all_to_all.11.coded, bf16[768,256]{1,0:T(8,128)(2,1)S(1)} %copy-done.1, f32[16,128]{1,0:T(8,128)S(1)} %copy-done.3, f32[16,128]{1,0:T(8,128)S(1)} %copy-done.4), custom_call_target="tpu_custom_call" | custom-call | tf_op jit(solution)/shard_map/inverse_y/pallas_call | solution.py:635
  (1 shorter events, 0.0 us)
Async XLA Ops:
  1.1 8.0 %collective-permute-start = (bf16[16,256]{1,0:T(8,128)(2,1)S(1)}, bf16[16,256]{1,0:T(8,128)(2,1)S(1)}, u32[]{:S(2)}, u32[]{:S(2)}) collective-permute-start(bf16[16,256]{1,0:T(8,128)(2,1)S(1)} %get-tuple-element.11), channel_id=1, source_target_pairs={{8,16},{16,8},{9,17},{17,9},{10,18},{18,10},{11,19},{19,11},{12,20... | collective-permute-start | bytes 24584 | tf_op jit(solution)/shard_map/ppermute | solution.py:666
  1.7 7.4 %collective-permute-start.1 = (bf16[16,256]{1,0:T(8,128)(2,1)S(1)}, bf16[16,256]{1,0:T(8,128)(2,1)S(1)}, u32[]{:S(2)}, u32[]{:S(2)}) collective-permute-start(bf16[16,256]{1,0:T(8,128)(2,1)S(1)} %get-tuple-element.12), channel_id=1, source_target_pairs={{0,8},{16,24},{8,0},{24,16},{1,9},{17,25},{9,1},{25,17},{2,10},{18... | collective-permute-start | bytes 24584 | tf_op jit(solution)/shard_map/ppermute | solution.py:666
  9.1 11.2 %copy-start.7 = (f32[3]{0:T(128)S(1)}, f32[3]{0:T(128)}, u32[]{:S(2)}) copy-start(f32[3]{0:T(128)} %wave.1) | copy-start | bytes 40
  10.3 13.1 %copy-start = (bf16[768,256]{1,0:T(8,128)(2,1)S(1)}, bf16[768,256]{1,0:T(8,128)(2,1)}, u32[]{:S(2)}) copy-start(bf16[768,256]{1,0:T(8,128)(2,1)} %constant.14.clone.refs_8_) | copy-start | bytes 1179652
  10.3 13.1 %copy-start.5 = (f32[16,128]{1,0:T(8,128)S(1)}, f32[16,128]{1,0:T(8,128)}, u32[]{:S(2)}) copy-start(f32[16,128]{1,0:T(8,128)} %constant.15.clone.refs_9_) | copy-start | bytes 24580
  10.3 13.0 %copy-start.6 = (f32[16,128]{1,0:T(8,128)S(1)}, f32[16,128]{1,0:T(8,128)}, u32[]{:S(2)}) copy-start(f32[16,128]{1,0:T(8,128)} %constant.16.clone.refs_10_) | copy-start | bytes 24580
  10.4 6.9 %collective-permute-start.2 = (bf16[208,128]{1,0:T(8,128)(2,1)S(1)}, bf16[208,128]{1,0:T(8,128)(2,1)S(1)}, u32[]{:S(2)}, u32[]{:S(2)}) collective-permute-start(bf16[208,128]{1,0:T(8,128)(2,1)S(1)} %get-tuple-element.24), channel_id=1, source_target_pairs={{0,6},{1,7},{2,4},{3,5},{4,2},{5,3},{6,0},{7,1},{8,14},{9,15},{10,... | collective-permute-start | bytes 159752 | tf_op jit(solution)/shard_map/ppermute | solution.py:670
  14.0 5.6 %collective-permute-start.3 = (bf16[208,128]{1,0:T(8,128)(2,1)S(1)}, bf16[208,128]{1,0:T(8,128)(2,1)S(1)}, u32[]{:S(2)}, u32[]{:S(2)}) collective-permute-start(bf16[208,128]{1,0:T(8,128)(2,1)S(1)} %get-tuple-element.23), channel_id=1, source_target_pairs={{0,4},{1,5},{2,6},{3,7},{4,0},{5,1},{6,2},{7,3},{8,12},{9,13},{10,... | collective-permute-start | bytes 159752 | tf_op jit(solution)/shard_map/ppermute | solution.py:670
  14.0 8.1 %collective-permute-start.4 = (bf16[208,128]{1,0:T(8,128)(2,1)S(1)}, bf16[208,128]{1,0:T(8,128)(2,1)S(1)}, u32[]{:S(2)}, u32[]{:S(2)}) collective-permute-start(bf16[208,128]{1,0:T(8,128)(2,1)S(1)} %get-tuple-element.22), channel_id=1, source_target_pairs={{0,2},{1,3},{2,0},{3,1},{4,6},{5,7},{6,4},{7,5},{8,10},{9,11},{10,... | collective-permute-start | bytes 159752 | tf_op jit(solution)/shard_map/ppermute | solution.py:670
  14.8 7.3 %collective-permute-start.5 = (bf16[208,128]{1,0:T(8,128)(2,1)S(1)}, bf16[208,128]{1,0:T(8,128)(2,1)S(1)}, u32[]{:S(2)}, u32[]{:S(2)}) collective-permute-start(bf16[208,128]{1,0:T(8,128)(2,1)S(1)} %get-tuple-element.21), channel_id=1, source_target_pairs={{0,7},{1,6},{2,5},{3,4},{4,3},{5,2},{6,1},{7,0},{8,15},{9,14},{10,... | collective-permute-start | bytes 159752 | tf_op jit(solution)/shard_map/ppermute | solution.py:670
  16.5 6.9 %collective-permute-start.6 = (bf16[208,128]{1,0:T(8,128)(2,1)S(1)}, bf16[208,128]{1,0:T(8,128)(2,1)S(1)}, u32[]{:S(2)}, u32[]{:S(2)}) collective-permute-start(bf16[208,128]{1,0:T(8,128)(2,1)S(1)} %get-tuple-element.20), channel_id=1, source_target_pairs={{0,5},{1,4},{2,7},{3,6},{4,1},{5,0},{6,3},{7,2},{8,13},{9,12},{10,... | collective-permute-start | bytes 159752 | tf_op jit(solution)/shard_map/ppermute | solution.py:670
  17.2 6.1 %collective-permute-start.7 = (bf16[208,128]{1,0:T(8,128)(2,1)S(1)}, bf16[208,128]{1,0:T(8,128)(2,1)S(1)}, u32[]{:S(2)}, u32[]{:S(2)}) collective-permute-start(bf16[208,128]{1,0:T(8,128)(2,1)S(1)} %get-tuple-element.19), channel_id=1, source_target_pairs={{0,3},{1,2},{2,1},{3,0},{4,7},{5,6},{6,5},{7,4},{8,11},{9,10},{10,... | collective-permute-start | bytes 159752 | tf_op jit(solution)/shard_map/ppermute | solution.py:670
  19.6 3.7 %collective-permute-start.8 = (bf16[208,128]{1,0:T(8,128)(2,1)S(1)}, bf16[208,128]{1,0:T(8,128)(2,1)S(1)}, u32[]{:S(2)}, u32[]{:S(2)}) collective-permute-start(bf16[208,128]{1,0:T(8,128)(2,1)S(1)} %get-tuple-element.18), channel_id=1, source_target_pairs={{0,1},{1,0},{2,3},{3,2},{4,5},{5,4},{6,7},{7,6},{8,9},{9,8},{10,11... | collective-permute-start | bytes 159752 | tf_op jit(solution)/shard_map/ppermute | solution.py:670
  23.4 27.7 %copy-start.2 = (bf16[256,768]{1,0:T(8,128)(2,1)S(1)}, bf16[256,768]{1,0:T(8,128)(2,1)}, u32[]{:S(2)}) copy-start(bf16[256,768]{1,0:T(8,128)(2,1)} %constant.17.clone.matrix) | copy-start | bytes 1179652
  51.1 27.1 %copy-start.1 = (bf16[768,256]{1,0:T(8,128)(2,1)S(1)}, bf16[768,256]{1,0:T(8,128)(2,1)}, u32[]{:S(2)}) copy-start(bf16[768,256]{1,0:T(8,128)(2,1)} %constant.18.clone.matrix) | copy-start | bytes 1179652
  51.1 27.1 %copy-start.3 = (f32[16,128]{1,0:T(8,128)S(1)}, f32[16,128]{1,0:T(8,128)}, u32[]{:S(2)}) copy-start(f32[16,128]{1,0:T(8,128)} %constant.19.clone.tw_c) | copy-start | bytes 24580
  51.1 27.1 %copy-start.4 = (f32[16,128]{1,0:T(8,128)S(1)}, f32[16,128]{1,0:T(8,128)}, u32[]{:S(2)}) copy-start(f32[16,128]{1,0:T(8,128)} %constant.20.clone.tw_s) | copy-start | bytes 24580
